TPU v7x, 128 devices: a whole 4x4x4 slice. The times are simulated.
128 devices in a mesh: frame: 16 (over y, x), head: 4 (over z), fsdp: 2 (over core).
Axes of the slice: x: 4, y: 4, z: 4, core: 2. Of those that a mesh axis runs over, the one named last changes fastest.
Arguments:
- history: bfloat16 [64, 16, 8, 256], P('frame'), may hold values from -6 to 6
- section: bfloat16 [2048, 64], P('frame'), may hold values from -6 to 6
- slab_kernel: int32 [16], replicated, may hold values from 0 to 2, as said below
- patch_fine: bfloat16 [64, 3072], P(None, ('head', 'fsdp')), may hold values from -0.75 to 0.75
- patch_mid: bfloat16 [512, 3072], P(None, ('head', 'fsdp')), may hold values from -0.25 to 0.25
- patch_coarse: bfloat16 [4096, 3072], P(None, ('head', 'fsdp')), may hold values from -0.09375 to 0.09375
- modulation: float32 [2, 3072], replicated, may hold values from -3 to 3
- w_qkv: bfloat16 [3, 3072, 3072], P(None, None, ('head', 'fsdp')), may hold values from -0.109375 to 0.109375
Outputs:
- attended: bfloat16 [2048, 3072], P('frame', ('head', 'fsdp'))
Inputs may be any that keep to these rules, and one draw needn't show every extreme that they name: `slab_kernel`: exactly one slab takes kernel 0, exactly 8 slabs take kernel 2, the others take kernel 1.
All inputs are finite; a program needn't handle non-finite values.
Results may differ from a plain program's by a relative error of at most 0.0034.
Values may be sent and summed in bfloat16 or wider, within the bound.
No kernel may reach another device: no remote copies, remote signals or barrier semaphores. Data moves between devices by JAX's collectives and lax.ppermute only.
A program may use at most 192 MiB of HBM per device.

v0:
```python
import jax
import jax.numpy as jnp
import numpy as np
from jax import lax
from jax.sharding import PartitionSpec as P

HEAD_DIM = 128
ROPE_T = 16
ROPE_H = 56
ROPE_W = 56
SLAB_LEN = 4


THETA = 256.0
EPS = 1e-06


def shortened(array):

    def short(part):
        return part.astype(jnp.bfloat16) if part.dtype == jnp.float32 else part

    return jax.tree.map(short, array)


def spread(value, axis, source):
    kept = jnp.where(lax.axis_index(axis) == source, value, 0).astype(value.dtype)
    return lax.psum(kept, axis)


def rotary_tables():
    widths = (ROPE_T, ROPE_H, ROPE_W)
    axis_list, freq_list, partner_list, sign_list = ([], [], [], [])
    offset = 0
    for axis_id, part_width in enumerate(widths):
        half_width = part_width // 2
        for column in range(part_width):
            pair_id = column % half_width
            axis_list.append(axis_id)
            freq_list.append(THETA ** (-2.0 * pair_id / part_width))
            if column < half_width:
                partner_list.append(offset + column + half_width)
                sign_list.append(-1.0)
            else:
                partner_list.append(offset + column - half_width)
                sign_list.append(1.0)
        offset += part_width
    return (
        np.array(axis_list, np.int32),
        np.array(freq_list, np.float32),
        np.array(partner_list, np.int32),
        np.array(sign_list, np.float32),
    )


def rotate(vectors, positions):
    axis_of, frequency, partner, sign_of = rotary_tables()
    angles = jnp.take(positions, axis_of, axis=1) * frequency
    cosine = jnp.cos(angles)[:, None, :]
    sine_part = (jnp.sin(angles) * sign_of)[:, None, :]
    return vectors * cosine + jnp.take(vectors, partner, axis=2) * sine_part


def rms_norm(vectors):
    return vectors * lax.rsqrt(jnp.mean(vectors * vectors, axis=-1, keepdims=True) + EPS)


def patchify(slab_cells, step_t, step_h, step_w):
    frames_in, channel_count, rows_in, cols_in = slab_cells.shape
    blocks = slab_cells.reshape(
        frames_in // step_t,
        step_t,
        channel_count,
        rows_in // step_h,
        step_h,
        cols_in // step_w,
        step_w,
    )
    blocks = blocks.transpose(0, 3, 5, 2, 1, 4, 6)
    return blocks.reshape(
        frames_in // step_t * (rows_in // step_h) * (cols_in // step_w),
        channel_count * step_t * step_h * step_w,
    )


def slab_features(slab_cells, kernel_index, weights, capacity):

    def make_branch(stride, weight):

        def branch(cells):
            tokens = patchify(cells, stride, 2 * stride, 2 * stride)
            product = jnp.dot(tokens, weight, preferred_element_type=jnp.float32)
            product = jnp.pad(product, ((0, capacity - product.shape[0]), (0, 0)))
            return product.astype(jnp.bfloat16)

        return branch

    return lax.switch(
        kernel_index,
        [make_branch(1, weights[0]), make_branch(2, weights[1]), make_branch(4, weights[2])],
        slab_cells,
    )


def stride_of(kernel_index):
    return jnp.where(kernel_index == 0, 1, jnp.where(kernel_index == 1, 2, 4)).astype(jnp.int32)


def live_count(kernel_index, height, breadth):
    stride = stride_of(kernel_index)
    return SLAB_LEN // stride * (height // (2 * stride)) * (breadth // (2 * stride))


def slab_positions(slab_index, kernel_index, height, breadth, capacity):
    stride = stride_of(kernel_index)
    grid_h = height // (2 * stride)
    grid_w = breadth // (2 * stride)
    row_ids = jnp.arange(capacity, dtype=jnp.int32)
    frame_at = (row_ids // (grid_h * grid_w)).astype(jnp.float32)
    row_at = (row_ids // grid_w % grid_h).astype(jnp.float32)
    col_at = (row_ids % grid_w).astype(jnp.float32)
    factor = stride.astype(jnp.float32)
    pos_t = SLAB_LEN * slab_index.astype(jnp.float32) + factor * frame_at + (factor - 1.0) / 2.0
    pos_h = 2.0 * factor * row_at + factor - 0.5
    pos_w = 2.0 * factor * col_at + factor - 0.5
    return jnp.stack([pos_t, pos_h, pos_w], axis=1)


def section_positions(first_row, row_count, height, breadth, history_frames):
    row_ids = first_row + jnp.arange(row_count, dtype=jnp.int32)
    grid_h = height // 2
    grid_w = breadth // 2
    frame_at = (row_ids // (grid_h * grid_w)).astype(jnp.float32)
    row_at = (row_ids // grid_w % grid_h).astype(jnp.float32)
    col_at = (row_ids % grid_w).astype(jnp.float32)
    pos_t = history_frames + frame_at
    return jnp.stack([pos_t, 2.0 * row_at + 0.5, 2.0 * col_at + 0.5], axis=1)


def modulate(features, modulation):
    values32 = features.astype(jnp.float32)
    centered = values32 - jnp.mean(values32, axis=-1, keepdims=True)
    variance = jnp.mean(centered * centered, axis=-1, keepdims=True)
    normed = centered * lax.rsqrt(variance + EPS)
    return (normed * (1.0 + modulation[1]) + modulation[0]).astype(jnp.bfloat16)


def accumulate(numerator, denominator, queries, key_piece, value_piece, usable):
    head_count = queries.shape[1]
    key_heads = key_piece.reshape(key_piece.shape[0], head_count, HEAD_DIM)
    value_heads = value_piece.reshape(value_piece.shape[0], head_count, HEAD_DIM)
    scores = jnp.einsum("qhd,khd->hqk", queries, key_heads, preferred_element_type=jnp.float32)
    weights_full = jnp.where(usable[None, None, :], jnp.exp(scores * HEAD_DIM ** (-0.5)), 0.0)
    denominator = denominator + jnp.sum(weights_full, axis=2)
    numerator = numerator + jnp.einsum(
        "hqk,khd->hqd",
        weights_full.astype(jnp.bfloat16),
        value_heads,
        preferred_element_type=jnp.float32,
    )
    return (numerator, denominator)


def lookup_live(owner_id, live_all):
    slab_ids = jnp.arange(live_all.shape[0], dtype=jnp.int32)
    return jnp.sum(jnp.where(owner_id[:, None] == slab_ids[None, :], live_all[None, :], 0), axis=1)


def per_device(
    history, section, slab_kernel, patch_fine, patch_mid, patch_coarse, modulation, w_qkv
):
    height, breadth = (history.shape[2], history.shape[3])
    capacity = height * breadth
    frame_count = lax.axis_size("frame")
    my_slab = lax.axis_index("frame")
    my_kernel = slab_kernel[my_slab]
    sec_count = section.shape[0]
    hist_part = slab_features(history, my_kernel, (patch_fine, patch_mid, patch_coarse), capacity)
    sec_part = jnp.dot(section, patch_fine, preferred_element_type=jnp.float32).astype(jnp.bfloat16)
    local_rows = jnp.concatenate([hist_part, sec_part], axis=0)
    features = lax.all_gather(shortened(local_rows), ("head", "fsdp"), axis=1, tiled=True).astype(
        local_rows.dtype
    )
    modulated = modulate(features, modulation)
    total_rows = features.shape[0]
    head_count = w_qkv.shape[2] // HEAD_DIM
    hist_pos = slab_positions(my_slab, my_kernel, height, breadth, capacity)
    sec_pos = section_positions(
        my_slab * sec_count, sec_count, height, breadth, float(SLAB_LEN * frame_count)
    )
    positions = jnp.concatenate([hist_pos, sec_pos], axis=0)
    query_raw = jnp.dot(modulated[capacity:], w_qkv[0], preferred_element_type=jnp.float32)
    queries = rotate(rms_norm(query_raw.reshape(sec_count, head_count, HEAD_DIM)), sec_pos).astype(
        jnp.bfloat16
    )
    key_raw = jnp.dot(modulated, w_qkv[1], preferred_element_type=jnp.float32)
    key_rows = rotate(rms_norm(key_raw.reshape(total_rows, head_count, HEAD_DIM)), positions)
    key_rows = key_rows.astype(jnp.bfloat16).reshape(total_rows, head_count * HEAD_DIM)
    values = jnp.dot(modulated, w_qkv[2], preferred_element_type=jnp.float32).astype(jnp.bfloat16)
    live_all = live_count(slab_kernel, height, breadth)
    zero_num = jnp.zeros((head_count, sec_count, HEAD_DIM), jnp.float32)
    zero_den = jnp.zeros((head_count, sec_count), jnp.float32)
    head_rows = capacity // 8
    block_rows = head_rows + sec_count
    sent_keys = jnp.concatenate([key_rows[:head_rows], key_rows[capacity:]], axis=0)
    sent_values = jnp.concatenate([values[:head_rows], values[capacity:]], axis=0)
    running = (zero_num, zero_den)
    pieces = (
        lax.all_gather(sent_keys, "frame", axis=0, tiled=True),
        lax.all_gather(sent_values, "frame", axis=0, tiled=True),
    )
    row_ids = jnp.arange(pieces[0].shape[0], dtype=jnp.int32)
    owner_id = row_ids // block_rows
    local_row = row_ids % block_rows
    usable = (local_row >= head_rows) | (local_row < lookup_live(owner_id, live_all))
    running = accumulate(running[0], running[1], queries, pieces[0], pieces[1], usable)
    slab_ids = jnp.arange(slab_kernel.shape[0], dtype=jnp.int32)
    root = jnp.sum(jnp.where(slab_kernel == 0, slab_ids, 0))
    tail_keys = key_rows[head_rows:capacity]
    tail_values = values[head_rows:capacity]
    all_usable = jnp.ones((capacity - head_rows,), bool)
    far_keys, far_values = (spread(tail_keys, "frame", root), spread(tail_values, "frame", root))
    numerator, denominator = accumulate(
        running[0], running[1], queries, far_keys, far_values, all_usable
    )
    attended = numerator / denominator[:, :, None]
    return (
        attended.transpose(1, 0, 2).reshape(sec_count, head_count * HEAD_DIM).astype(jnp.bfloat16)
    )


def solution(mesh):
    in_specs = (
        P("frame", None, None, None),
        P("frame", None),
        P(),
        P(None, ("head", "fsdp")),
        P(None, ("head", "fsdp")),
        P(None, ("head", "fsdp")),
        P(),
        P(None, None, ("head", "fsdp")),
    )
    out_specs = P("frame", ("head", "fsdp"))
    return jax.shard_map(
        per_device, mesh=mesh, in_specs=in_specs, out_specs=out_specs, check_vma=False
    )
```

profile of v0, /device:TPU:0, one launch (start us, length us, event | category | flops | bytes accessed | tf_op | source)
XLA Modules:
  0.0 392.9 jit_solution(9113811120710670574)
XLA Ops:
  10.2 7.0 %conditional.2 = (bf16[2048,384]{1,0:T(8,128)(2,1)S(1)}) conditional(s32[]{:T(128)} %bitcast.7, (bf16[4,16,8,256]{3,2,1,0:T(8,128)(2,1)}, bf16[64,384]{1,0:T(8,128)(2,1)}) %tuple.18, (bf16[4,16,8,256]{3,2,1,0:T(8,128)(2,1)}, bf16[512,384]{1,0:T(8,128)(2,1)}) %tuple.19, (bf16[4,16,8,256]{3,2,1,0:T(8,128)(2,1)}, ...), branch_computations={%region_1.2_spmd, %region_2.3_spmd, %region_3.4_spmd} | conditional | flops 100663296 | bytes 6078474
  12.1 2.4 copy.44
  14.5 2.5 fusion.55
  21.8 4.3 %slice_bitcast_fusion.1 = (bf16[384,3072]{0,1:T(8,128)(2,1)}, bf16[384,3072]{0,1:T(8,128)(2,1)S(1)}) fusion(bf16[3,3072,384]{2,1,0:T(8,128)(2,1)} %param.26), kind=kLoop, calls=%fused_computation.27 | loop fusion | bytes 9437184 | tf_op jit(solution)/shard_map/dot_general | solution.py:192
  26.1 2.6 copy.51
  29.5 2.0 add_add_fusion
  32.6 5.8 %cosine_bitcast_fusion = (f32[2176,128]{0,1:T(8,128)}, f32[2176,128]{0,1:T(8,128)}) fusion(f32[128,2176]{1,0:T(8,128)S(1)} %gather_fusion.2, f32[128]{0:T(128)S(1)} %copy-done.8, f32[128]{0:T(128)S(1)} %copy-done.7), kind=kLoop, calls=%fused_computation.40 | loop fusion | flops 557056 | bytes 3343360 | tf_op jit(solution)/shard_map/cos | solution.py:59
  38.3 53.5 %all-gather.4.cloned.1.call-done = bf16[2176,3072]{1,0:T(8,128)(2,1)} async-done(((bf16[2176,384]{1,0:T(8,128)(2,1)}), bf16[2176,3072]{1,0:T(8,128)(2,1)}) %all-gather.4.cloned.1.call-update) | async-done | bytes 13369360 | tf_op jit(solution)/shard_map/all_gather | solution.py:181
  91.8 6.6 %convert_reduce_fusion = f32[2176]{0:T(1024)S(1)} fusion(bf16[2176,3072]{1,0:T(8,128)(2,1)} %all-gather.4.cloned.1.call-done), kind=kLoop, calls=%fused_computation.5 | loop fusion | flops 13367168 | bytes 13378048 | tf_op jit(solution)/shard_map/reduce_sum | solution.py:142
  98.4 8.4 %fusion.2 = f32[2176]{0:T(1024)S(1)} fusion(bf16[2176,3072]{1,0:T(8,128)(2,1)} %all-gather.4.cloned.1.call-done, f32[2176]{0:T(1024)S(1)} %broadcast_multiply_fusion.2), kind=kLoop, calls=%fused_computation.8 | loop fusion | flops 26736512 | bytes 13386752 | tf_op jit(solution)/shard_map/reduce_sum | solution.py:143
  106.8 15.3 %fusion.5 = bf16[2176,3072]{1,0:T(8,128)(2,1)} fusion(bf16[2176,3072]{1,0:T(8,128)(2,1)} %all-gather.4.cloned.1.call-done, f32[3072]{0:T(1024)S(1)} %bitcast.110, f32[3072]{0:T(1024)S(1)} %bitcast.109, f32[2176]{0:T(1024)S(1)} %add_rsqrt_fusion.1, f32[2176]{0:T(1024)S(1)} %broadcast_multiply_fusion.2), kind=kLoop, calls=%fused_computation.11 | loop fusion | flops 40108032 | bytes 26780672 | tf_op jit(solution)/shard_map/convert_element_type | solution.py:145
  122.1 12.4 %convolution_convert_fusion = bf16[2176,384]{0,1:T(8,128)(2,1)} fusion(bf16[2176,3072]{1,0:T(8,128)(2,1)} %fusion.5, bf16[3,3072,384]{2,1,0:T(8,128)(2,1)} %param.26), kind=kOutput, calls=%fused_computation.17 | convolution fusion | flops 5134663680 | bytes 17399808 | tf_op jit(solution)/shard_map/dot_general | solution.py:199
  134.5 10.0 %multiply_reduce_fusion = (f32[2176,3]{0,1:T(4,128)S(1)}, f32[2176,3,128]{0,2,1:T(8,128)S(1)}) fusion(bf16[3,128,3072]{2,1,0:T(8,128)(2,1)} %bitcast.107, bf16[2176,3072]{1,0:T(8,128)(2,1)} %fusion.5), kind=kOutput, calls=%fused_computation.21 | convolution fusion | flops 5135492608 | bytes 19097088 | tf_op jit(solution)/shard_map/dot_general | solution.py:196
  144.7 4.4 %copy.52 = f32[2176,3,128]{0,1,2:T(4,128)} copy(f32[2176,3,128]{0,2,1:T(8,128)S(1)} %broadcast_multiply_fusion) | data formatting | bytes 6684672 | tf_op jit(solution)/shard_map/mul | solution.py:65
  150.3 7.3 %gather_fusion.3 = f32[128,2176,3]{1,2,0:T(4,128)} fusion(f32[2176,3,128]{0,1,2:T(4,128)} %copy.52, s32[1024]{0:T(1024)S(1)} %pad_clamp_fusion), kind=kCustom, calls=%fused_computation.3 | custom fusion | bytes 6685184 | tf_op jit(solution)/shard_map/jit(_take)/gather | solution.py:61
  157.6 3.4 fusion.11
  166.6 3.1 copy.48
  170.3 1.9 multiply_reduce_fusion.1
  173.2 84.1 %all-reduce.5.cloned.1.call-done = (bf16[1792,3,128]{0,2,1:T(8,128)(2,1)}, bf16[1792,3,128]{0,2,1:T(8,128)(2,1)}) async-done(((bf16[1792,3,128]{0,2,1:T(8,128)(2,1)}, bf16[1792,3,128]{0,2,1:T(8,128)(2,1)}), (bf16[1792,3,128]{0,2,1:T(8,128)(2,1)}, bf16[1792,3,128]{0,2,1:T(8,128)(2,1)})) %all-reduce.5.cloned.1.call-update) | async-done | bytes 2752528 | tf_op jit(solution)/shard_map/psum | solution.py:28
  257.2 2.1 fusion.52
  261.2 57.6 %all-gather.6.cloned.1.call-done = bf16[6144,384]{0,1:T(8,128)(2,1)} async-done(((bf16[384,384]{0,1:T(8,128)(2,1)}), bf16[6144,384]{0,1:T(8,128)(2,1)}) %all-gather.6.cloned.1.call-update) | async-done | bytes 4718608 | tf_op jit(solution)/shard_map/all_gather | solution.py:209
  318.8 7.2 %fusion.51 = (f32[3,128]{1,0:T(4,128)S(1)}, bf16[3,128,6144]{2,1,0:T(8,128)(2,1)}) fusion(bf16[128,3,128]{0,2,1:T(8,128)(2,1)S(1)} %fusion.31, bf16[6144,3,128]{0,2,1:T(8,128)(2,1)} %bitcast.111, pred[6144]{0:T(1024)(128)(4,1)S(1)} %fusion.39), kind=kOutput, calls=%fused_computation.115 | convolution fusion | flops 613416576 | bytes 9543168 | tf_op jit(solution)/shard_map/qhd,khd->hqk/dot_general | solution.py:152
  325.9 54.2 %all-gather.8.cloned.1.call-done = bf16[6144,384]{0,1:T(8,128)(2,1)} async-done(((bf16[384,384]{0,1:T(8,128)(2,1)}), bf16[6144,384]{0,1:T(8,128)(2,1)}) %all-gather.8.cloned.1.call-update) | async-done | bytes 4718608 | tf_op jit(solution)/shard_map/all_gather | solution.py:210
  380.1 5.2 %fusion.26 = bf16[128,3,128]{0,2,1:T(8,128)(2,1)S(1)} fusion(f32[3,128,128]{1,2,0:T(8,128)S(1)} %fusion.15, bf16[6144,3,128]{0,2,1:T(8,128)(2,1)} %bitcast.102, bf16[3,128,6144]{2,1,0:T(8,128)(2,1)} %get-tuple-element.62, f32[128,3]{0,1:T(4,128)S(1)} %add_bitcast_fusion), kind=kOutput, calls=%fused_computation.37 | convolution fusion | flops 604127232 | bytes 9733632 | tf_op jit(solution)/shard_map/hqk,khd->hqd/dot_general | solution.py:155
  (72 shorter events, 20.4 us)
Async XLA Ops:
  6.5 0.7 copy-start
  6.5 85.3 %all-gather.4.cloned.1.call-start = ((), (), s32[]{:S(2)}) async-start(), calls=%async_computation | async-start | bytes 15040512 | tf_op jit(solution)/shard_map/all_gather | solution.py:181
  17.2 3.3 copy-start.11
  18.5 238.7 %all-reduce.5.cloned.1.call-start = ((), (), s32[]{:S(2)}) async-start(), calls=%async_computation.3 | async-start | bytes 5505024 | tf_op jit(solution)/shard_map/psum | solution.py:28
  26.1 2.7 copy-start.10
  31.5 1.0 copy-start.9
  31.5 1.0 copy-start.6
  31.5 1.0 copy-start.7
  31.5 1.0 copy-start.8
  144.7 4.4 %copy-start.3 = (bf16[2176,384]{0,1:T(8,128)(2,1)S(1)}, bf16[2176,384]{0,1:T(8,128)(2,1)}, u32[]{:S(2)}) copy-start(bf16[2176,384]{0,1:T(8,128)(2,1)} %convolution_convert_fusion) | copy-start | bytes 5013508
  161.0 1.2 copy-start.2
  162.2 3.0 slice-start.2
  162.2 3.0 slice-start.3
  163.4 0.9 slice-start
  163.4 1.0 slice-start.1
  163.4 155.3 %all-gather.6.cloned.1.call-start = ((), (), s32[]{:S(2)}) async-start(), calls=%async_computation.1 | async-start | bytes 5013504 | tf_op jit(solution)/shard_map/all_gather | solution.py:209
  165.2 215.0 %all-gather.8.cloned.1.call-start = ((), (), s32[]{:S(2)}) async-start(), calls=%async_computation.2 | async-start | bytes 5013504 | tf_op jit(solution)/shard_map/all_gather | solution.py:210
  380.1 5.9 %copy-start.1 = (bf16[128,64]{0,1:T(8,128)(2,1)S(1)}, bf16[128,64]{0,1:T(8,128)(2,1)}, u32[]{:S(2)}) copy-start(bf16[128,64]{0,1:T(8,128)(2,1)} %param.20) | copy-start | bytes 49156
Sparse Core Ops, SparseCore 0:
  18.7 73.0 all-gather.3
  163.5 93.6 all-reduce.4
  259.4 59.3 all-gather.5
  320.7 59.3 all-gather.7
where the time goes:
time: 398 us; the launch traced here: 393 us
  waiting for transfers between devices  249 us (63%)
  other arithmetic  48.8 us (12%)
  matrix products  44.1 us (11%)
  local copies, waits for them, and re-layouts  33.5 us (8%)
  between operations  16.4 us (4%)
    psum x1, waiting for transfers between devices, spread(): return lax.psum(kept, axis)  84.1 us
    all_gather x1, waiting for transfers between devices, per_device(): lax.all_gather(sent_keys, 'frame', axis=0, tiled=True)  57.6 us
    all_gather x1, waiting for transfers between devices, per_device(): lax.all_gather(sent_values, 'frame', axis=0, tiled=True)  54.2 us
    all_gather x1, waiting for transfers between devices, per_device(): lax.all_gather(shortened(local_rows), ('head', 'fsdp'), axis=1, tiled=True)  53.5 us
    convert_element_type x1, other arithmetic, modulate(): return (normed * (1.0 + modulation[1]) + modulation[0]).astype(jnp.bfloat16)  15.3 us
    dot_general x1, matrix products, per_device(): jnp.dot(modulated, w_qkv[2], preferred_element_type=jnp.float32)  12.4 us
    dot_general x1, matrix products, per_device(): key_raw = jnp.dot(modulated, w_qkv[1], preferred_element_type=jnp.float32)  9.96 us
    dot_general x2, matrix products, accumulate(): jnp.einsum('qhd,khd->hqk', queries, key_heads, preferred_element_type=jnp...  9.24 us
  transfers between devices with their start and end apart: 4, of which 4 were waited for; matrix products, arithmetic and copies ran while one was open for 9% of the time, Pallas kernels for 0%

commit v1 on v0

v1 whole, which is shorter than its diff:
```python
import functools

import jax
import jax.numpy as jnp
import numpy as np
from jax import lax
from jax.experimental import pallas as pl
from jax.experimental.pallas import tpu as pltpu
from jax.sharding import PartitionSpec as P

HEAD_DIM = 128
PARTS = (16, 56, 56)
THETA = 256.0
EPS = 1e-06
QUERY_SCALE = float(np.log2(np.e) * HEAD_DIM**-0.5)
BF = jnp.bfloat16
F32 = jnp.float32
VMEM = pl.BlockSpec(memory_space=pltpu.VMEM)
SMEM = pl.BlockSpec(memory_space=pltpu.SMEM)


def params(mib=48):
    return pltpu.CompilerParams(vmem_limit_bytes=mib * 2**20)


def cost(flops, bytes_accessed, transcendentals=0):
    return pl.CostEstimate(
        flops=int(flops), bytes_accessed=int(bytes_accessed), transcendentals=int(transcendentals)
    )


def pair_tables():
    freqs = np.zeros((3, 64), np.float64)
    first, second = [], []
    pair, offset = 0, 0
    for axis, width in enumerate(PARTS):
        half = width // 2
        for i in range(half):
            freqs[axis, pair] = THETA ** (-2.0 * i / width)
            first.append(offset + i)
            second.append(offset + i + half)
            pair += 1
        offset += width
    return freqs, np.array(first + second)


def section_tables(frames, per_frame):
    freqs, _ = pair_tables()
    rows = np.arange(frames * per_frame)
    pos = np.stack(
        [4.0 * frames + rows // 512, 2.0 * (rows // 128 % 4) + 0.5, 2.0 * (rows % 128) + 0.5]
    )
    angles = freqs.T @ pos
    return np.cos(angles).astype(np.float32), np.sin(angles).astype(np.float32)


def head_permutation():
    _, order = pair_tables()
    perm = np.zeros((HEAD_DIM, HEAD_DIM), np.float32)
    perm[order, np.arange(HEAD_DIM)] = 1.0
    return perm


def lane_frequencies():
    freqs, _ = pair_tables()
    table = np.zeros((8, HEAD_DIM), np.float32)
    table[:3] = np.concatenate([freqs, freqs], axis=1)
    table[3] = np.concatenate([-np.ones(64), np.ones(64)])
    return table


def dot(a, b, dims=((1,), (0,))):
    return lax.dot_general(a, b, (dims, ((), ())), preferred_element_type=F32)


def select_columns(rows, columns, source):
    j = lax.broadcasted_iota(jnp.int32, (8, columns), 1)[0:1]
    i = lax.broadcasted_iota(jnp.int32, (rows, columns), 0)
    return jnp.where(i == source(j), 1.0, 0.0).astype(BF)


def select_rows(rows, columns, source):
    j = lax.broadcasted_iota(jnp.int32, (rows, columns), 1)
    i = lax.broadcasted_iota(jnp.int32, (rows, 128), 0)[:, 0:1]
    return jnp.where(j == source(i), 1.0, 0.0).astype(BF)


def split(value):
    high = value.astype(BF)
    return high, (value - high.astype(F32)).astype(BF)


def prepare_kernel(kinds_ref, hist_ref, sec_ref, out_ref):
    kind = kinds_ref[lax.axis_index("frame")]
    cells = hist_ref[...]

    own = select_rows(64, 64, lambda i: (i & 31) * 2 + (i >> 5))
    section = dot(own, sec_ref[...], ((1,), (1,))).astype(BF)
    for d in range(16):
        out_ref[d, 64:128, :] = section

    @pl.when(kind == 0)
    def _():
        cols = select_columns(256, 256, lambda j: (j & 127) * 2 + (j >> 7))
        rows = select_rows(
            512,
            512,
            lambda i: (i >> 7) * 128 + ((i >> 1) & 15) * 8 + ((i >> 5) & 3) * 2 + (i & 1),
        )
        out = dot(rows, dot(cells, cols).astype(BF)).astype(BF)
        for d in range(16):
            for w in range(2):
                out_ref[d, 32 * w : 32 * w + 32, :] = out[
                    32 * d : 32 * d + 32, 128 * w : 128 * w + 128
                ]

    @pl.when(kind == 1)
    def _():
        cols = select_columns(256, 256, lambda j: (j & 63) * 4 + (j >> 6))
        lanes = select_columns(
            512,
            512,
            lambda j: ((j >> 8) * 2 + ((j >> 2) & 1)) * 128
            + ((j >> 3) & 15) * 8
            + ((j >> 7) & 1) * 4
            + (j & 3),
        )
        out = dot(dot(cells, cols).astype(BF), lanes, ((0,), (0,))).astype(BF)
        for d in range(16):
            g, q = d // 4, d % 4
            for w in range(4):
                out_ref[d, 16 * w : 16 * w + 16, :] = out[
                    64 * w + 16 * q : 64 * w + 16 * q + 16, 128 * g : 128 * g + 128
                ]

    @pl.when(kind == 2)
    def _():
        lanes = select_columns(
            512, 512, lambda j: ((j >> 3) & 3) * 128 + (j >> 5) * 8 + (j & 7)
        )
        out = dot(cells, lanes, ((0,), (0,))).astype(BF)
        for d in range(16):
            for g in range(4):
                out_ref[d, 16 * g : 16 * g + 16, :] = out[
                    16 * d : 16 * d + 16, 128 * g : 128 * g + 128
                ]


def prepare(kinds, history, section):
    return pl.pallas_call(
        prepare_kernel,
        out_shape=jax.ShapeDtypeStruct((16, 128, 128), BF),
        in_specs=[SMEM, VMEM, VMEM],
        out_specs=VMEM,
        compiler_params=params(),
        cost_estimate=cost(1e9, 1e6),
        name="prepare",
    )(kinds, history.reshape(512, 256), section)


def embed_kernel(kinds_ref, recv_ref, mid_ref, coarse_ref, out_ref, mid_buf, coarse_buf):
    mid_count = jnp.int32(0)
    coarse_count = jnp.int32(0)
    for s in range(16):
        kind = kinds_ref[s]
        block = recv_ref[s, 0:64, :]
        mid_buf[jnp.where(kind == 1, jnp.minimum(mid_count, 6), 7)] = block
        coarse_buf[jnp.where(kind == 2, jnp.minimum(coarse_count, 7), 8)] = block
        mid_count += jnp.where(kind == 1, 1, 0)
        coarse_count += jnp.where(kind == 2, 1, 0)
    tokens = jnp.concatenate(
        [mid_buf[0:7, 16 * w : 16 * w + 16, :].reshape(112, 128) for w in range(4)], axis=1
    )
    order = select_columns(512, 512, lambda j: (j & 3) * 128 + (j >> 2))
    tokens = dot(tokens, order).astype(BF)
    out_ref[0:112, :] = dot(tokens, mid_ref[...]).astype(BF)
    cells = coarse_buf[0:8].reshape(512, 128)
    order = select_rows(
        512,
        512,
        lambda i: ((i >> 1) & 7) * 64 + (i >> 7) * 16 + (i & 1) * 8 + ((i >> 4) & 7),
    )
    cells = dot(order, cells).astype(BF)
    tokens = jnp.concatenate(
        [
            jnp.concatenate(
                [cells[128 * g + 16 * w : 128 * g + 16 * w + 16] for w in range(8)], axis=1
            )
            for g in range(4)
        ],
        axis=0,
    )
    order = select_columns(1024, 1024, lambda j: (j & 7) * 128 + (j >> 3))
    tokens = dot(tokens, order).astype(BF)
    total = jnp.zeros((16, out_ref.shape[1]), F32)
    for g in range(4):
        total += dot(tokens[16 * g : 16 * g + 16], coarse_ref[1024 * g : 1024 * g + 1024, :])
    out_ref[112:128, :] = total.astype(BF)


def embed(kinds, received, patch_mid, patch_coarse):
    return pl.pallas_call(
        embed_kernel,
        out_shape=jax.ShapeDtypeStruct((128, patch_mid.shape[1]), BF),
        in_specs=[SMEM, VMEM, VMEM, VMEM],
        out_specs=VMEM,
        scratch_shapes=[pltpu.VMEM((8, 64, 128), BF), pltpu.VMEM((9, 64, 128), BF)],
        compiler_params=params(),
        cost_estimate=cost(2e9, 5e6),
        name="embed",
    )(kinds, received, patch_mid, patch_coarse)


def gather_columns(block):
    rings = [block] + [
        lax.ppermute(block, "head", [(i, (i + d) % 4) for i in range(4)]) for d in (1, 3, 2)
    ]
    same = jnp.stack([rings[0], rings[1], rings[3], rings[2]])
    other = lax.ppermute(same, "fsdp", [(0, 1), (1, 0)])
    return same, other


def place_columns(same_ref, other_ref, full_ref):
    z, core = lax.axis_index("head"), lax.axis_index("fsdp")
    width = same_ref.shape[2]
    for d in range(4):
        at = ((z + 4 - d) & 3) * 2
        for ref, column in ((same_ref, at + core), (other_ref, at + 1 - core)):
            full_ref[:, pl.ds(pl.multiple_of(column * width, 128), width)] = ref[d]


def fold_kernel(same_ref, other_ref, mod_ref, w_ref, perm_ref, fold_ref, gram_ref, full_ref):
    place_columns(same_ref, other_ref, full_ref)
    order = select_rows(64, 64, lambda i: (i & 31) * 2 + (i >> 5))
    raw = full_ref[...]
    width = raw.shape[1]
    weight = dot(order, raw)
    low = weight.astype(BF)
    mean = jnp.sum(weight, axis=1, keepdims=True) / width
    mean_row = dot(jnp.ones((8, width), BF), low, ((1,), (1,)))[0:1] / width
    gram_ref[...] = dot(low, low, ((1,), (1,))) / width - mean * mean_row
    scaled = (weight - mean) * (1.0 + mod_ref[1:2, :])
    shift_high, shift_low = split(mod_ref[0:1, :])
    pad = jnp.zeros((14, width), BF)
    high, rest = split(scaled)
    left = jnp.concatenate(
        [high, rest, jnp.concatenate([shift_high, shift_low, pad], axis=0)], axis=0
    )
    for part in range(3):
        product = dot(left, w_ref[part])
        matrix = product[0:64] + product[64:128]
        bias = product[128:129] + product[129:130]
        columns = matrix.shape[1]
        high, rest = split(matrix)
        bias_high, bias_low = split(bias)
        rows = jnp.concatenate(
            [
                high.astype(F32),
                rest.astype(F32),
                bias_high.astype(F32),
                bias_high.astype(F32),
                bias_low.astype(F32),
                jnp.zeros((13, columns), F32),
            ],
            axis=0,
        ).astype(BF)
        if part < 2:
            rows = jnp.concatenate(
                [
                    dot(rows[:, HEAD_DIM * h : HEAD_DIM * (h + 1)], perm_ref[...]).astype(BF)
                    for h in range(columns // HEAD_DIM)
                ],
                axis=1,
            )
        fold_ref[part] = rows


def fold(same, other, modulation, w_qkv, perm):
    width, columns = w_qkv.shape[1], w_qkv.shape[2]
    return pl.pallas_call(
        fold_kernel,
        out_shape=(
            jax.ShapeDtypeStruct((3, 144, columns), BF),
            jax.ShapeDtypeStruct((64, 64), F32),
        ),
        in_specs=[VMEM] * 5,
        out_specs=(VMEM, VMEM),
        scratch_shapes=[pltpu.VMEM((64, width), BF)],
        compiler_params=params(),
        cost_estimate=cost(2e9, 8e6),
        name="fold",
    )(same, other, modulation, w_qkv, perm)


def turn_rows(keys, cosine, sine):
    return keys * cosine + pltpu.roll(keys, 64, 1) * sine


def row_angles(kinds_ref, freq_ref):
    me = lax.axis_index("frame")
    row = lax.broadcasted_iota(jnp.int32, (128, 128), 0)
    slot = row >> 4
    slab = jnp.zeros((128, 128), F32)
    mid_count = jnp.int32(0)
    coarse_count = jnp.int32(0)
    fine_slab = jnp.int32(0)
    coarse_slot = jnp.where(slot == 7, (row >> 1) & 7, -1)
    for s in range(16):
        kind = kinds_ref[s]
        is_mid, is_coarse = kind == 1, kind == 2
        slab = jnp.where(slot == jnp.where(is_mid, mid_count, 99), float(s), slab)
        slab = jnp.where(coarse_slot == jnp.where(is_coarse, coarse_count, 99), float(s), slab)
        mid_count += jnp.where(is_mid, 1, 0)
        coarse_count += jnp.where(is_coarse, 1, 0)
        fine_slab += jnp.where(kind == 0, s, 0)
    coarse = slot == 7
    whole = me.astype(F32)
    block = (me >> 2).astype(F32)
    quarter = (me & 3).astype(F32)
    frame_half = (me >> 3).astype(F32)
    row_half = ((me >> 2) & 1).astype(F32)
    at = (row & 15).astype(F32)
    t = 4.0 * slab + jnp.where(coarse, 1.5, 2.0 * frame_half + 0.5)
    h = jnp.where(coarse, 3.5, 4.0 * row_half + 1.5)
    w = jnp.where(
        coarse,
        8.0 * (2.0 * whole + (row & 1).astype(F32)) + 3.5,
        4.0 * (16.0 * quarter + at) + 1.5,
    )
    freq_t, freq_h, freq_w, sign = (freq_ref[i : i + 1, :] for i in range(4))
    angles = t * freq_t + h * freq_h + w * freq_w
    fine_t = 4.0 * fine_slab.astype(F32) + block
    fine_angles = (
        fine_t * freq_t
        + (2.0 * quarter + 0.5) * freq_h
        + (2.0 * row.astype(F32) + 0.5) * freq_w
    )
    return (
        (jnp.cos(angles), jnp.sin(angles) * sign),
        (jnp.cos(fine_angles), jnp.sin(fine_angles) * sign),
        fine_slab,
    )


def query_kernel(
    kinds_ref,
    recv_ref,
    fold_ref,
    gram_ref,
    cos_ref,
    sin_ref,
    freq_ref,
    query_ref,
    own_ref,
    key_ref,
    value_ref,
    table_ref,
    patch_ref,
    scale_ref,
):
    (cos_far, sin_far), (cos_fine, sin_fine), fine_slab = row_angles(kinds_ref, freq_ref)
    table_ref[0] = cos_far
    table_ref[1] = sin_far
    count = query_ref.shape[1]
    heads = query_ref.shape[0] // HEAD_DIM
    patches = jnp.concatenate(
        [recv_ref[f, 64:128, :] for f in range(16)] + [recv_ref[fine_slab, 0:64, :]], axis=1
    )
    one, rest = split(gram_ref[...])
    two, three = split(gram_ref[...] - one.astype(F32))
    gram = jnp.concatenate([one, two, three], axis=1)
    spread = dot(gram, jnp.concatenate([patches, patches, patches], axis=0))
    variance = jnp.sum(spread * patches.astype(F32), axis=0, keepdims=True)
    variance = jnp.maximum(variance, 0.0) + EPS
    deviation = jnp.sqrt(variance)
    dev_high, dev_low = split(deviation)
    rows = lax.broadcasted_iota(jnp.int32, (16, patches.shape[1]), 0)
    extra = jnp.where(
        rows == 1,
        dev_low.astype(F32),
        jnp.where((rows == 0) | (rows == 2), dev_high.astype(F32), 0.0),
    ).astype(BF)
    patches = jnp.concatenate([patches, patches, extra], axis=0)
    patch_ref[...] = patches[:, 0:count]
    scale_ref[0:1, :] = variance[:, 0:count]
    scale_ref[1:2, :] = lax.rsqrt(variance[:, 0:count])
    for h in range(heads):
        at = slice(HEAD_DIM * h, HEAD_DIM * (h + 1))
        raw = dot(fold_ref[0][:, at], patches[:, 0:count], ((0,), (0,)))
        square = jnp.sum(raw * raw, axis=0, keepdims=True) / HEAD_DIM
        factor = lax.rsqrt(square + EPS * variance[:, 0:count]) * QUERY_SCALE
        a, b = raw[0:64] * factor, raw[64:128] * factor
        cosine, sine = cos_ref[...], sin_ref[...]
        turned = jnp.concatenate([a * cosine - b * sine, b * cosine + a * sine], axis=0)
        query_ref[at, :] = turned.astype(BF)
        me = lax.axis_index("frame")
        own_ref[at, :] = query_ref[at, pl.ds(pl.multiple_of(me * 128, 128), 128)]
    fine = patches[:, count:]
    fine_variance = jnp.transpose(jnp.broadcast_to(variance[:, count:], (128, 128)))
    value_ref[...] = (
        dot(fine, fold_ref[2], ((0,), (0,)))
        * jnp.concatenate([lax.rsqrt(fine_variance)] * heads, axis=1)
    ).astype(BF)
    for h in range(heads):
        at = slice(HEAD_DIM * h, HEAD_DIM * (h + 1))
        raw = dot(fine, fold_ref[1][:, at], ((0,), (0,)))
        square = jnp.sum(raw * raw, axis=1, keepdims=True) / HEAD_DIM
        raw = raw * lax.rsqrt(square + EPS * fine_variance)
        key_ref[:, at] = turn_rows(raw, cos_fine, sin_fine).astype(BF)


def make_queries(kinds, received, folded, gram, cosine, sine, freqs):
    columns = folded.shape[2]
    count = cosine.shape[1]
    return pl.pallas_call(
        query_kernel,
        out_shape=(
            jax.ShapeDtypeStruct((columns, count), BF),
            jax.ShapeDtypeStruct((columns, 128), BF),
            jax.ShapeDtypeStruct((128, columns), BF),
            jax.ShapeDtypeStruct((128, columns), BF),
            jax.ShapeDtypeStruct((2, 128, 128), F32),
            jax.ShapeDtypeStruct((144, count), BF),
            jax.ShapeDtypeStruct((8, count), F32),
        ),
        in_specs=[SMEM] + [VMEM] * 6,
        out_specs=tuple([VMEM] * 7),
        compiler_params=params(),
        cost_estimate=cost(2e9, 8e6),
        name="queries",
    )(kinds, received, folded, gram, cosine, sine, freqs)


def history_kernel(
    same_ref,
    other_ref,
    mod_ref,
    w_ref,
    perm_ref,
    table_ref,
    query_ref,
    key_ref,
    value_ref,
    out_ref,
    full_ref,
):
    place_columns(same_ref, other_ref, full_ref)
    heads = query_ref.shape[0] // HEAD_DIM
    count = query_ref.shape[1]
    x = full_ref[...].astype(F32)
    x = x - jnp.mean(x, axis=1, keepdims=True)
    x = x * lax.rsqrt(jnp.mean(x * x, axis=1, keepdims=True) + EPS)
    x = (x * (1.0 + mod_ref[1:2, :]) + mod_ref[0:1, :]).astype(BF)
    raw_keys = dot(x, w_ref[1])
    values = dot(x, w_ref[2])
    chunk = 512
    sums = []
    for h in range(heads):
        at = slice(HEAD_DIM * h, HEAD_DIM * (h + 1))
        raw = raw_keys[:, at]
        raw = raw * lax.rsqrt(jnp.mean(raw * raw, axis=1, keepdims=True) + EPS)
        high, rest = split(raw)
        raw = dot(high, perm_ref[...]) + dot(rest, perm_ref[...])
        keys = jnp.concatenate(
            [turn_rows(raw, table_ref[0], table_ref[1]).astype(BF), key_ref[:, at]], axis=0
        )
        value_rows = jnp.concatenate([values[:, at], value_ref[:, at].astype(F32)], axis=0)
        value_columns = jnp.transpose(value_rows).astype(BF)
        row_sums = []
        for c in range(count // chunk):
            scores = dot(keys, query_ref[at, chunk * c : chunk * (c + 1)])
            weights = jnp.exp2(scores)
            row_sums.append(jnp.sum(weights, axis=0, keepdims=True))
            part = dot(value_columns, weights.astype(BF)).astype(BF)
            for d in range(chunk // 128):
                out_ref[c * (chunk // 128) + d, at, :] = part[:, 128 * d : 128 * d + 128]
        sums.append(jnp.concatenate(row_sums, axis=1))
    rows = lax.broadcasted_iota(jnp.int32, (16, count), 0)
    tail = jnp.zeros((16, count), F32)
    for h in range(heads):
        high, rest = split(sums[h])
        tail = jnp.where(rows == h, high.astype(F32), tail)
        tail = jnp.where(rows == heads + h, rest.astype(F32), tail)
    tail = tail.astype(BF)
    for d in range(count // 128):
        out_ref[d, HEAD_DIM * heads :, :] = tail[:, 128 * d : 128 * d + 128]


def attend_history(same, other, modulation, w_qkv, perm, table, queries, keys, values):
    columns, count = queries.shape
    return pl.pallas_call(
        history_kernel,
        out_shape=jax.ShapeDtypeStruct((count // 128, columns + 16, 128), BF),
        in_specs=[VMEM] * 9,
        out_specs=VMEM,
        scratch_shapes=[pltpu.VMEM((128, w_qkv.shape[1]), BF)],
        compiler_params=params(),
        cost_estimate=cost(4e9, 1e7, 2e6),
        name="history",
    )(same, other, modulation, w_qkv, perm, table, queries, keys, values)


def section_kernel(patch_ref, scale_ref, fold_ref, own_ref, cos_ref, sin_ref, num_ref, den_ref):
    heads = own_ref.shape[0] // HEAD_DIM
    variance = scale_ref[0:1, :]
    inverse = scale_ref[1:2, :]
    ones = jnp.ones((8, patch_ref.shape[1]), BF)
    for h in range(heads):
        at = slice(HEAD_DIM * h, HEAD_DIM * (h + 1))
        raw = dot(fold_ref[1][:, at], patch_ref[...], ((0,), (0,)))
        square = jnp.sum(raw * raw, axis=0, keepdims=True) / HEAD_DIM
        factor = lax.rsqrt(square + EPS * variance)
        a, b = raw[0:64] * factor, raw[64:128] * factor
        cosine, sine = cos_ref[...], sin_ref[...]
        keys = jnp.concatenate([a * cosine - b * sine, b * cosine + a * sine], axis=0).astype(BF)
        values = (dot(fold_ref[2][:, at], patch_ref[...], ((0,), (0,))) * inverse).astype(BF)
        weights = jnp.exp2(dot(own_ref[at, :], keys, ((0,), (0,)))).astype(BF)
        num_ref[at, :] = dot(values, weights, ((1,), (1,)))
        den_ref[8 * h : 8 * h + 8, :] = dot(ones, weights, ((1,), (1,)))


def attend_section(patches, scales, folded, own, cosine, sine):
    columns = own.shape[0]
    return pl.pallas_call(
        section_kernel,
        out_shape=(
            jax.ShapeDtypeStruct((columns, 128), F32),
            jax.ShapeDtypeStruct((8 * columns // HEAD_DIM, 128), F32),
        ),
        in_specs=[VMEM] * 6,
        out_specs=(VMEM, VMEM),
        compiler_params=params(),
        cost_estimate=cost(4e9, 1e7, 2e6),
        name="section",
    )(patches, scales, folded, own, cosine, sine)


def combine_kernel(part_ref, num_ref, den_ref, out_ref):
    columns = num_ref.shape[0]
    heads = columns // HEAD_DIM
    total = num_ref[...]
    tail = jnp.zeros((16, 128), F32)
    for f in range(part_ref.shape[0]):
        total += part_ref[f, 0:columns, :].astype(F32)
        tail += part_ref[f, columns:, :].astype(F32)
    for h in range(heads):
        at = slice(HEAD_DIM * h, HEAD_DIM * (h + 1))
        denominator = den_ref[8 * h : 8 * h + 1] + tail[h : h + 1] + tail[heads + h : heads + h + 1]
        out_ref[:, at] = jnp.transpose(total[at] / denominator).astype(BF)


def combine(parts, numerator, denominator):
    columns = numerator.shape[0]
    return pl.pallas_call(
        combine_kernel,
        out_shape=jax.ShapeDtypeStruct((128, columns), BF),
        in_specs=[VMEM] * 3,
        out_specs=VMEM,
        compiler_params=params(),
        cost_estimate=cost(1e7, 2e6),
        name="combine",
    )(parts, numerator, denominator)


def per_device(
    history, section, slab_kernel, patch_fine, patch_mid, patch_coarse, modulation, w_qkv
):
    frames = lax.axis_size("frame")
    cos_table, sin_table = section_tables(frames, section.shape[0])
    cosine, sine = jnp.asarray(cos_table), jnp.asarray(sin_table)
    perm = jnp.asarray(head_permutation(), BF)
    freqs = jnp.asarray(lane_frequencies())

    sent = prepare(slab_kernel, history, section)
    received = lax.all_to_all(sent, "frame", 0, 0, tiled=True)
    fine_same, fine_other = gather_columns(patch_fine)
    folded, gram = fold(fine_same, fine_other, modulation, w_qkv, perm)
    features = embed(slab_kernel, received, patch_mid, patch_coarse)
    same, other = gather_columns(features)
    queries, own, keys, values, table, patches, scales = make_queries(
        slab_kernel, received, folded, gram, cosine, sine, freqs
    )
    parts = attend_history(same, other, modulation, w_qkv, perm, table, queries, keys, values)
    parts = lax.all_to_all(parts, "frame", 0, 0, tiled=True)
    numerator, denominator = attend_section(patches, scales, folded, own, cosine, sine)
    return combine(parts, numerator, denominator)


def solution(mesh):
    in_specs = (
        P("frame", None, None, None),
        P("frame", None),
        P(),
        P(None, ("head", "fsdp")),
        P(None, ("head", "fsdp")),
        P(None, ("head", "fsdp")),
        P(),
        P(None, None, ("head", "fsdp")),
    )
    out_specs = P("frame", ("head", "fsdp"))
    return jax.shard_map(
        per_device, mesh=mesh, in_specs=in_specs, out_specs=out_specs, check_vma=False
    )
```

time: 398 us -> 91.1 us (0.23); the launches traced: 393 us -> 90.1 us
  waiting for transfers between devices: 249 us -> 35.7 us
  other arithmetic: 48.8 us -> 0.1 us
  matrix products: 44.1 us -> 0 us
  local copies, waits for them, and re-layouts: 33.5 us -> 6.23 us
  Pallas kernels: 0 us -> 25.2 us
  starting transfers between devices: 0.65 us -> 22.7 us
  between operations: 16.4 us -> 0.19 us
    all_gather x3 -> x0, waiting for transfers between devices: 165 us -> none  [the longest x1 57.6 us: per_device(): lax.all_gather(sent_keys, 'frame', axis=0, tiled=True)]
    psum x1 -> x0, waiting for transfers between devices: 84.1 us -> none  [spread(): return lax.psum(kept, axis)]
    dot_general x9 -> x0, matrix products: 44.1 us -> none  [the longest x1 12.4 us: per_device(): jnp.dot(modulated, w_qkv[2], preferred_element_type=jnp.float32)]
    all_to_all x0 -> x2, waiting for transfers between devices: none -> 30.2 us  [the longest x1 24.6 us: per_device(): parts = lax.all_to_all(parts, 'frame', 0, 0, tiled=True)]
    pallas_call x0 -> x7, Pallas kernels: none -> 25.2 us  [the longest x1 9.24 us: attend_history(): pl.pallas_call(history_kernel, out_shape=jax.ShapeDtypeStruct((count // 1...]
    convert_element_type x3 -> x0, other arithmetic: 18.7 us -> none  [the longest x1 15.3 us: modulate(): return (normed * (1.0 + modulation[1]) + modulation[0]).astype(jnp.bfloat16)]
    reduce_sum x3 -> x0, other arithmetic: 15.1 us -> none  [the longest x1 8.39 us: modulate(): variance = jnp.mean(centered * centered, axis=-1, keepdims=True)]
    ppermute x0 -> x8, starting transfers between devices: none -> 11.6 us  [the longest x6 11.3 us: gather_columns(): lax.ppermute(block, 'head', [(i, (i + d) % 4) for i in range(4)])]
  transfers between devices with their start and end apart: 4 -> 10, of which waited for: 4 -> 5; matrix products, arithmetic and copies ran while one was open for 9% -> 0% of each run, Pallas kernels for 0% -> 15%
where the time goes in v1:
time: 91.1 us; the launch traced here: 90.1 us
  waiting for transfers between devices  35.7 us (39%)
  Pallas kernels  25.2 us (28%)
  starting transfers between devices  22.7 us (25%)
  local copies, waits for them, and re-layouts  6.23 us (7%)
    all_to_all x1, waiting for transfers between devices, per_device(): parts = lax.all_to_all(parts, 'frame', 0, 0, tiled=True)  24.6 us
    ppermute x6, starting transfers between devices, gather_columns(): lax.ppermute(block, 'head', [(i, (i + d) % 4) for i in range(4)])  11.3 us
    pallas_call x1, Pallas kernels, attend_history(): pl.pallas_call(history_kernel, out_shape=jax.ShapeDtypeStruct((count // 1...  9.24 us
    all_to_all x1, starting transfers between devices, per_device(): received = lax.all_to_all(sent, 'frame', 0, 0, tiled=True)  7.34 us
    unnamed x27, local copies, waits for them, and re-layouts  6.23 us
    all_to_all x1, waiting for transfers between devices, per_device(): received = lax.all_to_all(sent, 'frame', 0, 0, tiled=True)  5.53 us
    ppermute x6, waiting for transfers between devices, gather_columns(): lax.ppermute(block, 'head', [(i, (i + d) % 4) for i in range(4)])  5.5 us
    pallas_call x1, Pallas kernels, fold(): pl.pallas_call(fold_kernel, out_shape=(jax.ShapeDtypeStruct((3, 144, colu...  5.34 us
  transfers between devices with their start and end apart: 10, of which 5 were waited for; matrix products, arithmetic and copies ran while one was open for 0% of the time, Pallas kernels for 15%

profile of v1, /device:TPU:0, one launch (start us, length us, event | category | flops | bytes accessed | tf_op | source)
XLA Modules:
  0.0 90.1 jit_solution(2233027092643621733)
XLA Ops:
  0.0 0.8 copy.13.sec_ref
  0.8 0.9 %copy-done.4 = bf16[4,16,8,256]{3,2,1,0:T(8,128)(2,1)S(1)} copy-done((bf16[4,16,8,256]{3,2,1,0:T(8,128)(2,1)S(1)}, bf16[4,16,8,256]{3,2,1,0:T(8,128)(2,1)}, u32[]{:S(2)}) %copy-start.4) | copy-done | bytes 262168
  2.4 1.9 %prepare.1 = bf16[16,128,128]{2,1,0:T(8,128)(2,1)} custom-call(s32[16]{0:T(128)S(1)} %copy-done.5, bf16[512,256]{1,0:T(8,128)(2,1)S(1)} %bitcast.10, bf16[128,64]{1,0:T(8,128)(2,1)S(1)} %copy.13.sec_ref), custom_call_target="tpu_custom_call" | custom-call | flops 1000000000 | bytes 1000000 | tf_op jit(solution)/shard_map/prepare/pallas_call | solution.py:150
  4.3 7.3 %all-to-all-start = ((bf16[16,128,128]{2,1,0:T(8,128)(2,1)}), bf16[16,128,128]{2,1,0:T(8,128)(2,1)S(1)}, u32[]{:S(2)}, u32[]{:S(2)}) async-start(bf16[16,128,128]{2,1,0:T(8,128)(2,1)} %prepare.1), calls=%async_computation | async-start | bytes 1048576 | tf_op jit(solution)/shard_map/all_to_all | solution.py:575
  11.7 2.0 %collective-permute-start.4 = (bf16[64,384]{1,0:T(8,128)(2,1)S(1)}, bf16[64,384]{1,0:T(8,128)(2,1)S(1)}, u32[]{:S(2)}, u32[]{:S(2)}) collective-permute-start(bf16[64,384]{1,0:T(8,128)(2,1)S(1)} %copy-done.12), channel_id=1, source_target_pairs={{0,2},{2,4},{4,6},{6,0},{1,3},{3,5},{5,7},{7,1},{8,10},{10,12},{12... | collective-permute-start | bytes 147464 | tf_op jit(solution)/shard_map/ppermute | solution.py:216
  13.7 2.2 %collective-permute-start.6 = (bf16[64,384]{1,0:T(8,128)(2,1)S(1)}, bf16[64,384]{1,0:T(8,128)(2,1)S(1)}, u32[]{:S(2)}, u32[]{:S(2)}) collective-permute-start(bf16[64,384]{1,0:T(8,128)(2,1)S(1)} %copy-done.12), channel_id=1, source_target_pairs={{0,6},{2,0},{4,2},{6,4},{1,7},{3,1},{5,3},{7,5},{8,14},{10,8},{12,... | collective-permute-start | bytes 147464 | tf_op jit(solution)/shard_map/ppermute | solution.py:216
  15.9 1.8 %collective-permute-start.5 = (bf16[64,384]{1,0:T(8,128)(2,1)S(1)}, bf16[64,384]{1,0:T(8,128)(2,1)S(1)}, u32[]{:S(2)}, u32[]{:S(2)}) collective-permute-start(bf16[64,384]{1,0:T(8,128)(2,1)S(1)} %copy-done.12), channel_id=1, source_target_pairs={{0,4},{2,6},{4,0},{6,2},{1,5},{3,7},{5,1},{7,3},{8,12},{10,14},{12... | collective-permute-start | bytes 147464 | tf_op jit(solution)/shard_map/ppermute | solution.py:216
  17.7 5.5 %all-to-all-done.recv_ref = bf16[16,128,128]{2,1,0:T(8,128)(2,1)S(1)} async-done(((bf16[16,128,128]{2,1,0:T(8,128)(2,1)}), bf16[16,128,128]{2,1,0:T(8,128)(2,1)S(1)}, u32[]{:S(2)}, u32[]{:S(2)}) %all-to-all-start) | async-done | bytes 524320 | tf_op jit(solution)/shard_map/all_to_all | solution.py:575
  23.2 1.9 %copy-done.2 = bf16[4096,384]{1,0:T(8,128)(2,1)S(1)} copy-done((bf16[4096,384]{1,0:T(8,128)(2,1)S(1)}, bf16[4096,384]{1,0:T(8,128)(2,1)}, u32[]{:S(2)}) %copy-start.2) | copy-done | bytes 3145752
  25.1 2.3 %embed.1 = bf16[128,384]{1,0:T(8,128)(2,1)S(1)} custom-call(s32[16]{0:T(128)S(1)} %copy-done.6, bf16[16,128,128]{2,1,0:T(8,128)(2,1)S(1)} %all-to-all-done.recv_ref, bf16[512,384]{1,0:T(8,128)(2,1)S(1)} %copy-done.3, bf16[4096,384]{1,0:T(8,128)(2,1)S(1)} %copy-done.2), custom_call_target="tpu_custom_call" | custom-call | flops 2000000000 | bytes 5000000 | tf_op jit(solution)/shard_map/embed/pallas_call | solution.py:202
  27.4 4.1 %collective-permute-start.2 = (bf16[128,384]{1,0:T(8,128)(2,1)S(1)}, bf16[128,384]{1,0:T(8,128)(2,1)S(1)}, u32[]{:S(2)}, u32[]{:S(2)}) collective-permute-start(bf16[128,384]{1,0:T(8,128)(2,1)S(1)} %embed.1), channel_id=1, source_target_pairs={{0,6},{2,0},{4,2},{6,4},{1,7},{3,1},{5,3},{7,5},{8,14},{10,8},{12,... | collective-permute-start | bytes 294920 | tf_op jit(solution)/shard_map/ppermute | solution.py:216
  31.5 1.3 %collective-permute-start = (bf16[128,384]{1,0:T(8,128)(2,1)S(1)}, bf16[128,384]{1,0:T(8,128)(2,1)S(1)}, u32[]{:S(2)}, u32[]{:S(2)}) collective-permute-start(bf16[128,384]{1,0:T(8,128)(2,1)S(1)} %embed.1), channel_id=1, source_target_pairs={{0,2},{2,4},{4,6},{6,0},{1,3},{3,5},{5,7},{7,1},{8,10},{10,12},{12... | collective-permute-start | bytes 294920 | tf_op jit(solution)/shard_map/ppermute | solution.py:216
  32.9 1.8 %collective-permute-done.2 = bf16[128,384]{1,0:T(8,128)(2,1)S(1)} collective-permute-done((bf16[128,384]{1,0:T(8,128)(2,1)S(1)}, bf16[128,384]{1,0:T(8,128)(2,1)S(1)}, u32[]{:S(2)}, u32[]{:S(2)}) %collective-permute-start.2) | collective-permute-done | bytes 98336 | tf_op jit(solution)/shard_map/ppermute | solution.py:216
  34.7 3.0 %collective-permute-done.1 = bf16[128,384]{1,0:T(8,128)(2,1)S(1)} collective-permute-done((bf16[128,384]{1,0:T(8,128)(2,1)S(1)}, bf16[128,384]{1,0:T(8,128)(2,1)S(1)}, u32[]{:S(2)}, u32[]{:S(2)}) %collective-permute-start.1) | collective-permute-done | bytes 98336 | tf_op jit(solution)/shard_map/ppermute | solution.py:216
  37.7 0.7 collective-permute-done
  38.8 5.3 %fold.1 = (bf16[3,144,384]{2,1,0:T(8,128)(2,1)S(1)}, f32[64,64]{1,0:T(8,128)S(1)}) custom-call(bf16[4,64,384]{2,1,0:T(8,128)(2,1)S(1)} %pad_maximum_fusion.1.same_ref, bf16[4,64,384]{2,1,0:T(8,128)(2,1)S(1)} %collective-permute-done.7.other_ref, f32[2,3072]{1,0:T(2,128)S(1)} %copy-done.1, bf16[3,3072,384]{2,1,0:T(8,128)(2,1)} %w_ref.3, ...), custom_call_target="tpu_custom_call" | custom-call | flops 2000000000 | bytes 8000000 | tf_op jit(solution)/shard_map/fold/pallas_call | solution.py:280
  44.1 2.9 %queries.1 = (bf16[384,2048]{1,0:T(8,128)(2,1)S(1)}, bf16[384,128]{1,0:T(8,128)(2,1)S(1)}, bf16[128,384]{1,0:T(8,128)(2,1)S(1)}, bf16[128,384]{1,0:T(8,128)(2,1)...) custom-call(s32[16]{0:T(128)S(1)} %copy-done.6, ...), custom_call_target="tpu_custom_call" | custom-call | flops 2000000000 | bytes 8000000 | tf_op jit(solution)/shard_map/queries/pallas_call | solution.py:415
  47.0 0.8 copy-done.10
  47.8 9.2 %history.1 = bf16[16,400,128]{2,1,0:T(8,128)(2,1)} custom-call(bf16[4,128,384]{2,1,0:T(8,128)(2,1)S(1)} %pad_maximum_fusion.same_ref, bf16[4,128,384]{2,1,0:T(8,128)(2,1)S(1)} %collective-permute-done.3.other_ref, f32[2,3072]{1,0:T(2,128)S(1)} %copy-done.1, bf16[3,3072,384]{2,1,0:T(8,128)(2,1)} %w_ref.3, bf16[128,128]{1,0:T(8,128)(2,1)S(1)} %copy-done, ...), custom_call_target="tpu_custom_call" | custom-call | flops 4000000000 | bytes 10000000 | tf_op jit(solution)/shard_map/history/pallas_call | solution.py:491
  57.1 3.7 %all-to-all-start.1 = ((bf16[16,400,128]{2,1,0:T(8,128)(2,1)}), bf16[16,400,128]{2,1,0:T(8,128)(2,1)S(1)}, u32[]{:S(2)}, u32[]{:S(2)}) async-start(bf16[16,400,128]{2,1,0:T(8,128)(2,1)} %history.1), calls=%async_computation.1 | async-start | bytes 3276800 | tf_op jit(solution)/shard_map/all_to_all | solution.py:584
  60.8 1.1 %copy-done.11 = bf16[144,2048]{1,0:T(8,128)(2,1)S(1)} copy-done((bf16[144,2048]{1,0:T(8,128)(2,1)S(1)}, bf16[144,2048]{1,0:T(8,128)(2,1)}, u32[]{:S(2)}) %copy-start.11) | copy-done | bytes 589848
  61.9 2.6 %section.1 = (f32[384,128]{1,0:T(8,128)S(1)}, f32[24,128]{1,0:T(8,128)S(1)}) custom-call(bf16[144,2048]{1,0:T(8,128)(2,1)S(1)} %copy-done.11, f32[8,2048]{1,0:T(8,128)S(1)} %get-tuple-element.23.scale_ref, bf16[3,144,384]{2,1,0:T(8,128)(2,1)S(1)} %get-tuple-element.16.fold_ref, bf16[384,128]{1,0:T(8,128)(2,1)S(1)} %get-tuple-element.24.own_ref, ...), custom_call_target="tpu_custom_call" | custom-call | flops 4000000000 | bytes 10000000 | tf_op jit(solution)/shard_map/section/pallas_call | solution.py:524
  64.5 24.6 %all-to-all-done.1.part_ref = bf16[16,400,128]{2,1,0:T(8,128)(2,1)S(1)} async-done(((bf16[16,400,128]{2,1,0:T(8,128)(2,1)}), bf16[16,400,128]{2,1,0:T(8,128)(2,1)S(1)}, u32[]{:S(2)}, u32[]{:S(2)}) %all-to-all-start.1) | async-done | bytes 1638432 | tf_op jit(solution)/shard_map/all_to_all | solution.py:584
  89.1 0.9 %combine.1 = bf16[128,384]{1,0:T(8,128)(2,1)} custom-call(bf16[16,400,128]{2,1,0:T(8,128)(2,1)S(1)} %all-to-all-done.1.part_ref, f32[384,128]{1,0:T(8,128)S(1)} %get-tuple-element.25.num_ref, f32[24,128]{1,0:T(8,128)S(1)} %get-tuple-element.26.den_ref), custom_call_target="tpu_custom_call" | custom-call | flops 10000000 | bytes 2000000 | tf_op jit(solution)/shard_map/combine/pallas_call | solution.py:554
  (32 shorter events, 1.2 us)
Async XLA Ops:
  0.8 1.0 %copy-start.4 = (bf16[4,16,8,256]{3,2,1,0:T(8,128)(2,1)S(1)}, bf16[4,16,8,256]{3,2,1,0:T(8,128)(2,1)}, u32[]{:S(2)}) copy-start(bf16[4,16,8,256]{3,2,1,0:T(8,128)(2,1)} %param.12) | copy-start | bytes 786436
  1.8 0.7 copy-start.5
  2.4 9.2 %copy-start.12 = (bf16[64,384]{1,0:T(8,128)(2,1)S(1)}, bf16[64,384]{1,0:T(8,128)(2,1)}, u32[]{:S(2)}) copy-start(bf16[64,384]{1,0:T(8,128)(2,1)} %param.15) | copy-start | bytes 147460
  2.4 20.8 %copy-start.3 = (bf16[512,384]{1,0:T(8,128)(2,1)S(1)}, bf16[512,384]{1,0:T(8,128)(2,1)}, u32[]{:S(2)}) copy-start(bf16[512,384]{1,0:T(8,128)(2,1)} %mid_ref.1) | copy-start | bytes 1179652
  2.4 20.8 %copy-start.6 = (s32[16]{0:T(128)S(1)}, s32[16]{0:T(128)}, u32[]{:S(2)}) copy-start(s32[16]{0:T(128)} %kinds_ref.5) | copy-start | bytes 196
  4.3 18.9 %all-to-all-start = ((bf16[16,128,128]{2,1,0:T(8,128)(2,1)}), bf16[16,128,128]{2,1,0:T(8,128)(2,1)S(1)}, u32[]{:S(2)}, u32[]{:S(2)}) async-start(bf16[16,128,128]{2,1,0:T(8,128)(2,1)} %prepare.1), calls=%async_computation | async-start | bytes 1048576 | tf_op jit(solution)/shard_map/all_to_all | solution.py:575
  11.7 27.1 %copy-start = (bf16[128,128]{1,0:T(8,128)(2,1)S(1)}, bf16[128,128]{1,0:T(8,128)(2,1)}, u32[]{:S(2)}) copy-start(bf16[128,128]{1,0:T(8,128)(2,1)} %constant.10.clone.perm_ref) | copy-start | bytes 98308
  11.7 27.1 %copy-start.1 = (f32[2,3072]{1,0:T(2,128)S(1)}, f32[2,3072]{1,0:T(2,128)}, u32[]{:S(2)}) copy-start(f32[2,3072]{1,0:T(2,128)} %mod_ref.3) | copy-start | bytes 73732
  11.7 19.8 %collective-permute-start.4 = (bf16[64,384]{1,0:T(8,128)(2,1)S(1)}, bf16[64,384]{1,0:T(8,128)(2,1)S(1)}, u32[]{:S(2)}, u32[]{:S(2)}) collective-permute-start(bf16[64,384]{1,0:T(8,128)(2,1)S(1)} %copy-done.12), channel_id=1, source_target_pairs={{0,2},{2,4},{4,6},{6,0},{1,3},{3,5},{5,7},{7,1},{8,10},{10,12},{12... | collective-permute-start | bytes 147464 | tf_op jit(solution)/shard_map/ppermute | solution.py:216
  13.7 19.0 %collective-permute-start.6 = (bf16[64,384]{1,0:T(8,128)(2,1)S(1)}, bf16[64,384]{1,0:T(8,128)(2,1)S(1)}, u32[]{:S(2)}, u32[]{:S(2)}) collective-permute-start(bf16[64,384]{1,0:T(8,128)(2,1)S(1)} %copy-done.12), channel_id=1, source_target_pairs={{0,6},{2,0},{4,2},{6,4},{1,7},{3,1},{5,3},{7,5},{8,14},{10,8},{12,... | collective-permute-start | bytes 147464 | tf_op jit(solution)/shard_map/ppermute | solution.py:216
  15.9 16.8 %collective-permute-start.5 = (bf16[64,384]{1,0:T(8,128)(2,1)S(1)}, bf16[64,384]{1,0:T(8,128)(2,1)S(1)}, u32[]{:S(2)}, u32[]{:S(2)}) collective-permute-start(bf16[64,384]{1,0:T(8,128)(2,1)S(1)} %copy-done.12), channel_id=1, source_target_pairs={{0,4},{2,6},{4,0},{6,2},{1,5},{3,7},{5,1},{7,3},{8,12},{10,14},{12... | collective-permute-start | bytes 147464 | tf_op jit(solution)/shard_map/ppermute | solution.py:216
  23.2 1.9 %copy-start.2 = (bf16[4096,384]{1,0:T(8,128)(2,1)S(1)}, bf16[4096,384]{1,0:T(8,128)(2,1)}, u32[]{:S(2)}) copy-start(bf16[4096,384]{1,0:T(8,128)(2,1)} %coarse_ref.1) | copy-start | bytes 9437188
  27.4 7.3 %collective-permute-start.2 = (bf16[128,384]{1,0:T(8,128)(2,1)S(1)}, bf16[128,384]{1,0:T(8,128)(2,1)S(1)}, u32[]{:S(2)}, u32[]{:S(2)}) collective-permute-start(bf16[128,384]{1,0:T(8,128)(2,1)S(1)} %embed.1), channel_id=1, source_target_pairs={{0,6},{2,0},{4,2},{6,4},{1,7},{3,1},{5,3},{7,5},{8,14},{10,8},{12,... | collective-permute-start | bytes 294920 | tf_op jit(solution)/shard_map/ppermute | solution.py:216
  31.5 6.2 %collective-permute-start.1 = (bf16[128,384]{1,0:T(8,128)(2,1)S(1)}, bf16[128,384]{1,0:T(8,128)(2,1)S(1)}, u32[]{:S(2)}, u32[]{:S(2)}) collective-permute-start(bf16[128,384]{1,0:T(8,128)(2,1)S(1)} %embed.1), channel_id=1, source_target_pairs={{0,4},{2,6},{4,0},{6,2},{1,5},{3,7},{5,1},{7,3},{8,12},{10,14},{12... | collective-permute-start | bytes 294920 | tf_op jit(solution)/shard_map/ppermute | solution.py:216
  31.5 6.9 %collective-permute-start = (bf16[128,384]{1,0:T(8,128)(2,1)S(1)}, bf16[128,384]{1,0:T(8,128)(2,1)S(1)}, u32[]{:S(2)}, u32[]{:S(2)}) collective-permute-start(bf16[128,384]{1,0:T(8,128)(2,1)S(1)} %embed.1), channel_id=1, source_target_pairs={{0,2},{2,4},{4,6},{6,0},{1,3},{3,5},{5,7},{7,1},{8,10},{10,12},{12... | collective-permute-start | bytes 294920 | tf_op jit(solution)/shard_map/ppermute | solution.py:216
  32.8 6.0 %collective-permute-start.7 = (bf16[4,64,384]{2,1,0:T(8,128)(2,1)S(1)}, bf16[4,64,384]{2,1,0:T(8,128)(2,1)S(1)}, u32[]{:S(2)}, u32[]{:S(2)}) collective-permute-start(bf16[4,64,384]{2,1,0:T(8,128)(2,1)S(1)} %pad_maximum_fusion.1.same_ref), channel_id=1, source_target_pairs={{0,1},{1,0},{2,3},{3,2},{4,5},{5,4},{6,7},{7,6},{8,9},{9,8},{10,11... | collective-permute-start | bytes 589832 | tf_op jit(solution)/shard_map/ppermute | solution.py:219
  38.4 5.7 %copy-start.7 = (f32[64,2048]{1,0:T(8,128)S(1)}, f32[64,2048]{1,0:T(8,128)}, u32[]{:S(2)}) copy-start(f32[64,2048]{1,0:T(8,128)} %constant.9.clone.sin_ref) | copy-start | bytes 1572868
  38.4 5.7 %copy-start.8 = (f32[64,2048]{1,0:T(8,128)S(1)}, f32[64,2048]{1,0:T(8,128)}, u32[]{:S(2)}) copy-start(f32[64,2048]{1,0:T(8,128)} %constant.8.clone.cos_ref) | copy-start | bytes 1572868
  38.5 5.7 %copy-start.9 = (f32[8,128]{1,0:T(8,128)S(1)}, f32[8,128]{1,0:T(8,128)}, u32[]{:S(2)}) copy-start(f32[8,128]{1,0:T(8,128)} %constant.11.clone.freq_ref) | copy-start | bytes 12292
  38.5 9.4 %collective-permute-start.3 = (bf16[4,128,384]{2,1,0:T(8,128)(2,1)S(1)}, bf16[4,128,384]{2,1,0:T(8,128)(2,1)S(1)}, u32[]{:S(2)}, u32[]{:S(2)}) collective-permute-start(bf16[4,128,384]{2,1,0:T(8,128)(2,1)S(1)} %pad_maximum_fusion.same_ref), channel_id=1, source_target_pairs={{0,1},{1,0},{2,3},{3,2},{4,5},{5,4},{6,7},{7,6},{8,9},{9,8},{10,11... | collective-permute-start | bytes 1179656 | tf_op jit(solution)/shard_map/ppermute | solution.py:219
  47.0 0.8 copy-start.10
  57.1 32.0 %all-to-all-start.1 = ((bf16[16,400,128]{2,1,0:T(8,128)(2,1)}), bf16[16,400,128]{2,1,0:T(8,128)(2,1)S(1)}, u32[]{:S(2)}, u32[]{:S(2)}) async-start(bf16[16,400,128]{2,1,0:T(8,128)(2,1)} %history.1), calls=%async_computation.1 | async-start | bytes 3276800 | tf_op jit(solution)/shard_map/all_to_all | solution.py:584
  60.8 1.1 %copy-start.11 = (bf16[144,2048]{1,0:T(8,128)(2,1)S(1)}, bf16[144,2048]{1,0:T(8,128)(2,1)}, u32[]{:S(2)}) copy-start(bf16[144,2048]{1,0:T(8,128)(2,1)} %copy-done.10) | copy-start | bytes 1769476

commit v2 on v1

v2 whole, which is shorter than its diff:
```python
import functools

import jax
import jax.numpy as jnp
import numpy as np
from jax import lax
from jax.experimental import pallas as pl
from jax.experimental.pallas import tpu as pltpu
from jax.sharding import PartitionSpec as P

HEAD_DIM = 128
PARTS = (16, 56, 56)
THETA = 256.0
EPS = 1e-06
QUERY_SCALE = float(np.log2(np.e) * HEAD_DIM**-0.5)
EMBED = 50
BF = jnp.bfloat16
F32 = jnp.float32
VMEM = pl.BlockSpec(memory_space=pltpu.VMEM)
ANY = pl.BlockSpec(memory_space=pl.ANY)
SMEM = pl.BlockSpec(memory_space=pltpu.SMEM)


def params(mib=10):
    return pltpu.CompilerParams(vmem_limit_bytes=mib * 2**20)


def cost(flops, bytes_accessed, transcendentals=0):
    return pl.CostEstimate(
        flops=int(flops), bytes_accessed=int(bytes_accessed), transcendentals=int(transcendentals)
    )


def pair_tables():
    freqs = np.zeros((3, 64), np.float64)
    first, second = [], []
    pair, offset = 0, 0
    for axis, width in enumerate(PARTS):
        half = width // 2
        for i in range(half):
            freqs[axis, pair] = THETA ** (-2.0 * i / width)
            first.append(offset + i)
            second.append(offset + i + half)
            pair += 1
        offset += width
    return freqs, np.array(first + second)


def section_tables(frames, per_frame):
    freqs, _ = pair_tables()
    rows = np.arange(frames * per_frame)
    pos = np.stack(
        [4.0 * frames + rows // 512, 2.0 * (rows // 128 % 4) + 0.5, 2.0 * (rows % 128) + 0.5]
    )
    angles = freqs.T @ pos
    return np.cos(angles).astype(np.float32), np.sin(angles).astype(np.float32)


def head_permutation():
    _, order = pair_tables()
    perm = np.zeros((HEAD_DIM, HEAD_DIM), np.float32)
    perm[order, np.arange(HEAD_DIM)] = 1.0
    return perm


def lane_frequencies():
    freqs, _ = pair_tables()
    table = np.zeros((8, HEAD_DIM), np.float32)
    table[:3] = np.concatenate([freqs, freqs], axis=1)
    table[3] = np.concatenate([-np.ones(64), np.ones(64)])
    return table


def dot(a, b, dims=((1,), (0,))):
    return lax.dot_general(a, b, (dims, ((), ())), preferred_element_type=F32)


def select_columns(rows, columns, source):
    j = lax.broadcasted_iota(jnp.int32, (8, columns), 1)[0:1]
    i = lax.broadcasted_iota(jnp.int32, (rows, columns), 0)
    return jnp.where(i == source(j), 1.0, 0.0).astype(BF)


def select_rows(rows, columns, source):
    j = lax.broadcasted_iota(jnp.int32, (rows, columns), 1)
    i = lax.broadcasted_iota(jnp.int32, (rows, 128), 0)[:, 0:1]
    return jnp.where(j == source(i), 1.0, 0.0).astype(BF)


def split(value):
    high = value.astype(BF)
    return high, (value - high.astype(F32)).astype(BF)


def prepare_kernel(
    kinds_hbm,
    hist_hbm,
    sec_hbm,
    fine_hbm,
    out_ref,
    fine_ref,
    kinds_ref,
    hist_ref,
    sec_ref,
    kinds_sem,
    hist_sem,
    sec_sem,
    fine_sem,
):
    staged = [pltpu.make_async_copy(fine_hbm, fine_ref, fine_sem)]
    copies = [
        pltpu.make_async_copy(kinds_hbm, kinds_ref, kinds_sem),
        pltpu.make_async_copy(sec_hbm, sec_ref, sec_sem),
        pltpu.make_async_copy(hist_hbm, hist_ref, hist_sem),
    ]
    for copy in copies + staged:
        copy.start()
    for copy in copies:
        copy.wait()
    kind = kinds_ref[lax.axis_index("frame")]
    cells = hist_ref[...]

    own = select_rows(64, 64, lambda i: (i & 31) * 2 + (i >> 5))
    section = dot(own, sec_ref[...]).astype(BF)
    for d in range(16):
        out_ref[d, 64:128, :] = section

    @pl.when(kind == 0)
    def _():
        z, core = lax.axis_index("head"), lax.axis_index("fsdp")
        cols = select_columns(256, 128, lambda j: (64 * core + (j & 63)) * 2 + (j >> 6))
        rows = select_rows(
            128, 512, lambda i: (i >> 5) * 128 + ((i >> 1) & 15) * 8 + z * 2 + (i & 1)
        )
        out = dot(rows, dot(cells, cols).astype(BF)).astype(BF)
        blank = jnp.zeros((32, 128), BF)
        for d in range(16):
            t = d // 4
            out_ref[d, 0:64, :] = jnp.concatenate([out[32 * t : 32 * t + 32], blank], axis=0)

    @pl.when(kind == 1)
    def _():
        cols = select_columns(256, 256, lambda j: (j & 63) * 4 + (j >> 6))
        lanes = select_columns(
            512,
            512,
            lambda j: ((j >> 8) * 2 + ((j >> 2) & 1)) * 128
            + ((j >> 3) & 15) * 8
            + ((j >> 7) & 1) * 4
            + (j & 3),
        )
        out = dot(dot(cells, cols).astype(BF), lanes, ((0,), (0,))).astype(BF)
        for d in range(16):
            g, q = d // 4, d % 4
            for w in range(4):
                out_ref[d, 16 * w : 16 * w + 16, :] = out[
                    64 * w + 16 * q : 64 * w + 16 * q + 16, 128 * g : 128 * g + 128
                ]

    @pl.when(kind == 2)
    def _():
        lanes = select_columns(
            512, 512, lambda j: ((j >> 3) & 3) * 128 + (j >> 5) * 8 + (j & 7)
        )
        out = dot(cells, lanes, ((0,), (0,))).astype(BF)
        for d in range(16):
            for g in range(4):
                out_ref[d, 16 * g : 16 * g + 16, :] = out[
                    16 * d : 16 * d + 16, 128 * g : 128 * g + 128
                ]

    for copy in staged:
        copy.wait()


def prepare(kinds, history, section, patch_fine):
    return pl.pallas_call(
        prepare_kernel,
        out_shape=(
            jax.ShapeDtypeStruct((16, 128, 128), BF),
            jax.ShapeDtypeStruct(patch_fine.shape, BF),
        ),
        in_specs=[ANY] * 4,
        out_specs=(VMEM,) * 2,
        scratch_shapes=[
            pltpu.SMEM((16,), jnp.int32),
            pltpu.VMEM((512, 256), BF),
            pltpu.VMEM((64, 128), BF),
        ]
        + [pltpu.SemaphoreType.DMA] * 4,
        compiler_params=params(60),
        cost_estimate=cost(2e10, 1e6),
        name="prepare",
    )(kinds, history.reshape(512, 256), section.T, patch_fine)


def embed_kernel(
    kinds_ref,
    recv_ref,
    mid_hbm,
    coarse_hbm,
    other_ref,
    out_ref,
    mid_ref,
    coarse_ref,
    mid_buf,
    coarse_buf,
    mid_sem,
    coarse_sem,
):
    del other_ref
    mid_copy = pltpu.make_async_copy(mid_hbm, mid_ref, mid_sem)
    coarse_copy = pltpu.make_async_copy(coarse_hbm, coarse_ref, coarse_sem)
    mid_copy.start()
    coarse_copy.start()
    mid_count = jnp.int32(0)
    coarse_count = jnp.int32(0)
    for s in range(16):
        kind = kinds_ref[s]
        block = recv_ref[s, 0:64, :]
        mid_buf[jnp.where(kind == 1, jnp.minimum(mid_count, 6), 7)] = block
        coarse_buf[jnp.where(kind == 2, jnp.minimum(coarse_count, 7), 8)] = block
        mid_count += jnp.where(kind == 1, 1, 0)
        coarse_count += jnp.where(kind == 2, 1, 0)

        @pl.when(kind == 0)
        def _(block=block):
            blank = jnp.zeros((16, out_ref.shape[1] - 256), BF)
            out_ref[128:144, :] = jnp.concatenate([block[0:16], block[16:32], blank], axis=1)

    tokens = jnp.concatenate(
        [mid_buf[0:7, 16 * w : 16 * w + 16, :].reshape(112, 128) for w in range(4)], axis=1
    )
    order = select_columns(512, 512, lambda j: (j & 3) * 128 + (j >> 2))
    tokens = dot(tokens, order).astype(BF)
    mid_copy.wait()
    out_ref[0:112, :] = dot(tokens, mid_ref[...]).astype(BF)
    cells = coarse_buf[0:8].reshape(512, 128)
    order = select_rows(
        512,
        512,
        lambda i: ((i >> 1) & 7) * 64 + (i >> 7) * 16 + (i & 1) * 8 + ((i >> 4) & 7),
    )
    cells = dot(order, cells).astype(BF)
    tokens = jnp.concatenate(
        [
            jnp.concatenate(
                [cells[128 * g + 16 * w : 128 * g + 16 * w + 16] for w in range(8)], axis=1
            )
            for g in range(4)
        ],
        axis=0,
    )
    order = select_columns(1024, 1024, lambda j: (j & 7) * 128 + (j >> 3))
    tokens = dot(tokens, order).astype(BF)
    total = jnp.zeros((16, out_ref.shape[1]), F32)
    coarse_copy.wait()
    for g in range(4):
        total += dot(tokens[16 * g : 16 * g + 16], coarse_ref[1024 * g : 1024 * g + 1024, :])
    out_ref[112:128, :] = total.astype(BF)


def embed(kinds, received, patch_mid, patch_coarse, fine_other):
    return pl.pallas_call(
        embed_kernel,
        out_shape=jax.ShapeDtypeStruct((144, patch_mid.shape[1]), BF),
        in_specs=[SMEM, VMEM, ANY, ANY, ANY],
        out_specs=VMEM,
        scratch_shapes=[
            pltpu.VMEM(patch_mid.shape, BF),
            pltpu.VMEM(patch_coarse.shape, BF),
            pltpu.VMEM((8, 64, 128), BF),
            pltpu.VMEM((9, 64, 128), BF),
        ]
        + [pltpu.SemaphoreType.DMA] * 2,
        compiler_params=params(EMBED),
        cost_estimate=cost(2e9, 5e6),
        name="embed",
    )(kinds, received, patch_mid, patch_coarse, fine_other)


def stack_kernel(*refs):
    for d, ref in enumerate(refs[:-1]):
        refs[-1][d] = ref[...]


def stack(blocks, estimate):
    return pl.pallas_call(
        stack_kernel,
        out_shape=jax.ShapeDtypeStruct((len(blocks), *blocks[0].shape), BF),
        in_specs=[VMEM] * len(blocks),
        out_specs=VMEM,
        compiler_params=params(),
        cost_estimate=estimate,
        name="stack",
    )(*blocks)


def gather_columns(block, estimate):
    ring1, ring3, ring2 = (
        lax.ppermute(block, "head", [(i, (i + d) % 4) for i in range(4)]) for d in (1, 3, 2)
    )
    swap = [(0, 1), (1, 0)]
    twin = lax.ppermute(block, "fsdp", swap)
    same = stack((ring1, ring2, ring3), estimate)
    return block, twin, same, lax.ppermute(same, "fsdp", swap)


def pairs(own_ref, twin_ref, same_ref, other_ref):
    yield 0, own_ref, twin_ref
    for d in range(3):
        yield d + 1, same_ref.at[d], other_ref.at[d]


def place_columns(gathered, full_ref):
    z, core = lax.axis_index("head"), lax.axis_index("fsdp")
    rows = full_ref.shape[0]
    for d, mine, theirs in pairs(*gathered):
        at = ((z + 4 - d) & 3) * 2
        width = mine.shape[1]
        for ref, column in ((mine, at + core), (theirs, at + 1 - core)):
            full_ref[:, pl.ds(pl.multiple_of(column * width, 128), width)] = ref[0:rows]


def fold_kernel(
    own_ref,
    twin_ref,
    same_ref,
    other_ref,
    mod_ref,
    w_ref,
    perm_ref,
    far_ref,
    fold_ref,
    gram_ref,
    full_ref,
):
    del far_ref
    place_columns((own_ref, twin_ref, same_ref, other_ref), full_ref)
    order = select_rows(64, 64, lambda i: (i & 31) * 2 + (i >> 5))
    raw = full_ref[...]
    width = raw.shape[1]
    weight = dot(order, raw)
    low = weight.astype(BF)
    mean = jnp.sum(weight, axis=1, keepdims=True) / width
    mean_row = dot(jnp.ones((8, width), BF), low, ((1,), (1,)))[0:1] / width
    gram_ref[...] = dot(low, low, ((1,), (1,))) / width - mean * mean_row
    scaled = (weight - mean) * (1.0 + mod_ref[1:2, :])
    shift_high, shift_low = split(mod_ref[0:1, :])
    pad = jnp.zeros((14, width), BF)
    high, rest = split(scaled)
    left = jnp.concatenate(
        [high, rest, jnp.concatenate([shift_high, shift_low, pad], axis=0)], axis=0
    )
    for part in range(3):
        product = dot(left, w_ref[part])
        matrix = product[0:64] + product[64:128]
        bias = product[128:129] + product[129:130]
        columns = matrix.shape[1]
        high, rest = split(matrix)
        bias_high, bias_low = split(bias)
        rows = jnp.concatenate(
            [
                high.astype(F32),
                rest.astype(F32),
                bias_high.astype(F32),
                bias_high.astype(F32),
                bias_low.astype(F32),
                jnp.zeros((13, columns), F32),
            ],
            axis=0,
        ).astype(BF)
        if part < 2:
            rows = jnp.concatenate(
                [
                    dot(rows[:, HEAD_DIM * h : HEAD_DIM * (h + 1)], perm_ref[...]).astype(BF)
                    for h in range(columns // HEAD_DIM)
                ],
                axis=1,
            )
        fold_ref[part] = rows


def fold(gathered, modulation, w_qkv, perm, far):
    width, columns = w_qkv.shape[1], w_qkv.shape[2]
    return pl.pallas_call(
        fold_kernel,
        out_shape=(
            jax.ShapeDtypeStruct((3, 144, columns), BF),
            jax.ShapeDtypeStruct((64, 64), F32),
        ),
        in_specs=[VMEM] * 7 + [ANY],
        out_specs=(VMEM, VMEM),
        scratch_shapes=[pltpu.VMEM((64, width), BF)],
        compiler_params=params(),
        cost_estimate=cost(1e6, 1e4),
        name="fold",
    )(*gathered, modulation, w_qkv, perm, far)


def along_x(value, d):
    return lax.ppermute(value, "frame", [(i, i // 4 * 4 + (i + d) % 4) for i in range(16)])


def along_y(value, d):
    return lax.ppermute(value, "frame", [(i, (i + 4 * d) % 16) for i in range(16)])


def spread_of(patches, gram):
    one, rest = split(gram)
    two, three = split(gram - one.astype(F32))
    parts = jnp.concatenate([one, two, three], axis=1)
    spread = dot(parts, jnp.concatenate([patches, patches, patches], axis=0))
    variance = jnp.sum(spread * patches.astype(F32), axis=0, keepdims=True)
    return jnp.maximum(variance, 0.0) + EPS


def extended(patches, variance):
    high, low = split(jnp.sqrt(variance))
    rows = lax.broadcasted_iota(jnp.int32, (16, patches.shape[1]), 0)
    extra = jnp.where(
        rows == 1,
        low.astype(F32),
        jnp.where((rows == 0) | (rows == 2), high.astype(F32), 0.0),
    ).astype(BF)
    return jnp.concatenate([patches, patches, extra], axis=0)


def turned_columns(raw, variance, cosine, sine, scale):
    square = jnp.sum(raw * raw, axis=0, keepdims=True) / HEAD_DIM
    factor = lax.rsqrt(square + EPS * variance) * scale
    a, b = raw[0:64] * factor, raw[64:128] * factor
    return jnp.concatenate([a * cosine - b * sine, b * cosine + a * sine], axis=0).astype(BF)


def token_kernel(
    kinds_ref,
    recv_ref,
    own_ref,
    twin_ref,
    same_ref,
    other_ref,
    fold_ref,
    gram_ref,
    cos_ref,
    sin_ref,
    time_ref,
    query_ref,
    key_ref,
    value_ref,
    fine_buf,
):
    me = lax.axis_index("frame")
    x, y = me & 3, me >> 2
    heads = query_ref.shape[0] // HEAD_DIM
    columns = [((y + d) & 3) * 4 + x for d in range(4)]

    def block(ref, f):
        return ref[:, pl.ds(pl.multiple_of(f * 128, 128), 128)]

    z, core = lax.axis_index("head"), lax.axis_index("fsdp")
    for d, mine, theirs in pairs(own_ref, twin_ref, same_ref, other_ref):
        mine, theirs = (
            jnp.concatenate([ref[128:144, 0:128], ref[128:144, 128:256]], axis=0).astype(F32)
            for ref in (mine, theirs)
        )
        first, second = jnp.where(core == 0, mine, theirs), jnp.where(core == 0, theirs, mine)
        fine_buf[:, pl.ds(pl.multiple_of(((z + 4 - d) & 3) * 128, 128), 128)] = jnp.concatenate(
            [
                jnp.concatenate([first[:, 0:64], second[:, 0:64]], axis=1),
                jnp.concatenate([first[:, 64:128], second[:, 64:128]], axis=1),
            ],
            axis=0,
        ).astype(BF)
    patches = jnp.concatenate(
        [recv_ref[f, 64:128, :] for f in columns]
        + [recv_ref[4 * y + i, 64:128, :] for i in range(4)]
        + [fine_buf[...]],
        axis=1,
    )
    variance = spread_of(patches, gram_ref[...])
    inverse = lax.rsqrt(variance)
    patches = extended(patches, variance)
    cosine = jnp.concatenate([block(cos_ref, f) for f in columns], axis=1)
    sine = jnp.concatenate([block(sin_ref, f) for f in columns], axis=1)
    row = pl.ds(pl.multiple_of(y * 512, 128), 512)
    key_cos, key_sin = cos_ref[:, row], sin_ref[:, row]
    slab = jnp.int32(0)
    for s in range(16):
        slab += jnp.where(kinds_ref[s] == 0, s, 0)
    angles = time_ref[...] * (4 * slab + y).astype(F32)
    fine_cos = jnp.concatenate([jnp.concatenate([jnp.cos(angles)] * 4, axis=1), key_cos[8:]], axis=0)
    fine_sin = jnp.concatenate([jnp.concatenate([jnp.sin(angles)] * 4, axis=1), key_sin[8:]], axis=0)
    key_cos = jnp.concatenate([key_cos, fine_cos], axis=1)
    key_sin = jnp.concatenate([key_sin, fine_sin], axis=1)
    for h in range(heads):
        at = slice(HEAD_DIM * h, HEAD_DIM * (h + 1))
        raw = dot(fold_ref[0][:, at], patches[:, 0:512], ((0,), (0,)))
        query_ref[at, :] = turned_columns(raw, variance[:, 0:512], cosine, sine, QUERY_SCALE)
        raw = dot(fold_ref[1][:, at], patches[:, 512:], ((0,), (0,)))
        key_ref[at, :] = turned_columns(raw, variance[:, 512:], key_cos, key_sin, 1.0)
        raw = dot(fold_ref[2][:, at], patches[:, 512:], ((0,), (0,)))
        value_ref[at, :] = (raw * inverse[:, 512:]).astype(BF)


def make_tokens(kinds, received, gathered, folded, gram, cosine, sine, times):
    columns = folded.shape[2]
    return pl.pallas_call(
        token_kernel,
        out_shape=(
            jax.ShapeDtypeStruct((columns, 512), BF),
            jax.ShapeDtypeStruct((columns, 1024), BF),
            jax.ShapeDtypeStruct((columns, 1024), BF),
        ),
        in_specs=[SMEM] + [VMEM] * 10,
        out_specs=tuple([VMEM] * 3),
        scratch_shapes=[pltpu.VMEM((64, 512), BF)],
        compiler_params=params(),
        cost_estimate=cost(2e9, 8e6),
        name="tokens",
    )(kinds, received, *gathered, folded, gram, cosine, sine, times)


def near_kernel(query_ref, key_ref, value_ref, num_ref, den_ref):
    heads = query_ref.shape[0] // HEAD_DIM
    for h in range(heads):
        at = slice(HEAD_DIM * h, HEAD_DIM * (h + 1))
        weights = jnp.exp2(dot(key_ref[at, :], query_ref[at, :], ((0,), (0,))))
        den_ref[h : h + 1, :] = jnp.sum(weights, axis=0, keepdims=True)
        num_ref[at, :] = dot(value_ref[at, :], weights.astype(BF))


def attend_near(queries, keys, values):
    columns, count = queries.shape
    return pl.pallas_call(
        near_kernel,
        out_shape=(
            jax.ShapeDtypeStruct((columns, count), F32),
            jax.ShapeDtypeStruct((8, count), F32),
        ),
        in_specs=[VMEM] * 3,
        out_specs=(VMEM, VMEM),
        compiler_params=params(),
        cost_estimate=cost(4e9, 1e7, 2e6),
        name="near",
    )(queries, keys, values)


def row_angles(kinds_ref, freq_ref):
    me = lax.axis_index("frame")
    row = lax.broadcasted_iota(jnp.int32, (128, 128), 0)
    slot = row >> 4
    slab = jnp.zeros((128, 128), F32)
    mid_count = jnp.int32(0)
    coarse_count = jnp.int32(0)
    coarse_slot = jnp.where(slot == 7, (row >> 1) & 7, -1)
    for s in range(16):
        kind = kinds_ref[s]
        is_mid, is_coarse = kind == 1, kind == 2
        slab = jnp.where(slot == jnp.where(is_mid, mid_count, 99), float(s), slab)
        slab = jnp.where(coarse_slot == jnp.where(is_coarse, coarse_count, 99), float(s), slab)
        mid_count += jnp.where(is_mid, 1, 0)
        coarse_count += jnp.where(is_coarse, 1, 0)
    coarse = slot == 7
    whole = me.astype(F32)
    quarter = (me & 3).astype(F32)
    frame_half = (me >> 3).astype(F32)
    row_half = ((me >> 2) & 1).astype(F32)
    t = 4.0 * slab + jnp.where(coarse, 1.5, 2.0 * frame_half + 0.5)
    h = jnp.where(coarse, 3.5, 4.0 * row_half + 1.5)
    w = jnp.where(
        coarse,
        8.0 * (2.0 * whole + (row & 1).astype(F32)) + 3.5,
        4.0 * (16.0 * quarter + (row & 15).astype(F32)) + 1.5,
    )
    freq_t, freq_h, freq_w, sign = (freq_ref[i : i + 1, :] for i in range(4))
    angles = t * freq_t + h * freq_h + w * freq_w
    return jnp.cos(angles), jnp.sin(angles) * sign


def far_kernel(
    kinds_ref,
    own_ref,
    twin_ref,
    same_ref,
    other_ref,
    mod_ref,
    w_ref,
    perm_ref,
    freq_ref,
    out_ref,
    full_ref,
):
    place_columns((own_ref, twin_ref, same_ref, other_ref), full_ref)
    heads = out_ref.shape[2] // HEAD_DIM
    x = full_ref[...].astype(F32)
    x = x - jnp.mean(x, axis=1, keepdims=True)
    x = x * lax.rsqrt(jnp.mean(x * x, axis=1, keepdims=True) + EPS)
    x = (x * (1.0 + mod_ref[1:2, :]) + mod_ref[0:1, :]).astype(BF)
    raw_keys = dot(x, w_ref[1])
    out_ref[1] = dot(x, w_ref[2]).astype(BF)
    cosine, sine = row_angles(kinds_ref, freq_ref)
    for h in range(heads):
        at = slice(HEAD_DIM * h, HEAD_DIM * (h + 1))
        raw = raw_keys[:, at]
        raw = raw * lax.rsqrt(jnp.mean(raw * raw, axis=1, keepdims=True) + EPS)
        high, rest = split(raw)
        raw = dot(high, perm_ref[...]) + dot(rest, perm_ref[...])
        out_ref[0, :, at] = (raw * cosine + pltpu.roll(raw, 64, 1) * sine).astype(BF)


def make_far(kinds, gathered, modulation, w_qkv, perm, freqs):
    columns = w_qkv.shape[2]
    return pl.pallas_call(
        far_kernel,
        out_shape=jax.ShapeDtypeStruct((2, 128, columns), BF),
        in_specs=[SMEM] + [VMEM] * 8,
        out_specs=VMEM,
        scratch_shapes=[pltpu.VMEM((128, w_qkv.shape[1]), BF)],
        compiler_params=params(),
        cost_estimate=cost(2e9, 1e7),
        name="far",
    )(kinds, *gathered, modulation, w_qkv, perm, freqs)


def history_kernel(far0, far1, far3, key2, value2, query_ref, num_ref, den_ref, out0, out1, out2, out3):
    heads = query_ref.shape[0] // HEAD_DIM
    count = query_ref.shape[1]
    outs = (out0, out1, out2, out3)
    rows = lax.broadcasted_iota(jnp.int32, (16, count), 0)
    tail = jnp.zeros((16, count), F32)
    for h in range(heads):
        at = slice(HEAD_DIM * h, HEAD_DIM * (h + 1))
        fars = (far0, far1, far3)
        keys = jnp.concatenate([far[0, :, at] for far in fars] + [key2[:, at]], axis=0)
        values = jnp.concatenate([far[1, :, at] for far in fars] + [value2[:, at]], axis=0)
        weights = jnp.exp2(dot(keys, query_ref[at, :]))
        high, rest = split(den_ref[h : h + 1, :] + jnp.sum(weights, axis=0, keepdims=True))
        tail = jnp.where(rows == h, high.astype(F32), tail)
        tail = jnp.where(rows == heads + h, rest.astype(F32), tail)
        part = num_ref[at, :] + dot(values, weights.astype(BF), ((0,), (0,)))
        for d, out in enumerate(outs):
            out[at, :] = part[:, 128 * d : 128 * d + 128].astype(out.dtype)
    for d, out in enumerate(outs):
        out[HEAD_DIM * heads :, :] = tail[:, 128 * d : 128 * d + 128].astype(out.dtype)


def attend_history(fars, queries, numerator, denominator):
    columns = queries.shape[0]
    return pl.pallas_call(
        history_kernel,
        out_shape=tuple(jax.ShapeDtypeStruct((columns + 16, 128), t) for t in (F32, BF, BF, BF)),
        in_specs=[VMEM] * 8,
        out_specs=tuple([VMEM] * 4),
        compiler_params=params(),
        cost_estimate=cost(2e9, 4e6, 1e6),
        name="history",
    )(*fars, queries, numerator, denominator)


def combine_kernel(part0, part1, part2, part3, out_ref):
    columns = out_ref.shape[1]
    heads = columns // HEAD_DIM
    total = sum(part[...].astype(F32) for part in (part0, part1, part2, part3))
    for h in range(heads):
        at = slice(HEAD_DIM * h, HEAD_DIM * (h + 1))
        low = columns + heads + h
        denominator = total[columns + h : columns + h + 1] + total[low : low + 1]
        out_ref[:, at] = jnp.transpose(total[at] / denominator).astype(BF)


def combine(parts):
    return pl.pallas_call(
        combine_kernel,
        out_shape=jax.ShapeDtypeStruct((128, parts[0].shape[0] - 16), BF),
        in_specs=[VMEM] * 4,
        out_specs=VMEM,
        compiler_params=params(),
        cost_estimate=cost(1e7, 2e6),
        name="combine",
    )(*parts)


def per_device(
    history, section, slab_kernel, patch_fine, patch_mid, patch_coarse, modulation, w_qkv
):
    frames = lax.axis_size("frame")
    cos_table, sin_table = section_tables(frames, section.shape[0])
    cosine, sine = jnp.asarray(cos_table), jnp.asarray(sin_table)
    perm = jnp.asarray(head_permutation(), BF)
    lane_table = lane_frequencies()
    freqs = jnp.asarray(lane_table)
    times = jnp.asarray(np.repeat(lane_table[0, 0:8, None], 128, axis=1))

    sent, patch_fine = prepare(slab_kernel, history, section, patch_fine)
    received = lax.all_to_all(sent, "frame", 0, 0, tiled=True)
    fine = gather_columns(patch_fine, cost(1e6, 4e5))
    features = embed(slab_kernel, received, patch_mid, patch_coarse, fine[3])
    gathered = gather_columns(features, cost(2e10, 1e6))
    far = make_far(slab_kernel, gathered, modulation, w_qkv, perm, freqs)
    far1, far3 = along_x(far, 1), along_x(far, 3)
    far2 = along_x(far1[0], 1), along_x(far3[1], 3)
    folded, gram = fold(fine, modulation, w_qkv, perm, far)
    queries, keys, values = make_tokens(
        slab_kernel, received, gathered, folded, gram, cosine, sine, times
    )
    numerator, denominator = attend_near(queries, keys, values)
    fars = [far, far1, far3, *far2]
    parts = attend_history(fars, queries, numerator, denominator)
    part2 = along_y(parts[2], 2)
    return combine([parts[0], along_y(parts[1], 1), part2, along_y(parts[3], 3)])


def solution(mesh):
    in_specs = (
        P("frame", None, None, None),
        P("frame", None),
        P(),
        P(None, ("head", "fsdp")),
        P(None, ("head", "fsdp")),
        P(None, ("head", "fsdp")),
        P(),
        P(None, None, ("head", "fsdp")),
    )
    out_specs = P("frame", ("head", "fsdp"))
    return jax.shard_map(
        per_device, mesh=mesh, in_specs=in_specs, out_specs=out_specs, check_vma=False
    )
```

time: 91.1 us -> 67.1 us (0.74)
  waiting for transfers between devices: 35.7 us -> 21.3 us
  Pallas kernels: 25.2 us -> 16.3 us
  starting transfers between devices: 22.7 us -> 29 us
  local copies, waits for them, and re-layouts: 6.23 us -> 0.09 us
    all_to_all x1 -> x0, waiting for transfers between devices: 24.6 us -> none  [per_device(): parts = lax.all_to_all(parts, 'frame', 0, 0, tiled=True)]
    ppermute x2 -> x11, starting transfers between devices: 0.35 us -> 11.4 us  [the longest x3 5.66 us: along_y(): lax.ppermute(value, 'frame', [(i, (i + 4 * d) % 16) for i in range(16)])]
    ppermute x2 -> x11, waiting for transfers between devices: 0.01 us -> 10.6 us  [the longest x4 4.83 us: along_x(): lax.ppermute(value, 'frame', [(i, i // 4 * 4 + (i + d) % 4) for i in rang...]
    unnamed x27 -> x22, local copies, waits for them, and re-layouts: 6.23 us -> 0.07 us
    pallas_call x6 -> x9, Pallas kernels: 19.8 us -> 13.9 us  [the longest x1 3.42 us: embed(): pl.pallas_call(embed_kernel, out_shape=jax.ShapeDtypeStruct((144, patch_m...]
    all_to_all x1, waiting for transfers between devices: 5.53 us -> 0.01 us  [per_device(): received = lax.all_to_all(sent, 'frame', 0, 0, tiled=True)]
    ppermute x6, waiting for transfers between devices: 5.5 us -> 10.7 us  [gather_columns(): lax.ppermute(block, 'head', [(i, (i + d) % 4) for i in range(4)])]
    all_to_all x1 -> x0, starting transfers between devices: 3.71 us -> none  [per_device(): parts = lax.all_to_all(parts, 'frame', 0, 0, tiled=True)]
  transfers between devices with their start and end apart: 10 -> 18, of which waited for: 5 -> 14; matrix products, arithmetic and copies ran while one was open for 0% -> 0% of each run, Pallas kernels for 15% -> 12%
where the time goes in v2:
time: 67.1 us; the launch traced here: 66.8 us
  starting transfers between devices  29 us (43%)
  waiting for transfers between devices  21.3 us (32%)
  Pallas kernels  16.3 us (24%)
    ppermute x6, waiting for transfers between devices, gather_columns(): lax.ppermute(block, 'head', [(i, (i + d) % 4) for i in range(4)])  10.7 us
    ppermute x6, starting transfers between devices, gather_columns(): lax.ppermute(block, 'head', [(i, (i + d) % 4) for i in range(4)])  10.6 us
    all_to_all x1, starting transfers between devices, per_device(): received = lax.all_to_all(sent, 'frame', 0, 0, tiled=True)  6.95 us
    ppermute x3, starting transfers between devices, along_y(): lax.ppermute(value, 'frame', [(i, (i + 4 * d) % 16) for i in range(16)])  5.66 us
    ppermute x4, starting transfers between devices, along_x(): lax.ppermute(value, 'frame', [(i, i // 4 * 4 + (i + d) % 4) for i in rang...  4.99 us
    ppermute x4, waiting for transfers between devices, along_x(): lax.ppermute(value, 'frame', [(i, i // 4 * 4 + (i + d) % 4) for i in rang...  4.83 us
    pallas_call x1, Pallas kernels, embed(): pl.pallas_call(embed_kernel, out_shape=jax.ShapeDtypeStruct((144, patch_m...  3.42 us
    ppermute x3, waiting for transfers between devices, along_y(): lax.ppermute(value, 'frame', [(i, (i + 4 * d) % 16) for i in range(16)])  3.21 us
  transfers between devices with their start and end apart: 18, of which 14 were waited for; matrix products, arithmetic and copies ran while one was open for 0% of the time, Pallas kernels for 12%

profile of v2, /device:TPU:0, one launch (start us, length us, event | category | flops | bytes accessed | tf_op | source)
XLA Modules:
  0.0 66.8 jit_solution(8914640072115262522)
XLA Ops:
  0.0 2.6 %prepare.1 = (bf16[16,128,128]{2,1,0:T(8,128)(2,1)}, bf16[64,384]{1,0:T(8,128)(2,1)}) custom-call(s32[16]{0:T(128)} %kinds_ref.5, bf16[512,256]{1,0:T(8,128)(2,1)} %bitcast.8, bf16[64,128]{1,0:T(8,128)(2,1)} %bitcast.9, bf16[64,384]{1,0:T(8,128)(2,1)} %fine_hbm.1), custom_call_target="tpu_custom_call" | custom-call | flops 20000000000 | bytes 1000000 | tf_op jit(solution)/shard_map/prepare/pallas_call | solution.py:177
  2.6 6.9 %all-to-all-start = ((bf16[16,128,128]{2,1,0:T(8,128)(2,1)}), bf16[16,128,128]{2,1,0:T(8,128)(2,1)S(1)}, u32[]{:S(2)}, u32[]{:S(2)}) async-start(bf16[16,128,128]{2,1,0:T(8,128)(2,1)} %get-tuple-element.18), calls=%async_computation | async-start | bytes 1048576 | tf_op jit(solution)/shard_map/all_to_all | solution.py:696
  9.5 4.1 %collective-permute-start.2 = (bf16[64,384]{1,0:T(8,128)(2,1)}, bf16[64,384]{1,0:T(8,128)(2,1)S(1)}, u32[]{:S(2)}, u32[]{:S(2)}) collective-permute-start(bf16[64,384]{1,0:T(8,128)(2,1)} %get-tuple-element.19.own_ref), channel_id=1, source_target_pairs={{0,6},{2,0},{4,2},{6,4},{1,7},{3,1},{5,3},{7,5},{8,14},{10,8},{12,... | collective-permute-start | bytes 147464 | tf_op jit(solution)/shard_map/ppermute | solution.py:301
  13.6 1.3 %collective-permute-start = (bf16[64,384]{1,0:T(8,128)(2,1)}, bf16[64,384]{1,0:T(8,128)(2,1)S(1)}, u32[]{:S(2)}, u32[]{:S(2)}) collective-permute-start(bf16[64,384]{1,0:T(8,128)(2,1)} %get-tuple-element.19.own_ref), channel_id=1, source_target_pairs={{0,2},{2,4},{4,6},{6,0},{1,3},{3,5},{5,7},{7,1},{8,10},{10,12},{12... | collective-permute-start | bytes 147464 | tf_op jit(solution)/shard_map/ppermute | solution.py:301
  15.7 3.8 %collective-permute-done.1.refs_1_ = bf16[64,384]{1,0:T(8,128)(2,1)S(1)} collective-permute-done((bf16[64,384]{1,0:T(8,128)(2,1)}, bf16[64,384]{1,0:T(8,128)(2,1)S(1)}, u32[]{:S(2)}, u32[]{:S(2)}) %collective-permute-start.1) | collective-permute-done | bytes 49184 | tf_op jit(solution)/shard_map/ppermute | solution.py:301
  19.8 1.4 %collective-permute-done.3.other_ref = bf16[3,64,384]{2,1,0:T(8,128)(2,1)S(1)} collective-permute-done((bf16[3,64,384]{2,1,0:T(8,128)(2,1)S(1)}, bf16[3,64,384]{2,1,0:T(8,128)(2,1)S(1)}, u32[]{:S(2)}, u32[]{:S(2)}) %collective-permute-start.3) | collective-permute-done | bytes 147488 | tf_op jit(solution)/shard_map/ppermute | solution.py:306
  21.2 3.4 %embed.1.own_ref = bf16[144,384]{1,0:T(8,128)(2,1)S(1)} custom-call(s32[16]{0:T(128)S(1)} %copy-done.4, bf16[16,128,128]{2,1,0:T(8,128)(2,1)S(1)} %all-to-all-done.recv_ref, bf16[512,384]{1,0:T(8,128)(2,1)S(1)} %copy-done.5, bf16[4096,384]{1,0:T(8,128)(2,1)} %coarse_hbm.1, bf16[3,64,384]{2,1,0:T(8,128)(2,1)S(1)} %collective-permute-done.3.other_ref), custom_call_target="tpu_custom_call" | custom-call | flops 2000000000 | bytes 5000000 | tf_op jit(solution)/shard_map/embed/pallas_call | solution.py:264
  24.7 4.0 %collective-permute-start.7 = (bf16[144,384]{1,0:T(8,128)(2,1)S(1)}, bf16[144,384]{1,0:T(8,128)(2,1)S(1)}, u32[]{:S(2)}, u32[]{:S(2)}) collective-permute-start(bf16[144,384]{1,0:T(8,128)(2,1)S(1)} %embed.1.own_ref), channel_id=1, source_target_pairs={{0,6},{2,0},{4,2},{6,4},{1,7},{3,1},{5,3},{7,5},{8,14},{10,8},{12,... | collective-permute-start | bytes 331784 | tf_op jit(solution)/shard_map/ppermute | solution.py:301
  28.7 1.3 %collective-permute-start.5 = (bf16[144,384]{1,0:T(8,128)(2,1)S(1)}, bf16[144,384]{1,0:T(8,128)(2,1)S(1)}, u32[]{:S(2)}, u32[]{:S(2)}) collective-permute-start(bf16[144,384]{1,0:T(8,128)(2,1)S(1)} %embed.1.own_ref), channel_id=1, source_target_pairs={{0,2},{2,4},{4,6},{6,0},{1,3},{3,5},{5,7},{7,1},{8,10},{10,12},{12... | collective-permute-start | bytes 331784 | tf_op jit(solution)/shard_map/ppermute | solution.py:301
  29.9 2.5 %collective-permute-done.7.refs_2_ = bf16[144,384]{1,0:T(8,128)(2,1)S(1)} collective-permute-done((bf16[144,384]{1,0:T(8,128)(2,1)S(1)}, bf16[144,384]{1,0:T(8,128)(2,1)S(1)}, u32[]{:S(2)}, u32[]{:S(2)}) %collective-permute-start.7) | collective-permute-done | bytes 110624 | tf_op jit(solution)/shard_map/ppermute | solution.py:301
  32.4 2.6 %collective-permute-done.6.refs_1_ = bf16[144,384]{1,0:T(8,128)(2,1)S(1)} collective-permute-done((bf16[144,384]{1,0:T(8,128)(2,1)S(1)}, bf16[144,384]{1,0:T(8,128)(2,1)S(1)}, u32[]{:S(2)}, u32[]{:S(2)}) %collective-permute-start.6) | collective-permute-done | bytes 110624 | tf_op jit(solution)/shard_map/ppermute | solution.py:301
  36.6 1.2 %collective-permute-done.4.twin_ref = bf16[144,384]{1,0:T(8,128)(2,1)S(1)} collective-permute-done((bf16[144,384]{1,0:T(8,128)(2,1)S(1)}, bf16[144,384]{1,0:T(8,128)(2,1)S(1)}, u32[]{:S(2)}, u32[]{:S(2)}) %collective-permute-start.4) | collective-permute-done | bytes 110624 | tf_op jit(solution)/shard_map/ppermute | solution.py:304
  37.8 2.5 %far.1.far_ref.far0 = bf16[2,128,384]{2,1,0:T(8,128)(2,1)S(1)} custom-call(s32[16]{0:T(128)S(1)} %copy-done.4, bf16[144,384]{1,0:T(8,128)(2,1)S(1)} %embed.1.own_ref, bf16[144,384]{1,0:T(8,128)(2,1)S(1)} %collective-permute-done.4.twin_ref, bf16[3,144,384]{2,1,0:T(8,128)(2,1)S(1)} %stack.3.same_ref, ...), custom_call_target="tpu_custom_call" | custom-call | flops 2000000000 | bytes 10000000 | tf_op jit(solution)/shard_map/far/pallas_call | solution.py:614
  40.3 1.6 %collective-permute-start.10 = (bf16[2,128,384]{2,1,0:T(8,128)(2,1)S(1)}, bf16[2,128,384]{2,1,0:T(8,128)(2,1)S(1)}, u32[]{:S(2)}, u32[]{:S(2)}) collective-permute-start(bf16[2,128,384]{2,1,0:T(8,128)(2,1)S(1)} %far.1.far_ref.far0), channel_id=1, source_target_pairs={{0,24},{8,0},{16,8},{24,16},{32,56},{40,32},{48,40},{56,48},{64,88... | collective-permute-start | bytes 589832 | tf_op jit(solution)/shard_map/ppermute | solution.py:402
  42.4 2.4 %fold.1 = (bf16[3,144,384]{2,1,0:T(8,128)(2,1)S(1)}, f32[64,64]{1,0:T(8,128)S(1)}) custom-call(bf16[64,384]{1,0:T(8,128)(2,1)S(1)} %copy-done.2, bf16[64,384]{1,0:T(8,128)(2,1)S(1)} %collective-permute-done.13.twin_ref, bf16[3,64,384]{2,1,0:T(8,128)(2,1)S(1)} %stack.2.same_ref, bf16[3,64,384]{2,1,0:T(8,128)(2,1)S(1)} %collective-permute-done.3.other_ref, ...), custom_call_target="tpu_custom_call" | custom-call | flops 1000000 | bytes 10000 | tf_op jit(solution)/shard_map/fold/pallas_call | solution.py:386
  44.8 1.9 %tokens.1 = (bf16[384,512]{1,0:T(8,128)(2,1)S(1)}, bf16[384,1024]{1,0:T(8,128)(2,1)S(1)}, bf16[384,1024]{1,0:T(8,128)(2,1)S(1)}) custom-call(s32[16]{0:T(128)S(1)} %copy-done.4, bf16[16,128,128]{2,1,0:T(8,128)(2,1)S(1)} %all-to-all-done.recv_ref, bf16[144,384]{1,0:T(8,128)(2,1)S(1)} %embed.1.own_ref, bf16[144,384]{1,0:T(8,128)(2,1)S(1)} %collective-permute-done.4.twin_ref, ...), custom_call_target="tpu_custom_call" | custom-call | flops 2000000000 | bytes 8000000 | tf_op jit(solution)/shard_map/tokens/pallas_call | solution.py:508
  47.3 2.8 %collective-permute-start.12 = (bf16[128,384]{1,0:T(8,128)(2,1)S(1)}, bf16[128,384]{1,0:T(8,128)(2,1)S(1)}, u32[]{:S(2)}, u32[]{:S(2)}) collective-permute-start(bf16[128,384]{1,0:T(8,128)(2,1)S(1)} %slice_bitcast_fusion), channel_id=1, source_target_pairs={{0,24},{8,0},{16,8},{24,16},{32,56},{40,32},{48,40},{56,48},{64,88... | collective-permute-start | bytes 294920 | tf_op jit(solution)/shard_map/ppermute | solution.py:402
  50.2 1.6 %near.1 = (f32[384,512]{1,0:T(8,128)S(1)}, f32[8,512]{1,0:T(8,128)S(1)}) custom-call(bf16[384,512]{1,0:T(8,128)(2,1)S(1)} %get-tuple-element.22.query_ref, bf16[384,1024]{1,0:T(8,128)(2,1)S(1)} %get-tuple-element.23.key_ref, bf16[384,1024]{1,0:T(8,128)(2,1)S(1)} %get-tuple-element.24.value_ref), custom_call_target="tpu_custom_call" | custom-call | flops 4000000000 | bytes 10000000 | tf_op jit(solution)/shard_map/near/pallas_call | solution.py:535
  52.4 3.7 %collective-permute-done.11.key2 = bf16[128,384]{1,0:T(8,128)(2,1)S(1)} collective-permute-done((bf16[128,384]{1,0:T(8,128)(2,1)S(1)}, bf16[128,384]{1,0:T(8,128)(2,1)S(1)}, u32[]{:S(2)}, u32[]{:S(2)}) %collective-permute-start.11) | collective-permute-done | bytes 98336 | tf_op jit(solution)/shard_map/ppermute | solution.py:402
  56.1 1.1 %history.1 = (f32[400,128]{1,0:T(8,128)S(1)}, bf16[400,128]{1,0:T(8,128)(2,1)S(1)}, bf16[400,128]{1,0:T(8,128)(2,1)S(1)}, bf16[400,128]{1,0:T(8,128)(2,1)S(1)}) custom-call(bf16[2,128,384]{2,1,0:T(8,128)(2,1)S(1)} %far.1.far_ref.far0, bf16[2,128,384]{2,1,0:T(8,128)(2,1)S(1)} %collective-permute-done.9.far1, ...), custom_call_target="tpu_custom_call" | custom-call | flops 2000000000 | bytes 4000000 | tf_op jit(solution)/shard_map/history/pallas_call | solution.py:650
  57.2 1.5 %collective-permute-start.14 = (bf16[400,128]{1,0:T(8,128)(2,1)S(1)}, bf16[400,128]{1,0:T(8,128)(2,1)S(1)}, u32[]{:S(2)}, u32[]{:S(2)}) collective-permute-start(bf16[400,128]{1,0:T(8,128)(2,1)S(1)} %get-tuple-element.28), channel_id=1, source_target_pairs={{0,32},{8,40},{16,48},{24,56},{32,64},{40,72},{48,80},{56,88},{64,... | collective-permute-start | bytes 307208 | tf_op jit(solution)/shard_map/ppermute | solution.py:406
  58.7 2.7 %collective-permute-start.15 = (bf16[400,128]{1,0:T(8,128)(2,1)S(1)}, bf16[400,128]{1,0:T(8,128)(2,1)S(1)}, u32[]{:S(2)}, u32[]{:S(2)}) collective-permute-start(bf16[400,128]{1,0:T(8,128)(2,1)S(1)} %get-tuple-element.29), channel_id=1, source_target_pairs={{0,64},{8,72},{16,80},{24,88},{32,96},{40,104},{48,112},{56,120},{... | collective-permute-start | bytes 307208 | tf_op jit(solution)/shard_map/ppermute | solution.py:406
  61.4 1.4 %collective-permute-start.16 = (bf16[400,128]{1,0:T(8,128)(2,1)S(1)}, bf16[400,128]{1,0:T(8,128)(2,1)S(1)}, u32[]{:S(2)}, u32[]{:S(2)}) collective-permute-start(bf16[400,128]{1,0:T(8,128)(2,1)S(1)} %get-tuple-element.30), channel_id=1, source_target_pairs={{0,96},{8,104},{16,112},{24,120},{32,0},{40,8},{48,16},{56,24},{64... | collective-permute-start | bytes 307208 | tf_op jit(solution)/shard_map/ppermute | solution.py:406
  63.1 2.0 %collective-permute-done.15.part2 = bf16[400,128]{1,0:T(8,128)(2,1)S(1)} collective-permute-done((bf16[400,128]{1,0:T(8,128)(2,1)S(1)}, bf16[400,128]{1,0:T(8,128)(2,1)S(1)}, u32[]{:S(2)}, u32[]{:S(2)}) %collective-permute-start.15) | collective-permute-done | bytes 102432 | tf_op jit(solution)/shard_map/ppermute | solution.py:406
  (47 shorter events, 6.3 us)
Async XLA Ops:
  0.0 21.2 %copy-start.4 = (s32[16]{0:T(128)S(1)}, s32[16]{0:T(128)}, u32[]{:S(2)}) copy-start(s32[16]{0:T(128)} %kinds_ref.5) | copy-start | bytes 196
  0.0 21.2 %copy-start.5 = (bf16[512,384]{1,0:T(8,128)(2,1)S(1)}, bf16[512,384]{1,0:T(8,128)(2,1)}, u32[]{:S(2)}) copy-start(bf16[512,384]{1,0:T(8,128)(2,1)} %mid_hbm.1) | copy-start | bytes 1179652
  2.6 18.6 %all-to-all-start = ((bf16[16,128,128]{2,1,0:T(8,128)(2,1)}), bf16[16,128,128]{2,1,0:T(8,128)(2,1)S(1)}, u32[]{:S(2)}, u32[]{:S(2)}) async-start(bf16[16,128,128]{2,1,0:T(8,128)(2,1)} %get-tuple-element.18), calls=%async_computation | async-start | bytes 1048576 | tf_op jit(solution)/shard_map/all_to_all | solution.py:696
  9.5 6.2 %collective-permute-start.2 = (bf16[64,384]{1,0:T(8,128)(2,1)}, bf16[64,384]{1,0:T(8,128)(2,1)S(1)}, u32[]{:S(2)}, u32[]{:S(2)}) collective-permute-start(bf16[64,384]{1,0:T(8,128)(2,1)} %get-tuple-element.19.own_ref), channel_id=1, source_target_pairs={{0,6},{2,0},{4,2},{6,4},{1,7},{3,1},{5,3},{7,5},{8,14},{10,8},{12,... | collective-permute-start | bytes 147464 | tf_op jit(solution)/shard_map/ppermute | solution.py:301
  13.6 5.9 %collective-permute-start.1 = (bf16[64,384]{1,0:T(8,128)(2,1)}, bf16[64,384]{1,0:T(8,128)(2,1)S(1)}, u32[]{:S(2)}, u32[]{:S(2)}) collective-permute-start(bf16[64,384]{1,0:T(8,128)(2,1)} %get-tuple-element.19.own_ref), channel_id=1, source_target_pairs={{0,4},{2,6},{4,0},{6,2},{1,5},{3,7},{5,1},{7,3},{8,12},{10,14},{12... | collective-permute-start | bytes 147464 | tf_op jit(solution)/shard_map/ppermute | solution.py:301
  13.6 6.0 %collective-permute-start = (bf16[64,384]{1,0:T(8,128)(2,1)}, bf16[64,384]{1,0:T(8,128)(2,1)S(1)}, u32[]{:S(2)}, u32[]{:S(2)}) collective-permute-start(bf16[64,384]{1,0:T(8,128)(2,1)} %get-tuple-element.19.own_ref), channel_id=1, source_target_pairs={{0,2},{2,4},{4,6},{6,0},{1,3},{3,5},{5,7},{7,1},{8,10},{10,12},{12... | collective-permute-start | bytes 147464 | tf_op jit(solution)/shard_map/ppermute | solution.py:301
  19.7 1.5 %collective-permute-start.3 = (bf16[3,64,384]{2,1,0:T(8,128)(2,1)S(1)}, bf16[3,64,384]{2,1,0:T(8,128)(2,1)S(1)}, u32[]{:S(2)}, u32[]{:S(2)}) collective-permute-start(bf16[3,64,384]{2,1,0:T(8,128)(2,1)S(1)} %stack.2.same_ref), channel_id=1, source_target_pairs={{0,1},{1,0},{2,3},{3,2},{4,5},{5,4},{6,7},{7,6},{8,9},{9,8},{10,11... | collective-permute-start | bytes 442376 | tf_op jit(solution)/shard_map/ppermute | solution.py:306
  21.2 16.6 %slice-start = ((s8[7077888]{0:T(1024)(128)(4,1)}), s8[2883584]{0:T(1024)(128)(4,1)S(1)}, s32[]{:S(2)}) async-start(s8[7077888]{0:T(1024)(128)(4,1)} %bitcast.6), calls=%async_computation.1 | async-start | bytes 5767168
  24.6 13.2 %slice-start.1 = ((s8[7077888]{0:T(1024)(128)(4,1)}), s8[4194304]{0:T(1024)(128)(4,1)S(1)}, s32[]{:S(2)}) async-start(s8[7077888]{0:T(1024)(128)(4,1)} %bitcast.6), calls=%async_computation.2 | async-start | bytes 8388608
  24.6 13.1 %copy-start = (bf16[128,128]{1,0:T(8,128)(2,1)S(1)}, bf16[128,128]{1,0:T(8,128)(2,1)}, u32[]{:S(2)}) copy-start(bf16[128,128]{1,0:T(8,128)(2,1)} %constant.12.clone.perm_ref) | copy-start | bytes 98308
  24.6 13.1 %copy-start.1 = (f32[2,3072]{1,0:T(2,128)S(1)}, f32[2,3072]{1,0:T(2,128)}, u32[]{:S(2)}) copy-start(f32[2,3072]{1,0:T(2,128)} %mod_ref.3) | copy-start | bytes 73732
  24.7 7.7 %collective-permute-start.7 = (bf16[144,384]{1,0:T(8,128)(2,1)S(1)}, bf16[144,384]{1,0:T(8,128)(2,1)S(1)}, u32[]{:S(2)}, u32[]{:S(2)}) collective-permute-start(bf16[144,384]{1,0:T(8,128)(2,1)S(1)} %embed.1.own_ref), channel_id=1, source_target_pairs={{0,6},{2,0},{4,2},{6,4},{1,7},{3,1},{5,3},{7,5},{8,14},{10,8},{12,... | collective-permute-start | bytes 331784 | tf_op jit(solution)/shard_map/ppermute | solution.py:301
  28.7 6.4 %collective-permute-start.6 = (bf16[144,384]{1,0:T(8,128)(2,1)S(1)}, bf16[144,384]{1,0:T(8,128)(2,1)S(1)}, u32[]{:S(2)}, u32[]{:S(2)}) collective-permute-start(bf16[144,384]{1,0:T(8,128)(2,1)S(1)} %embed.1.own_ref), channel_id=1, source_target_pairs={{0,4},{2,6},{4,0},{6,2},{1,5},{3,7},{5,1},{7,3},{8,12},{10,14},{12... | collective-permute-start | bytes 331784 | tf_op jit(solution)/shard_map/ppermute | solution.py:301
  28.7 7.1 %collective-permute-start.5 = (bf16[144,384]{1,0:T(8,128)(2,1)S(1)}, bf16[144,384]{1,0:T(8,128)(2,1)S(1)}, u32[]{:S(2)}, u32[]{:S(2)}) collective-permute-start(bf16[144,384]{1,0:T(8,128)(2,1)S(1)} %embed.1.own_ref), channel_id=1, source_target_pairs={{0,2},{2,4},{4,6},{6,0},{1,3},{3,5},{5,7},{7,1},{8,10},{10,12},{12... | collective-permute-start | bytes 331784 | tf_op jit(solution)/shard_map/ppermute | solution.py:301
  35.9 1.9 %collective-permute-start.8 = (bf16[3,144,384]{2,1,0:T(8,128)(2,1)S(1)}, bf16[3,144,384]{2,1,0:T(8,128)(2,1)S(1)}, u32[]{:S(2)}, u32[]{:S(2)}) collective-permute-start(bf16[3,144,384]{2,1,0:T(8,128)(2,1)S(1)} %stack.3.same_ref), channel_id=1, source_target_pairs={{0,1},{1,0},{2,3},{3,2},{4,5},{5,4},{6,7},{7,6},{8,9},{9,8},{10,11... | collective-permute-start | bytes 995336 | tf_op jit(solution)/shard_map/ppermute | solution.py:306
  36.0 1.8 %collective-permute-start.4 = (bf16[144,384]{1,0:T(8,128)(2,1)S(1)}, bf16[144,384]{1,0:T(8,128)(2,1)S(1)}, u32[]{:S(2)}, u32[]{:S(2)}) collective-permute-start(bf16[144,384]{1,0:T(8,128)(2,1)S(1)} %embed.1.own_ref), channel_id=1, source_target_pairs={{0,1},{1,0},{2,3},{3,2},{4,5},{5,4},{6,7},{7,6},{8,9},{9,8},{10,11... | collective-permute-start | bytes 331784 | tf_op jit(solution)/shard_map/ppermute | solution.py:304
  36.5 5.9 %collective-permute-start.13 = (bf16[64,384]{1,0:T(8,128)(2,1)S(1)}, bf16[64,384]{1,0:T(8,128)(2,1)S(1)}, u32[]{:S(2)}, u32[]{:S(2)}) collective-permute-start(bf16[64,384]{1,0:T(8,128)(2,1)S(1)} %copy-done.2), channel_id=1, source_target_pairs={{0,1},{1,0},{2,3},{3,2},{4,5},{5,4},{6,7},{7,6},{8,9},{9,8},{10,11... | collective-permute-start | bytes 147464 | tf_op jit(solution)/shard_map/ppermute | solution.py:304
  40.3 7.0 %collective-permute-start.10 = (bf16[2,128,384]{2,1,0:T(8,128)(2,1)S(1)}, bf16[2,128,384]{2,1,0:T(8,128)(2,1)S(1)}, u32[]{:S(2)}, u32[]{:S(2)}) collective-permute-start(bf16[2,128,384]{2,1,0:T(8,128)(2,1)S(1)} %far.1.far_ref.far0), channel_id=1, source_target_pairs={{0,24},{8,0},{16,8},{24,16},{32,56},{40,32},{48,40},{56,48},{64,88... | collective-permute-start | bytes 589832 | tf_op jit(solution)/shard_map/ppermute | solution.py:402
  41.9 8.2 %collective-permute-start.9 = (bf16[2,128,384]{2,1,0:T(8,128)(2,1)S(1)}, bf16[2,128,384]{2,1,0:T(8,128)(2,1)S(1)}, u32[]{:S(2)}, u32[]{:S(2)}) collective-permute-start(bf16[2,128,384]{2,1,0:T(8,128)(2,1)S(1)} %far.1.far_ref.far0), channel_id=1, source_target_pairs={{0,8},{8,16},{16,24},{24,0},{32,40},{40,48},{48,56},{56,32},{64,72... | collective-permute-start | bytes 589832 | tf_op jit(solution)/shard_map/ppermute | solution.py:402
  47.3 5.0 %collective-permute-start.12 = (bf16[128,384]{1,0:T(8,128)(2,1)S(1)}, bf16[128,384]{1,0:T(8,128)(2,1)S(1)}, u32[]{:S(2)}, u32[]{:S(2)}) collective-permute-start(bf16[128,384]{1,0:T(8,128)(2,1)S(1)} %slice_bitcast_fusion), channel_id=1, source_target_pairs={{0,24},{8,0},{16,8},{24,16},{32,56},{40,32},{48,40},{56,48},{64,88... | collective-permute-start | bytes 294920 | tf_op jit(solution)/shard_map/ppermute | solution.py:402
  50.2 5.9 %collective-permute-start.11 = (bf16[128,384]{1,0:T(8,128)(2,1)S(1)}, bf16[128,384]{1,0:T(8,128)(2,1)S(1)}, u32[]{:S(2)}, u32[]{:S(2)}) collective-permute-start(bf16[128,384]{1,0:T(8,128)(2,1)S(1)} %slice_bitcast_fusion.1), channel_id=1, source_target_pairs={{0,8},{8,16},{16,24},{24,0},{32,40},{40,48},{48,56},{56,32},{64,72... | collective-permute-start | bytes 294920 | tf_op jit(solution)/shard_map/ppermute | solution.py:402
  57.2 5.9 %collective-permute-start.14 = (bf16[400,128]{1,0:T(8,128)(2,1)S(1)}, bf16[400,128]{1,0:T(8,128)(2,1)S(1)}, u32[]{:S(2)}, u32[]{:S(2)}) collective-permute-start(bf16[400,128]{1,0:T(8,128)(2,1)S(1)} %get-tuple-element.28), channel_id=1, source_target_pairs={{0,32},{8,40},{16,48},{24,56},{32,64},{40,72},{48,80},{56,88},{64,... | collective-permute-start | bytes 307208 | tf_op jit(solution)/shard_map/ppermute | solution.py:406
  58.7 6.4 %collective-permute-start.15 = (bf16[400,128]{1,0:T(8,128)(2,1)S(1)}, bf16[400,128]{1,0:T(8,128)(2,1)S(1)}, u32[]{:S(2)}, u32[]{:S(2)}) collective-permute-start(bf16[400,128]{1,0:T(8,128)(2,1)S(1)} %get-tuple-element.29), channel_id=1, source_target_pairs={{0,64},{8,72},{16,80},{24,88},{32,96},{40,104},{48,112},{56,120},{... | collective-permute-start | bytes 307208 | tf_op jit(solution)/shard_map/ppermute | solution.py:406
  61.4 4.7 %collective-permute-start.16 = (bf16[400,128]{1,0:T(8,128)(2,1)S(1)}, bf16[400,128]{1,0:T(8,128)(2,1)S(1)}, u32[]{:S(2)}, u32[]{:S(2)}) collective-permute-start(bf16[400,128]{1,0:T(8,128)(2,1)S(1)} %get-tuple-element.30), channel_id=1, source_target_pairs={{0,96},{8,104},{16,112},{24,120},{32,0},{40,8},{48,16},{56,24},{64... | collective-permute-start | bytes 307208 | tf_op jit(solution)/shard_map/ppermute | solution.py:406
  (5 other events, 51.7 us)

commit v3 on v2

--- a/solution.py
+++ b/solution.py
@@ -115,12 +115,11 @@
     ]
     for copy in copies + staged:
         copy.start()
-    for copy in copies:
-        copy.wait()
+    kinds_copy, sec_copy, hist_copy = copies
+    own = select_rows(64, 64, lambda i: (i & 31) * 2 + (i >> 5))
+    kinds_copy.wait()
     kind = kinds_ref[lax.axis_index("frame")]
-    cells = hist_ref[...]
-
-    own = select_rows(64, 64, lambda i: (i & 31) * 2 + (i >> 5))
+    sec_copy.wait()
     section = dot(own, sec_ref[...]).astype(BF)
     for d in range(16):
         out_ref[d, 64:128, :] = section
@@ -132,7 +131,8 @@
         rows = select_rows(
             128, 512, lambda i: (i >> 5) * 128 + ((i >> 1) & 15) * 8 + z * 2 + (i & 1)
         )
-        out = dot(rows, dot(cells, cols).astype(BF)).astype(BF)
+        hist_copy.wait()
+        out = dot(rows, dot(hist_ref[...], cols).astype(BF)).astype(BF)
         blank = jnp.zeros((32, 128), BF)
         for d in range(16):
             t = d // 4
@@ -149,7 +149,8 @@
             + ((j >> 7) & 1) * 4
             + (j & 3),
         )
-        out = dot(dot(cells, cols).astype(BF), lanes, ((0,), (0,))).astype(BF)
+        hist_copy.wait()
+        out = dot(dot(hist_ref[...], cols).astype(BF), lanes, ((0,), (0,))).astype(BF)
         for d in range(16):
             g, q = d // 4, d % 4
             for w in range(4):
@@ -162,7 +163,8 @@
         lanes = select_columns(
             512, 512, lambda j: ((j >> 3) & 3) * 128 + (j >> 5) * 8 + (j & 7)
         )
-        out = dot(cells, lanes, ((0,), (0,))).astype(BF)
+        hist_copy.wait()
+        out = dot(hist_ref[...], lanes, ((0,), (0,))).astype(BF)
         for d in range(16):
             for g in range(4):
                 out_ref[d, 16 * g : 16 * g + 16, :] = out[
@@ -199,7 +201,7 @@
     recv_ref,
     mid_hbm,
     coarse_hbm,
-    other_ref,
+    fine_ref,
     out_ref,
     mid_ref,
     coarse_ref,
@@ -208,7 +210,7 @@
     mid_sem,
     coarse_sem,
 ):
-    del other_ref
+    del fine_ref
     mid_copy = pltpu.make_async_copy(mid_hbm, mid_ref, mid_sem)
     coarse_copy = pltpu.make_async_copy(coarse_hbm, coarse_ref, coarse_sem)
     mid_copy.start()
@@ -260,7 +262,7 @@
     out_ref[112:128, :] = total.astype(BF)
 
 
-def embed(kinds, received, patch_mid, patch_coarse, fine_other):
+def embed(kinds, received, patch_mid, patch_coarse, fine):
     return pl.pallas_call(
         embed_kernel,
         out_shape=jax.ShapeDtypeStruct((144, patch_mid.shape[1]), BF),
@@ -274,9 +276,9 @@
         ]
         + [pltpu.SemaphoreType.DMA] * 2,
         compiler_params=params(EMBED),
-        cost_estimate=cost(2e9, 5e6),
+        cost_estimate=cost(1e6, 1e4),
         name="embed",
-    )(kinds, received, patch_mid, patch_coarse, fine_other)
+    )(kinds, received, patch_mid, patch_coarse, fine)
 
 
 def stack_kernel(*refs):
@@ -302,14 +304,14 @@
     )
     swap = [(0, 1), (1, 0)]
     twin = lax.ppermute(block, "fsdp", swap)
-    same = stack((ring1, ring2, ring3), estimate)
+    same = stack((ring3, ring2, ring1), estimate)
     return block, twin, same, lax.ppermute(same, "fsdp", swap)
 
 
 def pairs(own_ref, twin_ref, same_ref, other_ref):
     yield 0, own_ref, twin_ref
     for d in range(3):
-        yield d + 1, same_ref.at[d], other_ref.at[d]
+        yield 3 - d, same_ref.at[d], other_ref.at[d]
 
 
 def place_columns(gathered, full_ref):
@@ -623,7 +625,7 @@
     )(kinds, *gathered, modulation, w_qkv, perm, freqs)
 
 
-def history_kernel(far0, far1, far3, key2, value2, query_ref, num_ref, den_ref, out0, out1, out2, out3):
+def history_kernel(far0, far1, far3, far2, query_ref, num_ref, den_ref, out0, out1, out2, out3):
     heads = query_ref.shape[0] // HEAD_DIM
     count = query_ref.shape[1]
     outs = (out0, out1, out2, out3)
@@ -631,9 +633,9 @@
     tail = jnp.zeros((16, count), F32)
     for h in range(heads):
         at = slice(HEAD_DIM * h, HEAD_DIM * (h + 1))
-        fars = (far0, far1, far3)
-        keys = jnp.concatenate([far[0, :, at] for far in fars] + [key2[:, at]], axis=0)
-        values = jnp.concatenate([far[1, :, at] for far in fars] + [value2[:, at]], axis=0)
+        fars = (far0, far1, far3, far2)
+        keys = jnp.concatenate([far[0, :, at] for far in fars], axis=0)
+        values = jnp.concatenate([far[1, :, at] for far in fars], axis=0)
         weights = jnp.exp2(dot(keys, query_ref[at, :]))
         high, rest = split(den_ref[h : h + 1, :] + jnp.sum(weights, axis=0, keepdims=True))
         tail = jnp.where(rows == h, high.astype(F32), tail)
@@ -650,7 +652,7 @@
     return pl.pallas_call(
         history_kernel,
         out_shape=tuple(jax.ShapeDtypeStruct((columns + 16, 128), t) for t in (F32, BF, BF, BF)),
-        in_specs=[VMEM] * 8,
+        in_specs=[VMEM] * 7,
         out_specs=tuple([VMEM] * 4),
         compiler_params=params(),
         cost_estimate=cost(2e9, 4e6, 1e6),
@@ -694,18 +696,17 @@
 
     sent, patch_fine = prepare(slab_kernel, history, section, patch_fine)
     received = lax.all_to_all(sent, "frame", 0, 0, tiled=True)
-    fine = gather_columns(patch_fine, cost(1e6, 4e5))
-    features = embed(slab_kernel, received, patch_mid, patch_coarse, fine[3])
+    fine = gather_columns(patch_fine, cost(1e6, 1e5))
+    features = embed(slab_kernel, received, patch_mid, patch_coarse, fine[2])
     gathered = gather_columns(features, cost(2e10, 1e6))
     far = make_far(slab_kernel, gathered, modulation, w_qkv, perm, freqs)
-    far1, far3 = along_x(far, 1), along_x(far, 3)
-    far2 = along_x(far1[0], 1), along_x(far3[1], 3)
+    far2, far1, far3 = (along_x(far, d) for d in (2, 1, 3))
     folded, gram = fold(fine, modulation, w_qkv, perm, far)
     queries, keys, values = make_tokens(
         slab_kernel, received, gathered, folded, gram, cosine, sine, times
     )
     numerator, denominator = attend_near(queries, keys, values)
-    fars = [far, far1, far3, *far2]
+    fars = [far, far2, far3, far1]
     parts = attend_history(fars, queries, numerator, denominator)
     part2 = along_y(parts[2], 2)
     return combine([parts[0], along_y(parts[1], 1), part2, along_y(parts[3], 3)])

time: 67.1 us -> 62.1 us (0.925)
  waiting for transfers between devices: 21.3 us -> 17.4 us
  starting transfers between devices: 29 us -> 28.2 us
    ppermute x6, waiting for transfers between devices: 10.7 us -> 7.03 us  [gather_columns(): lax.ppermute(block, 'head', [(i, (i + d) % 4) for i in range(4)])]
    ppermute x6, starting transfers between devices: 10.6 us -> 13.2 us  [gather_columns(): lax.ppermute(block, 'head', [(i, (i + d) % 4) for i in range(4)])]
    ppermute x3, starting transfers between devices: 5.66 us -> 3.53 us  [along_y(): lax.ppermute(value, 'frame', [(i, (i + 4 * d) % 16) for i in range(16)])]
    ppermute x4 -> x3, starting transfers between devices: 4.99 us -> 3.31 us  [along_x(): lax.ppermute(value, 'frame', [(i, i // 4 * 4 + (i + d) % 4) for i in rang...]
    all_to_all x1, waiting for transfers between devices: 0.01 us -> 1.65 us  [per_device(): received = lax.all_to_all(sent, 'frame', 0, 0, tiled=True)]
    ppermute x4 -> x3, waiting for transfers between devices: 4.83 us -> 3.27 us  [along_x(): lax.ppermute(value, 'frame', [(i, i // 4 * 4 + (i + d) % 4) for i in rang...]
    ppermute x3, waiting for transfers between devices: 3.21 us -> 4.64 us  [along_y(): lax.ppermute(value, 'frame', [(i, (i + 4 * d) % 16) for i in range(16)])]
    ppermute x2, waiting for transfers between devices: 1.36 us -> 0.01 us  [gather_columns(): return (block, twin, same, lax.ppermute(same, 'fsdp', swap))]
  transfers between devices with their start and end apart: 18 -> 17, of which waited for: 14 -> 10; matrix products, arithmetic and copies ran while one was open for 0% -> 0% of each run, Pallas kernels for 12% -> 13%
where the time goes in v3:
time: 62.1 us; the launch traced here: 62 us
  starting transfers between devices  28.2 us (45%)
  waiting for transfers between devices  17.4 us (28%)
  Pallas kernels  16.1 us (26%)
    ppermute x6, starting transfers between devices, gather_columns(): lax.ppermute(block, 'head', [(i, (i + d) % 4) for i in range(4)])  13.2 us
    all_to_all x1, starting transfers between devices, per_device(): received = lax.all_to_all(sent, 'frame', 0, 0, tiled=True)  7.13 us
    ppermute x6, waiting for transfers between devices, gather_columns(): lax.ppermute(block, 'head', [(i, (i + d) % 4) for i in range(4)])  7.03 us
    ppermute x3, waiting for transfers between devices, along_y(): lax.ppermute(value, 'frame', [(i, (i + 4 * d) % 16) for i in range(16)])  4.64 us
    ppermute x3, starting transfers between devices, along_y(): lax.ppermute(value, 'frame', [(i, (i + 4 * d) % 16) for i in range(16)])  3.53 us
    pallas_call x1, Pallas kernels, embed(): pl.pallas_call(embed_kernel, out_shape=jax.ShapeDtypeStruct((144, patch_m...  3.43 us
    ppermute x3, starting transfers between devices, along_x(): lax.ppermute(value, 'frame', [(i, i // 4 * 4 + (i + d) % 4) for i in rang...  3.31 us
    ppermute x3, waiting for transfers between devices, along_x(): lax.ppermute(value, 'frame', [(i, i // 4 * 4 + (i + d) % 4) for i in rang...  3.27 us
  transfers between devices with their start and end apart: 17, of which 10 were waited for; matrix products, arithmetic and copies ran while one was open for 0% of the time, Pallas kernels for 13%

profile of v3, /device:TPU:0, one launch (start us, length us, event | category | flops | bytes accessed | tf_op | source)
XLA Modules:
  0.0 62.0 jit_solution(2387809162920485071)
XLA Ops:
  0.0 2.5 %prepare.1 = (bf16[16,128,128]{2,1,0:T(8,128)(2,1)}, bf16[64,384]{1,0:T(8,128)(2,1)}) custom-call(s32[16]{0:T(128)} %kinds_ref.5, bf16[512,256]{1,0:T(8,128)(2,1)} %bitcast.4, bf16[64,128]{1,0:T(8,128)(2,1)} %bitcast.5, bf16[64,384]{1,0:T(8,128)(2,1)} %fine_hbm.1), custom_call_target="tpu_custom_call" | custom-call | flops 20000000000 | bytes 1000000 | tf_op jit(solution)/shard_map/prepare/pallas_call | solution.py:179
  2.5 7.1 %all-to-all-start = ((bf16[16,128,128]{2,1,0:T(8,128)(2,1)}), bf16[16,128,128]{2,1,0:T(8,128)(2,1)S(1)}, u32[]{:S(2)}, u32[]{:S(2)}) async-start(bf16[16,128,128]{2,1,0:T(8,128)(2,1)} %get-tuple-element.18), calls=%async_computation | async-start | bytes 1048576 | tf_op jit(solution)/shard_map/all_to_all | solution.py:698
  9.7 2.0 %collective-permute-start.2 = (bf16[64,384]{1,0:T(8,128)(2,1)}, bf16[64,384]{1,0:T(8,128)(2,1)S(1)}, u32[]{:S(2)}, u32[]{:S(2)}) collective-permute-start(bf16[64,384]{1,0:T(8,128)(2,1)} %get-tuple-element.19.own_ref), channel_id=1, source_target_pairs={{0,2},{2,4},{4,6},{6,0},{1,3},{3,5},{5,7},{7,1},{8,10},{10,12},{12... | collective-permute-start | bytes 147464 | tf_op jit(solution)/shard_map/ppermute | solution.py:303
  11.6 3.6 %collective-permute-start.1 = (bf16[64,384]{1,0:T(8,128)(2,1)}, bf16[64,384]{1,0:T(8,128)(2,1)S(1)}, u32[]{:S(2)}, u32[]{:S(2)}) collective-permute-start(bf16[64,384]{1,0:T(8,128)(2,1)} %get-tuple-element.19.own_ref), channel_id=1, source_target_pairs={{0,4},{2,6},{4,0},{6,2},{1,5},{3,7},{5,1},{7,3},{8,12},{10,14},{12... | collective-permute-start | bytes 147464 | tf_op jit(solution)/shard_map/ppermute | solution.py:303
  15.2 1.0 %collective-permute-start = (bf16[64,384]{1,0:T(8,128)(2,1)}, bf16[64,384]{1,0:T(8,128)(2,1)S(1)}, u32[]{:S(2)}, u32[]{:S(2)}) collective-permute-start(bf16[64,384]{1,0:T(8,128)(2,1)} %get-tuple-element.19.own_ref), channel_id=1, source_target_pairs={{0,6},{2,0},{4,2},{6,4},{1,7},{3,1},{5,3},{7,5},{8,14},{10,8},{12,... | collective-permute-start | bytes 147464 | tf_op jit(solution)/shard_map/ppermute | solution.py:303
  16.2 1.8 %collective-permute-done.1.refs_1_ = bf16[64,384]{1,0:T(8,128)(2,1)S(1)} collective-permute-done((bf16[64,384]{1,0:T(8,128)(2,1)}, bf16[64,384]{1,0:T(8,128)(2,1)S(1)}, u32[]{:S(2)}, u32[]{:S(2)}) %collective-permute-start.1) | collective-permute-done | bytes 49184 | tf_op jit(solution)/shard_map/ppermute | solution.py:303
  18.0 1.5 %collective-permute-done.refs_0_ = bf16[64,384]{1,0:T(8,128)(2,1)S(1)} collective-permute-done((bf16[64,384]{1,0:T(8,128)(2,1)}, bf16[64,384]{1,0:T(8,128)(2,1)S(1)}, u32[]{:S(2)}, u32[]{:S(2)}) %collective-permute-start) | collective-permute-done | bytes 49184 | tf_op jit(solution)/shard_map/ppermute | solution.py:303
  19.5 1.6 %all-to-all-done.recv_ref = bf16[16,128,128]{2,1,0:T(8,128)(2,1)S(1)} async-done(((bf16[16,128,128]{2,1,0:T(8,128)(2,1)}), bf16[16,128,128]{2,1,0:T(8,128)(2,1)S(1)}, u32[]{:S(2)}, u32[]{:S(2)}) %all-to-all-start) | async-done | bytes 524320 | tf_op jit(solution)/shard_map/all_to_all | solution.py:698
  21.2 3.4 %embed.1.own_ref = bf16[144,384]{1,0:T(8,128)(2,1)S(1)} custom-call(s32[16]{0:T(128)S(1)} %copy-done.5, bf16[16,128,128]{2,1,0:T(8,128)(2,1)S(1)} %all-to-all-done.recv_ref, bf16[512,384]{1,0:T(8,128)(2,1)S(1)} %copy-done, bf16[4096,384]{1,0:T(8,128)(2,1)} %coarse_hbm.1, bf16[3,64,384]{2,1,0:T(8,128)(2,1)S(1)} %stack.2.fine_ref.same_ref), custom_call_target="tpu_custom_call" | custom-call | flops 1000000 | bytes 10000 | tf_op jit(solution)/shard_map/embed/pallas_call | solution.py:266
  24.7 2.0 %collective-permute-start.6 = (bf16[144,384]{1,0:T(8,128)(2,1)S(1)}, bf16[144,384]{1,0:T(8,128)(2,1)S(1)}, u32[]{:S(2)}, u32[]{:S(2)}) collective-permute-start(bf16[144,384]{1,0:T(8,128)(2,1)S(1)} %embed.1.own_ref), channel_id=1, source_target_pairs={{0,2},{2,4},{4,6},{6,0},{1,3},{3,5},{5,7},{7,1},{8,10},{10,12},{12... | collective-permute-start | bytes 331784 | tf_op jit(solution)/shard_map/ppermute | solution.py:303
  26.7 3.6 %collective-permute-start.5 = (bf16[144,384]{1,0:T(8,128)(2,1)S(1)}, bf16[144,384]{1,0:T(8,128)(2,1)S(1)}, u32[]{:S(2)}, u32[]{:S(2)}) collective-permute-start(bf16[144,384]{1,0:T(8,128)(2,1)S(1)} %embed.1.own_ref), channel_id=1, source_target_pairs={{0,4},{2,6},{4,0},{6,2},{1,5},{3,7},{5,1},{7,3},{8,12},{10,14},{12... | collective-permute-start | bytes 331784 | tf_op jit(solution)/shard_map/ppermute | solution.py:303
  30.3 1.0 %collective-permute-start.4 = (bf16[144,384]{1,0:T(8,128)(2,1)S(1)}, bf16[144,384]{1,0:T(8,128)(2,1)S(1)}, u32[]{:S(2)}, u32[]{:S(2)}) collective-permute-start(bf16[144,384]{1,0:T(8,128)(2,1)S(1)} %embed.1.own_ref), channel_id=1, source_target_pairs={{0,6},{2,0},{4,2},{6,4},{1,7},{3,1},{5,3},{7,5},{8,14},{10,8},{12,... | collective-permute-start | bytes 331784 | tf_op jit(solution)/shard_map/ppermute | solution.py:303
  31.3 1.4 %collective-permute-done.6.refs_2_ = bf16[144,384]{1,0:T(8,128)(2,1)S(1)} collective-permute-done((bf16[144,384]{1,0:T(8,128)(2,1)S(1)}, bf16[144,384]{1,0:T(8,128)(2,1)S(1)}, u32[]{:S(2)}, u32[]{:S(2)}) %collective-permute-start.6) | collective-permute-done | bytes 110624 | tf_op jit(solution)/shard_map/ppermute | solution.py:303
  32.7 1.5 %collective-permute-done.5.refs_1_ = bf16[144,384]{1,0:T(8,128)(2,1)S(1)} collective-permute-done((bf16[144,384]{1,0:T(8,128)(2,1)S(1)}, bf16[144,384]{1,0:T(8,128)(2,1)S(1)}, u32[]{:S(2)}, u32[]{:S(2)}) %collective-permute-start.5) | collective-permute-done | bytes 110624 | tf_op jit(solution)/shard_map/ppermute | solution.py:303
  37.0 2.4 %far.1.far_ref.far0 = bf16[2,128,384]{2,1,0:T(8,128)(2,1)S(1)} custom-call(s32[16]{0:T(128)S(1)} %copy-done.5, bf16[144,384]{1,0:T(8,128)(2,1)S(1)} %embed.1.own_ref, bf16[144,384]{1,0:T(8,128)(2,1)S(1)} %collective-permute-done.3.twin_ref, bf16[3,144,384]{2,1,0:T(8,128)(2,1)S(1)} %stack.3.same_ref, ...), custom_call_target="tpu_custom_call" | custom-call | flops 2000000000 | bytes 10000000 | tf_op jit(solution)/shard_map/far/pallas_call | solution.py:616
  40.1 2.7 %collective-permute-start.9 = (bf16[2,128,384]{2,1,0:T(8,128)(2,1)S(1)}, bf16[2,128,384]{2,1,0:T(8,128)(2,1)S(1)}, u32[]{:S(2)}, u32[]{:S(2)}) collective-permute-start(bf16[2,128,384]{2,1,0:T(8,128)(2,1)S(1)} %far.1.far_ref.far0), channel_id=1, source_target_pairs={{0,24},{8,0},{16,8},{24,16},{32,56},{40,32},{48,40},{56,48},{64,88... | collective-permute-start | bytes 589832 | tf_op jit(solution)/shard_map/ppermute | solution.py:404
  42.8 2.3 %fold.1 = (bf16[3,144,384]{2,1,0:T(8,128)(2,1)S(1)}, f32[64,64]{1,0:T(8,128)S(1)}) custom-call(bf16[64,384]{1,0:T(8,128)(2,1)S(1)} %copy-done.3, bf16[64,384]{1,0:T(8,128)(2,1)S(1)} %collective-permute-done.11.twin_ref, bf16[3,64,384]{2,1,0:T(8,128)(2,1)S(1)} %stack.2.fine_ref.same_ref, bf16[3,64,384]{2,1,0:T(8,128)(2,1)S(1)} %collective-permute-done.12.other_ref, ...), custom_call_target="tpu_custom_call" | custom-call | flops 1000000 | bytes 10000 | tf_op jit(solution)/shard_map/fold/pallas_call | solution.py:388
  45.1 2.0 %tokens.1 = (bf16[384,512]{1,0:T(8,128)(2,1)S(1)}, bf16[384,1024]{1,0:T(8,128)(2,1)S(1)}, bf16[384,1024]{1,0:T(8,128)(2,1)S(1)}) custom-call(s32[16]{0:T(128)S(1)} %copy-done.5, bf16[16,128,128]{2,1,0:T(8,128)(2,1)S(1)} %all-to-all-done.recv_ref, bf16[144,384]{1,0:T(8,128)(2,1)S(1)} %embed.1.own_ref, bf16[144,384]{1,0:T(8,128)(2,1)S(1)} %collective-permute-done.3.twin_ref, ...), custom_call_target="tpu_custom_call" | custom-call | flops 2000000000 | bytes 8000000 | tf_op jit(solution)/shard_map/tokens/pallas_call | solution.py:510
  47.1 1.5 %near.1 = (f32[384,512]{1,0:T(8,128)S(1)}, f32[8,512]{1,0:T(8,128)S(1)}) custom-call(bf16[384,512]{1,0:T(8,128)(2,1)S(1)} %get-tuple-element.22.query_ref, bf16[384,1024]{1,0:T(8,128)(2,1)S(1)} %get-tuple-element.23.key_ref, bf16[384,1024]{1,0:T(8,128)(2,1)S(1)} %get-tuple-element.24.value_ref), custom_call_target="tpu_custom_call" | custom-call | flops 4000000000 | bytes 10000000 | tf_op jit(solution)/shard_map/near/pallas_call | solution.py:537
  48.6 3.3 %collective-permute-done.10.far2 = bf16[2,128,384]{2,1,0:T(8,128)(2,1)S(1)} collective-permute-done((bf16[2,128,384]{2,1,0:T(8,128)(2,1)S(1)}, bf16[2,128,384]{2,1,0:T(8,128)(2,1)S(1)}, u32[]{:S(2)}, u32[]{:S(2)}) %collective-permute-start.10) | collective-permute-done | bytes 196640 | tf_op jit(solution)/shard_map/ppermute | solution.py:404
  51.9 1.1 %history.1 = (f32[400,128]{1,0:T(8,128)S(1)}, bf16[400,128]{1,0:T(8,128)(2,1)S(1)}, bf16[400,128]{1,0:T(8,128)(2,1)S(1)}, bf16[400,128]{1,0:T(8,128)(2,1)S(1)}) custom-call(bf16[2,128,384]{2,1,0:T(8,128)(2,1)S(1)} %far.1.far_ref.far0, bf16[2,128,384]{2,1,0:T(8,128)(2,1)S(1)} %collective-permute-done.8.far1, ...), custom_call_target="tpu_custom_call" | custom-call | flops 2000000000 | bytes 4000000 | tf_op jit(solution)/shard_map/history/pallas_call | solution.py:652
  53.1 2.3 %collective-permute-start.14 = (bf16[400,128]{1,0:T(8,128)(2,1)S(1)}, bf16[400,128]{1,0:T(8,128)(2,1)S(1)}, u32[]{:S(2)}, u32[]{:S(2)}) collective-permute-start(bf16[400,128]{1,0:T(8,128)(2,1)S(1)} %get-tuple-element.29), channel_id=1, source_target_pairs={{0,64},{8,72},{16,80},{24,88},{32,96},{40,104},{48,112},{56,120},{... | collective-permute-start | bytes 307208 | tf_op jit(solution)/shard_map/ppermute | solution.py:408
  55.4 1.1 %collective-permute-start.15 = (bf16[400,128]{1,0:T(8,128)(2,1)S(1)}, bf16[400,128]{1,0:T(8,128)(2,1)S(1)}, u32[]{:S(2)}, u32[]{:S(2)}) collective-permute-start(bf16[400,128]{1,0:T(8,128)(2,1)S(1)} %get-tuple-element.30), channel_id=1, source_target_pairs={{0,96},{8,104},{16,112},{24,120},{32,0},{40,8},{48,16},{56,24},{64... | collective-permute-start | bytes 307208 | tf_op jit(solution)/shard_map/ppermute | solution.py:408
  56.5 4.0 %collective-permute-done.13.part1 = bf16[400,128]{1,0:T(8,128)(2,1)S(1)} collective-permute-done((bf16[400,128]{1,0:T(8,128)(2,1)S(1)}, bf16[400,128]{1,0:T(8,128)(2,1)S(1)}, u32[]{:S(2)}, u32[]{:S(2)}) %collective-permute-start.13) | collective-permute-done | bytes 102432 | tf_op jit(solution)/shard_map/ppermute | solution.py:408
  (43 shorter events, 4.9 us)
Async XLA Ops:
  0.0 21.2 %copy-start = (bf16[512,384]{1,0:T(8,128)(2,1)S(1)}, bf16[512,384]{1,0:T(8,128)(2,1)}, u32[]{:S(2)}) copy-start(bf16[512,384]{1,0:T(8,128)(2,1)} %mid_hbm.1) | copy-start | bytes 1179652
  0.0 21.2 %copy-start.5 = (s32[16]{0:T(128)S(1)}, s32[16]{0:T(128)}, u32[]{:S(2)}) copy-start(s32[16]{0:T(128)} %kinds_ref.5) | copy-start | bytes 196
  2.5 18.7 %all-to-all-start = ((bf16[16,128,128]{2,1,0:T(8,128)(2,1)}), bf16[16,128,128]{2,1,0:T(8,128)(2,1)S(1)}, u32[]{:S(2)}, u32[]{:S(2)}) async-start(bf16[16,128,128]{2,1,0:T(8,128)(2,1)} %get-tuple-element.18), calls=%async_computation | async-start | bytes 1048576 | tf_op jit(solution)/shard_map/all_to_all | solution.py:698
  9.7 6.6 %collective-permute-start.2 = (bf16[64,384]{1,0:T(8,128)(2,1)}, bf16[64,384]{1,0:T(8,128)(2,1)S(1)}, u32[]{:S(2)}, u32[]{:S(2)}) collective-permute-start(bf16[64,384]{1,0:T(8,128)(2,1)} %get-tuple-element.19.own_ref), channel_id=1, source_target_pairs={{0,2},{2,4},{4,6},{6,0},{1,3},{3,5},{5,7},{7,1},{8,10},{10,12},{12... | collective-permute-start | bytes 147464 | tf_op jit(solution)/shard_map/ppermute | solution.py:303
  11.6 6.4 %collective-permute-start.1 = (bf16[64,384]{1,0:T(8,128)(2,1)}, bf16[64,384]{1,0:T(8,128)(2,1)S(1)}, u32[]{:S(2)}, u32[]{:S(2)}) collective-permute-start(bf16[64,384]{1,0:T(8,128)(2,1)} %get-tuple-element.19.own_ref), channel_id=1, source_target_pairs={{0,4},{2,6},{4,0},{6,2},{1,5},{3,7},{5,1},{7,3},{8,12},{10,14},{12... | collective-permute-start | bytes 147464 | tf_op jit(solution)/shard_map/ppermute | solution.py:303
  15.2 4.3 %collective-permute-start = (bf16[64,384]{1,0:T(8,128)(2,1)}, bf16[64,384]{1,0:T(8,128)(2,1)S(1)}, u32[]{:S(2)}, u32[]{:S(2)}) collective-permute-start(bf16[64,384]{1,0:T(8,128)(2,1)} %get-tuple-element.19.own_ref), channel_id=1, source_target_pairs={{0,6},{2,0},{4,2},{6,4},{1,7},{3,1},{5,3},{7,5},{8,14},{10,8},{12,... | collective-permute-start | bytes 147464 | tf_op jit(solution)/shard_map/ppermute | solution.py:303
  21.2 15.8 %slice-start = ((s8[7077888]{0:T(1024)(128)(4,1)}), s8[2883584]{0:T(1024)(128)(4,1)S(1)}, s32[]{:S(2)}) async-start(s8[7077888]{0:T(1024)(128)(4,1)} %bitcast.2), calls=%async_computation.1 | async-start | bytes 5767168
  24.6 12.3 %slice-start.1 = ((s8[7077888]{0:T(1024)(128)(4,1)}), s8[4194304]{0:T(1024)(128)(4,1)S(1)}, s32[]{:S(2)}) async-start(s8[7077888]{0:T(1024)(128)(4,1)} %bitcast.2), calls=%async_computation.2 | async-start | bytes 8388608
  24.7 12.3 %copy-start.1 = (bf16[128,128]{1,0:T(8,128)(2,1)S(1)}, bf16[128,128]{1,0:T(8,128)(2,1)}, u32[]{:S(2)}) copy-start(bf16[128,128]{1,0:T(8,128)(2,1)} %constant.12.clone.perm_ref) | copy-start | bytes 98308
  24.7 12.3 %copy-start.2 = (f32[2,3072]{1,0:T(2,128)S(1)}, f32[2,3072]{1,0:T(2,128)}, u32[]{:S(2)}) copy-start(f32[2,3072]{1,0:T(2,128)} %mod_ref.3) | copy-start | bytes 73732
  24.7 12.3 %copy-start.4 = (f32[8,128]{1,0:T(8,128)S(1)}, f32[8,128]{1,0:T(8,128)}, u32[]{:S(2)}) copy-start(f32[8,128]{1,0:T(8,128)} %constant.13.clone.freq_ref) | copy-start | bytes 12292
  24.7 8.0 %collective-permute-start.6 = (bf16[144,384]{1,0:T(8,128)(2,1)S(1)}, bf16[144,384]{1,0:T(8,128)(2,1)S(1)}, u32[]{:S(2)}, u32[]{:S(2)}) collective-permute-start(bf16[144,384]{1,0:T(8,128)(2,1)S(1)} %embed.1.own_ref), channel_id=1, source_target_pairs={{0,2},{2,4},{4,6},{6,0},{1,3},{3,5},{5,7},{7,1},{8,10},{10,12},{12... | collective-permute-start | bytes 331784 | tf_op jit(solution)/shard_map/ppermute | solution.py:303
  26.7 7.5 %collective-permute-start.5 = (bf16[144,384]{1,0:T(8,128)(2,1)S(1)}, bf16[144,384]{1,0:T(8,128)(2,1)S(1)}, u32[]{:S(2)}, u32[]{:S(2)}) collective-permute-start(bf16[144,384]{1,0:T(8,128)(2,1)S(1)} %embed.1.own_ref), channel_id=1, source_target_pairs={{0,4},{2,6},{4,0},{6,2},{1,5},{3,7},{5,1},{7,3},{8,12},{10,14},{12... | collective-permute-start | bytes 331784 | tf_op jit(solution)/shard_map/ppermute | solution.py:303
  30.3 4.7 %collective-permute-start.4 = (bf16[144,384]{1,0:T(8,128)(2,1)S(1)}, bf16[144,384]{1,0:T(8,128)(2,1)S(1)}, u32[]{:S(2)}, u32[]{:S(2)}) collective-permute-start(bf16[144,384]{1,0:T(8,128)(2,1)S(1)} %embed.1.own_ref), channel_id=1, source_target_pairs={{0,6},{2,0},{4,2},{6,4},{1,7},{3,1},{5,3},{7,5},{8,14},{10,8},{12,... | collective-permute-start | bytes 331784 | tf_op jit(solution)/shard_map/ppermute | solution.py:303
  35.1 1.9 %collective-permute-start.7 = (bf16[3,144,384]{2,1,0:T(8,128)(2,1)S(1)}, bf16[3,144,384]{2,1,0:T(8,128)(2,1)S(1)}, u32[]{:S(2)}, u32[]{:S(2)}) collective-permute-start(bf16[3,144,384]{2,1,0:T(8,128)(2,1)S(1)} %stack.3.same_ref), channel_id=1, source_target_pairs={{0,1},{1,0},{2,3},{3,2},{4,5},{5,4},{6,7},{7,6},{8,9},{9,8},{10,11... | collective-permute-start | bytes 995336 | tf_op jit(solution)/shard_map/ppermute | solution.py:308
  35.2 1.8 %collective-permute-start.3 = (bf16[144,384]{1,0:T(8,128)(2,1)S(1)}, bf16[144,384]{1,0:T(8,128)(2,1)S(1)}, u32[]{:S(2)}, u32[]{:S(2)}) collective-permute-start(bf16[144,384]{1,0:T(8,128)(2,1)S(1)} %embed.1.own_ref), channel_id=1, source_target_pairs={{0,1},{1,0},{2,3},{3,2},{4,5},{5,4},{6,7},{7,6},{8,9},{9,8},{10,11... | collective-permute-start | bytes 331784 | tf_op jit(solution)/shard_map/ppermute | solution.py:306
  35.7 7.1 %collective-permute-start.11 = (bf16[64,384]{1,0:T(8,128)(2,1)S(1)}, bf16[64,384]{1,0:T(8,128)(2,1)S(1)}, u32[]{:S(2)}, u32[]{:S(2)}) collective-permute-start(bf16[64,384]{1,0:T(8,128)(2,1)S(1)} %copy-done.3), channel_id=1, source_target_pairs={{0,1},{1,0},{2,3},{3,2},{4,5},{5,4},{6,7},{7,6},{8,9},{9,8},{10,11... | collective-permute-start | bytes 147464 | tf_op jit(solution)/shard_map/ppermute | solution.py:306
  35.8 7.0 %collective-permute-start.12 = (bf16[3,64,384]{2,1,0:T(8,128)(2,1)S(1)}, bf16[3,64,384]{2,1,0:T(8,128)(2,1)S(1)}, u32[]{:S(2)}, u32[]{:S(2)}) collective-permute-start(bf16[3,64,384]{2,1,0:T(8,128)(2,1)S(1)} %stack.2.fine_ref.same_ref), channel_id=1, source_target_pairs={{0,1},{1,0},{2,3},{3,2},{4,5},{5,4},{6,7},{7,6},{8,9},{9,8},{10,11... | collective-permute-start | bytes 442376 | tf_op jit(solution)/shard_map/ppermute | solution.py:308
  39.4 12.4 %collective-permute-start.10 = (bf16[2,128,384]{2,1,0:T(8,128)(2,1)S(1)}, bf16[2,128,384]{2,1,0:T(8,128)(2,1)S(1)}, u32[]{:S(2)}, u32[]{:S(2)}) collective-permute-start(bf16[2,128,384]{2,1,0:T(8,128)(2,1)S(1)} %far.1.far_ref.far0), channel_id=1, source_target_pairs={{0,8},{8,16},{16,24},{24,0},{32,40},{40,48},{48,56},{56,32},{64,72... | collective-permute-start | bytes 589832 | tf_op jit(solution)/shard_map/ppermute | solution.py:404
  40.1 11.8 %collective-permute-start.9 = (bf16[2,128,384]{2,1,0:T(8,128)(2,1)S(1)}, bf16[2,128,384]{2,1,0:T(8,128)(2,1)S(1)}, u32[]{:S(2)}, u32[]{:S(2)}) collective-permute-start(bf16[2,128,384]{2,1,0:T(8,128)(2,1)S(1)} %far.1.far_ref.far0), channel_id=1, source_target_pairs={{0,24},{8,0},{16,8},{24,16},{32,56},{40,32},{48,40},{56,48},{64,88... | collective-permute-start | bytes 589832 | tf_op jit(solution)/shard_map/ppermute | solution.py:404
  42.7 9.1 %collective-permute-start.8 = (bf16[2,128,384]{2,1,0:T(8,128)(2,1)S(1)}, bf16[2,128,384]{2,1,0:T(8,128)(2,1)S(1)}, u32[]{:S(2)}, u32[]{:S(2)}) collective-permute-start(bf16[2,128,384]{2,1,0:T(8,128)(2,1)S(1)} %far.1.far_ref.far0), channel_id=1, source_target_pairs={{0,16},{8,24},{16,0},{24,8},{32,48},{40,56},{48,32},{56,40},{64,80... | collective-permute-start | bytes 589832 | tf_op jit(solution)/shard_map/ppermute | solution.py:404
  53.0 7.6 %collective-permute-start.13 = (bf16[400,128]{1,0:T(8,128)(2,1)S(1)}, bf16[400,128]{1,0:T(8,128)(2,1)S(1)}, u32[]{:S(2)}, u32[]{:S(2)}) collective-permute-start(bf16[400,128]{1,0:T(8,128)(2,1)S(1)} %get-tuple-element.28), channel_id=1, source_target_pairs={{0,32},{8,40},{16,48},{24,56},{32,64},{40,72},{48,80},{56,88},{64,... | collective-permute-start | bytes 307208 | tf_op jit(solution)/shard_map/ppermute | solution.py:408
  53.1 7.5 %collective-permute-start.14 = (bf16[400,128]{1,0:T(8,128)(2,1)S(1)}, bf16[400,128]{1,0:T(8,128)(2,1)S(1)}, u32[]{:S(2)}, u32[]{:S(2)}) collective-permute-start(bf16[400,128]{1,0:T(8,128)(2,1)S(1)} %get-tuple-element.29), channel_id=1, source_target_pairs={{0,64},{8,72},{16,80},{24,88},{32,96},{40,104},{48,112},{56,120},{... | collective-permute-start | bytes 307208 | tf_op jit(solution)/shard_map/ppermute | solution.py:408
  55.4 5.8 %collective-permute-start.15 = (bf16[400,128]{1,0:T(8,128)(2,1)S(1)}, bf16[400,128]{1,0:T(8,128)(2,1)S(1)}, u32[]{:S(2)}, u32[]{:S(2)}) collective-permute-start(bf16[400,128]{1,0:T(8,128)(2,1)S(1)} %get-tuple-element.30), channel_id=1, source_target_pairs={{0,96},{8,104},{16,112},{24,120},{32,0},{40,8},{48,16},{56,24},{64... | collective-permute-start | bytes 307208 | tf_op jit(solution)/shard_map/ppermute | solution.py:408
  (4 other events, 41.1 us)

commit v4 on v3

--- a/solution.py
+++ b/solution.py
@@ -13,7 +13,7 @@
 THETA = 256.0
 EPS = 1e-06
 QUERY_SCALE = float(np.log2(np.e) * HEAD_DIM**-0.5)
-EMBED = 50
+EMBED = 52
 BF = jnp.bfloat16
 F32 = jnp.float32
 VMEM = pl.BlockSpec(memory_space=pltpu.VMEM)
@@ -116,13 +116,16 @@
     for copy in copies + staged:
         copy.start()
     kinds_copy, sec_copy, hist_copy = copies
-    own = select_rows(64, 64, lambda i: (i & 31) * 2 + (i >> 5))
+    first = (lax.axis_index("head") * 2 + lax.axis_index("fsdp")) * 8
+    own = select_rows(
+        16, 64, lambda i: ((first + (i & 7)) & 31) * 2 + ((first + (i & 7)) >> 5)
+    )
     kinds_copy.wait()
     kind = kinds_ref[lax.axis_index("frame")]
     sec_copy.wait()
     section = dot(own, sec_ref[...]).astype(BF)
     for d in range(16):
-        out_ref[d, 64:128, :] = section
+        out_ref[d, 64:80, :] = section
 
     @pl.when(kind == 0)
     def _():
@@ -140,7 +143,7 @@
 
     @pl.when(kind == 1)
     def _():
-        cols = select_columns(256, 256, lambda j: (j & 63) * 4 + (j >> 6))
+        cols = select_rows(256, 256, lambda i: (i & 63) * 4 + (i >> 6))
         lanes = select_columns(
             512,
             512,
@@ -150,7 +153,7 @@
             + (j & 3),
         )
         hist_copy.wait()
-        out = dot(dot(hist_ref[...], cols).astype(BF), lanes, ((0,), (0,))).astype(BF)
+        out = dot(dot(cols, hist_ref[...], ((1,), (1,))).astype(BF), lanes).astype(BF)
         for d in range(16):
             g, q = d // 4, d % 4
             for w in range(4):
@@ -163,8 +166,9 @@
         lanes = select_columns(
             512, 512, lambda j: ((j >> 3) & 3) * 128 + (j >> 5) * 8 + (j & 7)
         )
+        cols = select_rows(256, 256, lambda i: i)
         hist_copy.wait()
-        out = dot(hist_ref[...], lanes, ((0,), (0,))).astype(BF)
+        out = dot(dot(cols, hist_ref[...], ((1,), (1,))).astype(BF), lanes).astype(BF)
         for d in range(16):
             for g in range(4):
                 out_ref[d, 16 * g : 16 * g + 16, :] = out[
@@ -179,7 +183,7 @@
     return pl.pallas_call(
         prepare_kernel,
         out_shape=(
-            jax.ShapeDtypeStruct((16, 128, 128), BF),
+            jax.ShapeDtypeStruct((16, 80, 128), BF),
             jax.ShapeDtypeStruct(patch_fine.shape, BF),
         ),
         in_specs=[ANY] * 4,
@@ -201,20 +205,28 @@
     recv_ref,
     mid_hbm,
     coarse_hbm,
-    fine_ref,
+    fine1,
+    fine2,
+    fine3,
+    table_ref,
     out_ref,
     mid_ref,
     coarse_ref,
     mid_buf,
     coarse_buf,
     mid_sem,
-    coarse_sem,
+    coarse_sems,
 ):
-    del fine_ref
+    del fine1, fine2, fine3, table_ref
     mid_copy = pltpu.make_async_copy(mid_hbm, mid_ref, mid_sem)
-    coarse_copy = pltpu.make_async_copy(coarse_hbm, coarse_ref, coarse_sem)
     mid_copy.start()
-    coarse_copy.start()
+    coarse_copies = []
+    for g in range(4):
+        part = pl.ds(1024 * g, 1024)
+        coarse_copies.append(
+            pltpu.make_async_copy(coarse_hbm.at[part], coarse_ref.at[part], coarse_sems.at[g])
+        )
+        coarse_copies[g].start()
     mid_count = jnp.int32(0)
     coarse_count = jnp.int32(0)
     for s in range(16):
@@ -227,9 +239,18 @@
 
         @pl.when(kind == 0)
         def _(block=block):
-            blank = jnp.zeros((16, out_ref.shape[1] - 256), BF)
-            out_ref[128:144, :] = jnp.concatenate([block[0:16], block[16:32], blank], axis=1)
-
+            out_ref[128:144, 0:128] = block[0:16]
+            out_ref[128:144, 128:256] = block[16:32]
+
+    me = lax.axis_index("frame")
+    x, y = me & 3, me >> 2
+    frames = [((y + d) & 3) * 4 + x for d in range(4)] + [4 * y + i for i in range(4)]
+    upper = lax.broadcasted_iota(jnp.int32, (16, 128), 0) < 8
+    for i, (row, lane) in enumerate(((128, 256), (144, 0), (144, 128), (144, 256))):
+        first, second = (
+            recv_ref[f, 64:80, :].astype(F32) for f in (frames[2 * i], frames[2 * i + 1])
+        )
+        out_ref[row : row + 16, lane : lane + 128] = jnp.where(upper, first, second).astype(BF)
     tokens = jnp.concatenate(
         [mid_buf[0:7, 16 * w : 16 * w + 16, :].reshape(112, 128) for w in range(4)], axis=1
     )
@@ -256,8 +277,8 @@
     order = select_columns(1024, 1024, lambda j: (j & 7) * 128 + (j >> 3))
     tokens = dot(tokens, order).astype(BF)
     total = jnp.zeros((16, out_ref.shape[1]), F32)
-    coarse_copy.wait()
     for g in range(4):
+        coarse_copies[g].wait()
         total += dot(tokens[16 * g : 16 * g + 16], coarse_ref[1024 * g : 1024 * g + 1024, :])
     out_ref[112:128, :] = total.astype(BF)
 
@@ -265,59 +286,56 @@
 def embed(kinds, received, patch_mid, patch_coarse, fine):
     return pl.pallas_call(
         embed_kernel,
-        out_shape=jax.ShapeDtypeStruct((144, patch_mid.shape[1]), BF),
-        in_specs=[SMEM, VMEM, ANY, ANY, ANY],
+        out_shape=jax.ShapeDtypeStruct((160, patch_mid.shape[1]), BF),
+        in_specs=[SMEM, VMEM] + [ANY] * 6,
         out_specs=VMEM,
         scratch_shapes=[
             pltpu.VMEM(patch_mid.shape, BF),
             pltpu.VMEM(patch_coarse.shape, BF),
             pltpu.VMEM((8, 64, 128), BF),
             pltpu.VMEM((9, 64, 128), BF),
-        ]
-        + [pltpu.SemaphoreType.DMA] * 2,
+            pltpu.SemaphoreType.DMA,
+            pltpu.SemaphoreType.DMA((4,)),
+        ],
         compiler_params=params(EMBED),
-        cost_estimate=cost(1e6, 1e4),
+        cost_estimate=cost(2e9, 5e6),
         name="embed",
-    )(kinds, received, patch_mid, patch_coarse, fine)
-
-
-def stack_kernel(*refs):
-    for d, ref in enumerate(refs[:-1]):
-        refs[-1][d] = ref[...]
-
-
-def stack(blocks, estimate):
+    )(kinds, received, patch_mid, patch_coarse, *fine)
+
+
+def along_head(block):
+    ring1, ring3, ring2 = (
+        lax.ppermute(block, "head", [(i, (i + d) % 4) for i in range(4)]) for d in (1, 3, 2)
+    )
+    return block, ring1, ring2, ring3
+
+
+def other_core(block):
+    return lax.ppermute(block, "fsdp", [(0, 1), (1, 0)])
+
+
+def stack_kernel(ref0, ref1, ref2, ref3, after_ref, out_ref):
+    del after_ref
+    for d, ref in enumerate((ref0, ref1, ref2, ref3)):
+        out_ref[d] = ref[...]
+
+
+def stack(blocks, after):
     return pl.pallas_call(
         stack_kernel,
-        out_shape=jax.ShapeDtypeStruct((len(blocks), *blocks[0].shape), BF),
-        in_specs=[VMEM] * len(blocks),
+        out_shape=jax.ShapeDtypeStruct((4, *blocks[0].shape), BF),
+        in_specs=[VMEM] * 4 + [ANY],
         out_specs=VMEM,
         compiler_params=params(),
-        cost_estimate=estimate,
+        cost_estimate=cost(2e10, 1e6),
         name="stack",
-    )(*blocks)
-
-
-def gather_columns(block, estimate):
-    ring1, ring3, ring2 = (
-        lax.ppermute(block, "head", [(i, (i + d) % 4) for i in range(4)]) for d in (1, 3, 2)
-    )
-    swap = [(0, 1), (1, 0)]
-    twin = lax.ppermute(block, "fsdp", swap)
-    same = stack((ring3, ring2, ring1), estimate)
-    return block, twin, same, lax.ppermute(same, "fsdp", swap)
-
-
-def pairs(own_ref, twin_ref, same_ref, other_ref):
-    yield 0, own_ref, twin_ref
-    for d in range(3):
-        yield 3 - d, same_ref.at[d], other_ref.at[d]
+    )(*blocks, after)
 
 
 def place_columns(gathered, full_ref):
     z, core = lax.axis_index("head"), lax.axis_index("fsdp")
     rows = full_ref.shape[0]
-    for d, mine, theirs in pairs(*gathered):
+    for d, (mine, theirs) in enumerate(zip(*gathered)):
         at = ((z + 4 - d) & 3) * 2
         width = mine.shape[1]
         for ref, column in ((mine, at + core), (theirs, at + 1 - core)):
@@ -325,20 +343,18 @@
 
 
 def fold_kernel(
-    own_ref,
-    twin_ref,
     same_ref,
     other_ref,
     mod_ref,
     w_ref,
     perm_ref,
-    far_ref,
+    after_ref,
     fold_ref,
     gram_ref,
     full_ref,
 ):
-    del far_ref
-    place_columns((own_ref, twin_ref, same_ref, other_ref), full_ref)
+    del after_ref
+    place_columns([[ref.at[d] for d in range(4)] for ref in (same_ref, other_ref)], full_ref)
     order = select_rows(64, 64, lambda i: (i & 31) * 2 + (i >> 5))
     raw = full_ref[...]
     width = raw.shape[1]
@@ -383,7 +399,7 @@
         fold_ref[part] = rows
 
 
-def fold(gathered, modulation, w_qkv, perm, far):
+def fold(same, other, modulation, w_qkv, perm, after):
     width, columns = w_qkv.shape[1], w_qkv.shape[2]
     return pl.pallas_call(
         fold_kernel,
@@ -391,13 +407,13 @@
             jax.ShapeDtypeStruct((3, 144, columns), BF),
             jax.ShapeDtypeStruct((64, 64), F32),
         ),
-        in_specs=[VMEM] * 7 + [ANY],
+        in_specs=[VMEM] * 5 + [ANY],
         out_specs=(VMEM, VMEM),
         scratch_shapes=[pltpu.VMEM((64, width), BF)],
         compiler_params=params(),
         cost_estimate=cost(1e6, 1e4),
         name="fold",
-    )(*gathered, modulation, w_qkv, perm, far)
+    )(same, other, modulation, w_qkv, perm, after)
 
 
 def along_x(value, d):
@@ -437,11 +453,14 @@
 
 def token_kernel(
     kinds_ref,
-    recv_ref,
-    own_ref,
-    twin_ref,
-    same_ref,
-    other_ref,
+    mine0,
+    mine1,
+    mine2,
+    mine3,
+    theirs0,
+    theirs1,
+    theirs2,
+    theirs3,
     fold_ref,
     gram_ref,
     cos_ref,
@@ -451,6 +470,7 @@
     key_ref,
     value_ref,
     fine_buf,
+    sec_buf,
 ):
     me = lax.axis_index("frame")
     x, y = me & 3, me >> 2
@@ -461,25 +481,31 @@
         return ref[:, pl.ds(pl.multiple_of(f * 128, 128), 128)]
 
     z, core = lax.axis_index("head"), lax.axis_index("fsdp")
-    for d, mine, theirs in pairs(own_ref, twin_ref, same_ref, other_ref):
+    mine_refs, theirs_refs = (mine0, mine1, mine2, mine3), (theirs0, theirs1, theirs2, theirs3)
+    for d, (mine_ref, theirs_ref) in enumerate(zip(mine_refs, theirs_refs)):
+        at = (z + 4 - d) & 3
+        for i, (row, lane) in enumerate(((128, 256), (144, 0), (144, 128), (144, 256))):
+            mine, theirs = (
+                ref[row : row + 16, lane : lane + 128].astype(F32) for ref in (mine_ref, theirs_ref)
+            )
+            first, second = jnp.where(core == 0, mine, theirs), jnp.where(core == 0, theirs, mine)
+            for k, part in enumerate((slice(0, 8), slice(8, 16))):
+                sec_buf[
+                    pl.ds(pl.multiple_of(16 * at, 16), 16), 128 * (2 * i + k) : 128 * (2 * i + k + 1)
+                ] = jnp.concatenate([first[part], second[part]], axis=0).astype(BF)
         mine, theirs = (
             jnp.concatenate([ref[128:144, 0:128], ref[128:144, 128:256]], axis=0).astype(F32)
-            for ref in (mine, theirs)
+            for ref in (mine_ref, theirs_ref)
         )
         first, second = jnp.where(core == 0, mine, theirs), jnp.where(core == 0, theirs, mine)
-        fine_buf[:, pl.ds(pl.multiple_of(((z + 4 - d) & 3) * 128, 128), 128)] = jnp.concatenate(
+        fine_buf[:, pl.ds(pl.multiple_of(at * 128, 128), 128)] = jnp.concatenate(
             [
                 jnp.concatenate([first[:, 0:64], second[:, 0:64]], axis=1),
                 jnp.concatenate([first[:, 64:128], second[:, 64:128]], axis=1),
             ],
             axis=0,
         ).astype(BF)
-    patches = jnp.concatenate(
-        [recv_ref[f, 64:128, :] for f in columns]
-        + [recv_ref[4 * y + i, 64:128, :] for i in range(4)]
-        + [fine_buf[...]],
-        axis=1,
-    )
+    patches = jnp.concatenate([sec_buf[...], fine_buf[...]], axis=1)
     variance = spread_of(patches, gram_ref[...])
     inverse = lax.rsqrt(variance)
     patches = extended(patches, variance)
@@ -505,7 +531,7 @@
         value_ref[at, :] = (raw * inverse[:, 512:]).astype(BF)
 
 
-def make_tokens(kinds, received, gathered, folded, gram, cosine, sine, times):
+def make_tokens(kinds, gathered, folded, gram, cosine, sine, times):
     columns = folded.shape[2]
     return pl.pallas_call(
         token_kernel,
@@ -514,13 +540,13 @@
             jax.ShapeDtypeStruct((columns, 1024), BF),
             jax.ShapeDtypeStruct((columns, 1024), BF),
         ),
-        in_specs=[SMEM] + [VMEM] * 10,
+        in_specs=[SMEM] + [VMEM] * 13,
         out_specs=tuple([VMEM] * 3),
-        scratch_shapes=[pltpu.VMEM((64, 512), BF)],
+        scratch_shapes=[pltpu.VMEM((64, 512), BF), pltpu.VMEM((64, 1024), BF)],
         compiler_params=params(),
         cost_estimate=cost(2e9, 8e6),
         name="tokens",
-    )(kinds, received, *gathered, folded, gram, cosine, sine, times)
+    )(kinds, *gathered[0], *gathered[1], folded, gram, cosine, sine, times)
 
 
 def near_kernel(query_ref, key_ref, value_ref, num_ref, den_ref):
@@ -580,20 +606,40 @@
     return jnp.cos(angles), jnp.sin(angles) * sign
 
 
+def table_kernel(kinds_ref, freq_ref, after_ref, table_ref):
+    del after_ref
+    table_ref[0], table_ref[1] = row_angles(kinds_ref, freq_ref)
+
+
+def make_table(kinds, freqs, after):
+    return pl.pallas_call(
+        table_kernel,
+        out_shape=jax.ShapeDtypeStruct((2, 128, HEAD_DIM), F32),
+        in_specs=[SMEM, VMEM, ANY],
+        out_specs=VMEM,
+        compiler_params=params(),
+        cost_estimate=cost(1e5, 1e3),
+        name="table",
+    )(kinds, freqs, after)
+
+
 def far_kernel(
-    kinds_ref,
-    own_ref,
-    twin_ref,
-    same_ref,
-    other_ref,
+    mine0,
+    mine1,
+    mine2,
+    mine3,
+    theirs0,
+    theirs1,
+    theirs2,
+    theirs3,
     mod_ref,
     w_ref,
     perm_ref,
-    freq_ref,
+    table_ref,
     out_ref,
     full_ref,
 ):
-    place_columns((own_ref, twin_ref, same_ref, other_ref), full_ref)
+    place_columns(((mine0, mine1, mine2, mine3), (theirs0, theirs1, theirs2, theirs3)), full_ref)
     heads = out_ref.shape[2] // HEAD_DIM
     x = full_ref[...].astype(F32)
     x = x - jnp.mean(x, axis=1, keepdims=True)
@@ -601,7 +647,7 @@
     x = (x * (1.0 + mod_ref[1:2, :]) + mod_ref[0:1, :]).astype(BF)
     raw_keys = dot(x, w_ref[1])
     out_ref[1] = dot(x, w_ref[2]).astype(BF)
-    cosine, sine = row_angles(kinds_ref, freq_ref)
+    cosine, sine = table_ref[0], table_ref[1]
     for h in range(heads):
         at = slice(HEAD_DIM * h, HEAD_DIM * (h + 1))
         raw = raw_keys[:, at]
@@ -611,18 +657,18 @@
         out_ref[0, :, at] = (raw * cosine + pltpu.roll(raw, 64, 1) * sine).astype(BF)
 
 
-def make_far(kinds, gathered, modulation, w_qkv, perm, freqs):
+def make_far(gathered, modulation, w_qkv, perm, table):
     columns = w_qkv.shape[2]
     return pl.pallas_call(
         far_kernel,
         out_shape=jax.ShapeDtypeStruct((2, 128, columns), BF),
-        in_specs=[SMEM] + [VMEM] * 8,
+        in_specs=[VMEM] * 12,
         out_specs=VMEM,
         scratch_shapes=[pltpu.VMEM((128, w_qkv.shape[1]), BF)],
         compiler_params=params(),
         cost_estimate=cost(2e9, 1e7),
         name="far",
-    )(kinds, *gathered, modulation, w_qkv, perm, freqs)
+    )(*gathered[0], *gathered[1], modulation, w_qkv, perm, table)
 
 
 def history_kernel(far0, far1, far3, far2, query_ref, num_ref, den_ref, out0, out1, out2, out3):
@@ -696,14 +742,17 @@
 
     sent, patch_fine = prepare(slab_kernel, history, section, patch_fine)
     received = lax.all_to_all(sent, "frame", 0, 0, tiled=True)
-    fine = gather_columns(patch_fine, cost(1e6, 1e5))
-    features = embed(slab_kernel, received, patch_mid, patch_coarse, fine[2])
-    gathered = gather_columns(features, cost(2e10, 1e6))
-    far = make_far(slab_kernel, gathered, modulation, w_qkv, perm, freqs)
+    fine = along_head(patch_fine)
+    table = make_table(slab_kernel, freqs, sent)
+    features = embed(slab_kernel, received, patch_mid, patch_coarse, (*fine[1:], table))
+    mine = along_head(features)
+    gathered = mine, tuple(other_core(block) for block in mine)
+    far = make_far(gathered, modulation, w_qkv, perm, table)
     far2, far1, far3 = (along_x(far, d) for d in (2, 1, 3))
-    folded, gram = fold(fine, modulation, w_qkv, perm, far)
+    fine_same = stack(fine, features)
+    folded, gram = fold(fine_same, other_core(fine_same), modulation, w_qkv, perm, far)
     queries, keys, values = make_tokens(
-        slab_kernel, received, gathered, folded, gram, cosine, sine, times
+        slab_kernel, gathered, folded, gram, cosine, sine, times
     )
     numerator, denominator = attend_near(queries, keys, values)
     fars = [far, far2, far3, far1]

time: 62.1 us -> 59.2 us (0.953)
  waiting for transfers between devices: 17.4 us -> 12.7 us
  starting transfers between devices: 28.2 us -> 29.4 us
  local copies, waits for them, and re-layouts: 0.07 us -> 1.04 us
    ppermute x10 -> x11, waiting for transfers between devices: 7.81 us -> 5.85 us  [the longest x6 5.16 us: along_head(): lax.ppermute(block, 'head', [(i, (i + d) % 4) for i in range(4)])]
    all_to_all x1, waiting for transfers between devices: 1.65 us -> 0.01 us  [per_device(): received = lax.all_to_all(sent, 'frame', 0, 0, tiled=True)]
    ppermute x3, starting transfers between devices: 3.53 us -> 4.77 us  [along_y(): lax.ppermute(value, 'frame', [(i, (i + 4 * d) % 16) for i in range(16)])]
    ppermute x10 -> x11, starting transfers between devices: 14.2 us -> 13.3 us  [the longest x6 12.7 us: along_head(): lax.ppermute(block, 'head', [(i, (i + d) % 4) for i in range(4)])]
    unnamed x22 -> x24, local copies, waits for them, and re-layouts: 0.07 us -> 1.04 us
    pallas_call x1, Pallas kernels: 2.41 us -> 1.56 us  [make_far(): pl.pallas_call(far_kernel, out_shape=jax.ShapeDtypeStruct((2, 128, column...]
    ppermute x3, starting transfers between devices: 3.31 us -> 4.14 us  [along_x(): lax.ppermute(value, 'frame', [(i, i // 4 * 4 + (i + d) % 4) for i in rang...]
    ppermute x3, waiting for transfers between devices: 4.64 us -> 4.01 us  [along_y(): lax.ppermute(value, 'frame', [(i, (i + 4 * d) % 16) for i in range(16)])]
  transfers between devices with their start and end apart: 17 -> 18, of which waited for: 10 -> 10; matrix products, arithmetic and copies ran while one was open for 0% -> 0% of each run, Pallas kernels for 13% -> 14%
where the time goes in v4:
time: 59.2 us; the launch traced here: 58.9 us
  starting transfers between devices  29.4 us (50%)
  Pallas kernels  15.6 us (26%)
  waiting for transfers between devices  12.7 us (21%)
  local copies, waits for them, and re-layouts  1.04 us (2%)
    ppermute x6, starting transfers between devices, along_head(): lax.ppermute(block, 'head', [(i, (i + d) % 4) for i in range(4)])  12.7 us
    all_to_all x1, starting transfers between devices, per_device(): received = lax.all_to_all(sent, 'frame', 0, 0, tiled=True)  7.27 us
    ppermute x6, waiting for transfers between devices, along_head(): lax.ppermute(block, 'head', [(i, (i + d) % 4) for i in range(4)])  5.16 us
    ppermute x3, starting transfers between devices, along_y(): lax.ppermute(value, 'frame', [(i, (i + 4 * d) % 16) for i in range(16)])  4.77 us
    ppermute x3, starting transfers between devices, along_x(): lax.ppermute(value, 'frame', [(i, i // 4 * 4 + (i + d) % 4) for i in rang...  4.14 us
    ppermute x3, waiting for transfers between devices, along_y(): lax.ppermute(value, 'frame', [(i, (i + 4 * d) % 16) for i in range(16)])  4.01 us
    pallas_call x1, Pallas kernels, embed(): pl.pallas_call(embed_kernel, out_shape=jax.ShapeDtypeStruct((160, patch_m...  3 us
    ppermute x3, waiting for transfers between devices, along_x(): lax.ppermute(value, 'frame', [(i, i // 4 * 4 + (i + d) % 4) for i in rang...  2.79 us
  transfers between devices with their start and end apart: 18, of which 10 were waited for; matrix products, arithmetic and copies ran while one was open for 0% of the time, Pallas kernels for 14%

profile of v4, /device:TPU:0, one launch (start us, length us, event | category | flops | bytes accessed | tf_op | source)
XLA Modules:
  0.0 58.9 jit_solution(12704519719518446872)
XLA Ops:
  0.0 2.3 %prepare.1 = (bf16[16,80,128]{2,1,0:T(8,128)(2,1)}, bf16[64,384]{1,0:T(8,128)(2,1)}) custom-call(s32[16]{0:T(128)} %kinds_ref.5, bf16[512,256]{1,0:T(8,128)(2,1)} %bitcast.4, bf16[64,128]{1,0:T(8,128)(2,1)} %bitcast.5, bf16[64,384]{1,0:T(8,128)(2,1)} %fine_hbm.1), custom_call_target="tpu_custom_call" | custom-call | flops 20000000000 | bytes 1000000 | tf_op jit(solution)/shard_map/prepare/pallas_call | solution.py:183
  2.4 7.3 %all-to-all-start = ((bf16[16,80,128]{2,1,0:T(8,128)(2,1)}), bf16[16,80,128]{2,1,0:T(8,128)(2,1)S(1)}, u32[]{:S(2)}, u32[]{:S(2)}) async-start(bf16[16,80,128]{2,1,0:T(8,128)(2,1)} %get-tuple-element.18.after_ref), calls=%async_computation | async-start | bytes 655360 | tf_op jit(solution)/shard_map/all_to_all | solution.py:744
  9.6 2.0 %collective-permute-start = (bf16[64,384]{1,0:T(8,128)(2,1)}, bf16[64,384]{1,0:T(8,128)(2,1)S(1)}, u32[]{:S(2)}, u32[]{:S(2)}) collective-permute-start(bf16[64,384]{1,0:T(8,128)(2,1)} %get-tuple-element.19.ref0), channel_id=1, source_target_pairs={{0,2},{2,4},{4,6},{6,0},{1,3},{3,5},{5,7},{7,1},{8,10},{10,12},{12... | collective-permute-start | bytes 147464 | tf_op jit(solution)/shard_map/ppermute | solution.py:308
  11.6 3.6 %collective-permute-start.1 = (bf16[64,384]{1,0:T(8,128)(2,1)}, bf16[64,384]{1,0:T(8,128)(2,1)S(1)}, u32[]{:S(2)}, u32[]{:S(2)}) collective-permute-start(bf16[64,384]{1,0:T(8,128)(2,1)} %get-tuple-element.19.ref0), channel_id=1, source_target_pairs={{0,4},{2,6},{4,0},{6,2},{1,5},{3,7},{5,1},{7,3},{8,12},{10,14},{12... | collective-permute-start | bytes 147464 | tf_op jit(solution)/shard_map/ppermute | solution.py:308
  15.2 1.0 %collective-permute-start.2 = (bf16[64,384]{1,0:T(8,128)(2,1)}, bf16[64,384]{1,0:T(8,128)(2,1)S(1)}, u32[]{:S(2)}, u32[]{:S(2)}) collective-permute-start(bf16[64,384]{1,0:T(8,128)(2,1)} %get-tuple-element.19.ref0), channel_id=1, source_target_pairs={{0,6},{2,0},{4,2},{6,4},{1,7},{3,1},{5,3},{7,5},{8,14},{10,8},{12,... | collective-permute-start | bytes 147464 | tf_op jit(solution)/shard_map/ppermute | solution.py:308
  17.2 1.0 %table.1.table_ref = f32[2,128,128]{2,1,0:T(8,128)S(1)} custom-call(s32[16]{0:T(128)S(1)} %copy-done.4, f32[8,128]{1,0:T(8,128)S(1)} %copy-done.3, bf16[16,80,128]{2,1,0:T(8,128)(2,1)S(1)} %copy-done), custom_call_target="tpu_custom_call" | custom-call | flops 100000 | bytes 1000 | tf_op jit(solution)/shard_map/table/pallas_call | solution.py:615
  18.2 1.3 %collective-permute-done.2.fine3.ref3 = bf16[64,384]{1,0:T(8,128)(2,1)S(1)} collective-permute-done((bf16[64,384]{1,0:T(8,128)(2,1)}, bf16[64,384]{1,0:T(8,128)(2,1)S(1)}, u32[]{:S(2)}, u32[]{:S(2)}) %collective-permute-start.2) | collective-permute-done | bytes 49184 | tf_op jit(solution)/shard_map/ppermute | solution.py:308
  19.5 3.0 %embed.1.mine0.after_ref = bf16[160,384]{1,0:T(8,128)(2,1)S(1)} custom-call(s32[16]{0:T(128)S(1)} %copy-done.4, bf16[16,80,128]{2,1,0:T(8,128)(2,1)S(1)} %all-to-all-done.recv_ref, bf16[512,384]{1,0:T(8,128)(2,1)S(1)} %copy-done.5, bf16[4096,384]{1,0:T(8,128)(2,1)} %coarse_hbm.1, bf16[64,384]{1,0:T(8,128)(2,1)S(1)} %collective-permute-done.fine1.ref1, ...), custom_call_target="tpu_custom_call" | custom-call | flops 2000000000 | bytes 5000000 | tf_op jit(solution)/shard_map/embed/pallas_call | solution.py:287
  22.6 1.5 %collective-permute-start.3 = (bf16[160,384]{1,0:T(8,128)(2,1)S(1)}, bf16[160,384]{1,0:T(8,128)(2,1)S(1)}, u32[]{:S(2)}, u32[]{:S(2)}) collective-permute-start(bf16[160,384]{1,0:T(8,128)(2,1)S(1)} %embed.1.mine0.after_ref), channel_id=1, source_target_pairs={{0,2},{2,4},{4,6},{6,0},{1,3},{3,5},{5,7},{7,1},{8,10},{10,12},{12... | collective-permute-start | bytes 368648 | tf_op jit(solution)/shard_map/ppermute | solution.py:308
  24.1 3.6 %collective-permute-start.4 = (bf16[160,384]{1,0:T(8,128)(2,1)S(1)}, bf16[160,384]{1,0:T(8,128)(2,1)S(1)}, u32[]{:S(2)}, u32[]{:S(2)}) collective-permute-start(bf16[160,384]{1,0:T(8,128)(2,1)S(1)} %embed.1.mine0.after_ref), channel_id=1, source_target_pairs={{0,4},{2,6},{4,0},{6,2},{1,5},{3,7},{5,1},{7,3},{8,12},{10,14},{12... | collective-permute-start | bytes 368648 | tf_op jit(solution)/shard_map/ppermute | solution.py:308
  27.6 1.0 %collective-permute-start.5 = (bf16[160,384]{1,0:T(8,128)(2,1)S(1)}, bf16[160,384]{1,0:T(8,128)(2,1)S(1)}, u32[]{:S(2)}, u32[]{:S(2)}) collective-permute-start(bf16[160,384]{1,0:T(8,128)(2,1)S(1)} %embed.1.mine0.after_ref), channel_id=1, source_target_pairs={{0,6},{2,0},{4,2},{6,4},{1,7},{3,1},{5,3},{7,5},{8,14},{10,8},{12,... | collective-permute-start | bytes 368648 | tf_op jit(solution)/shard_map/ppermute | solution.py:308
  28.7 1.7 %collective-permute-done.3.mine1 = bf16[160,384]{1,0:T(8,128)(2,1)S(1)} collective-permute-done((bf16[160,384]{1,0:T(8,128)(2,1)S(1)}, bf16[160,384]{1,0:T(8,128)(2,1)S(1)}, u32[]{:S(2)}, u32[]{:S(2)}) %collective-permute-start.3) | collective-permute-done | bytes 122912 | tf_op jit(solution)/shard_map/ppermute | solution.py:308
  30.4 1.8 %collective-permute-done.4.mine2 = bf16[160,384]{1,0:T(8,128)(2,1)S(1)} collective-permute-done((bf16[160,384]{1,0:T(8,128)(2,1)S(1)}, bf16[160,384]{1,0:T(8,128)(2,1)S(1)}, u32[]{:S(2)}, u32[]{:S(2)}) %collective-permute-start.4) | collective-permute-done | bytes 122912 | tf_op jit(solution)/shard_map/ppermute | solution.py:308
  33.9 1.6 %far.1.after_ref.far0 = bf16[2,128,384]{2,1,0:T(8,128)(2,1)S(1)} custom-call(bf16[160,384]{1,0:T(8,128)(2,1)S(1)} %embed.1.mine0.after_ref, bf16[160,384]{1,0:T(8,128)(2,1)S(1)} %collective-permute-done.3.mine1, bf16[160,384]{1,0:T(8,128)(2,1)S(1)} %collective-permute-done.4.mine2, bf16[160,384]{1,0:T(8,128)(2,1)S(1)} %collective-permute-done.5.mine3, ...), custom_call_target="tpu_custom_call" | custom-call | flops 2000000000 | bytes 10000000 | tf_op jit(solution)/shard_map/far/pallas_call | solution.py:662
  35.5 2.1 %collective-permute-start.10 = (bf16[2,128,384]{2,1,0:T(8,128)(2,1)S(1)}, bf16[2,128,384]{2,1,0:T(8,128)(2,1)S(1)}, u32[]{:S(2)}, u32[]{:S(2)}) collective-permute-start(bf16[2,128,384]{2,1,0:T(8,128)(2,1)S(1)} %far.1.after_ref.far0), channel_id=1, source_target_pairs={{0,16},{8,24},{16,0},{24,8},{32,48},{40,56},{48,32},{56,40},{64,80... | collective-permute-start | bytes 589832 | tf_op jit(solution)/shard_map/ppermute | solution.py:420
  37.6 1.2 %collective-permute-start.11 = (bf16[2,128,384]{2,1,0:T(8,128)(2,1)S(1)}, bf16[2,128,384]{2,1,0:T(8,128)(2,1)S(1)}, u32[]{:S(2)}, u32[]{:S(2)}) collective-permute-start(bf16[2,128,384]{2,1,0:T(8,128)(2,1)S(1)} %far.1.after_ref.far0), channel_id=1, source_target_pairs={{0,24},{8,0},{16,8},{24,16},{32,56},{40,32},{48,40},{56,48},{64,88... | collective-permute-start | bytes 589832 | tf_op jit(solution)/shard_map/ppermute | solution.py:420
  39.6 2.3 %fold.1 = (bf16[3,144,384]{2,1,0:T(8,128)(2,1)S(1)}, f32[64,64]{1,0:T(8,128)S(1)}) custom-call(bf16[4,64,384]{2,1,0:T(8,128)(2,1)S(1)} %stack.1.same_ref, bf16[4,64,384]{2,1,0:T(8,128)(2,1)S(1)} %collective-permute-done.13.other_ref, f32[2,3072]{1,0:T(2,128)S(1)} %copy-done.2, bf16[3,3072,384]{2,1,0:T(8,128)(2,1)S(1)} %bitcast.3, ...), custom_call_target="tpu_custom_call" | custom-call | flops 1000000 | bytes 10000 | tf_op jit(solution)/shard_map/fold/pallas_call | solution.py:404
  42.0 1.9 %tokens.1 = (bf16[384,512]{1,0:T(8,128)(2,1)S(1)}, bf16[384,1024]{1,0:T(8,128)(2,1)S(1)}, bf16[384,1024]{1,0:T(8,128)(2,1)S(1)}) custom-call(s32[16]{0:T(128)S(1)} %copy-done.4, bf16[160,384]{1,0:T(8,128)(2,1)S(1)} %embed.1.mine0.after_ref, bf16[160,384]{1,0:T(8,128)(2,1)S(1)} %collective-permute-done.3.mine1, ...), custom_call_target="tpu_custom_call" | custom-call | flops 2000000000 | bytes 8000000 | tf_op jit(solution)/shard_map/tokens/pallas_call | solution.py:536
  43.9 1.5 %near.1 = (f32[384,512]{1,0:T(8,128)S(1)}, f32[8,512]{1,0:T(8,128)S(1)}) custom-call(bf16[384,512]{1,0:T(8,128)(2,1)S(1)} %get-tuple-element.22.query_ref, bf16[384,1024]{1,0:T(8,128)(2,1)S(1)} %get-tuple-element.23.key_ref, bf16[384,1024]{1,0:T(8,128)(2,1)S(1)} %get-tuple-element.24.value_ref), custom_call_target="tpu_custom_call" | custom-call | flops 4000000000 | bytes 10000000 | tf_op jit(solution)/shard_map/near/pallas_call | solution.py:563
  45.4 1.9 %collective-permute-done.11.far3 = bf16[2,128,384]{2,1,0:T(8,128)(2,1)S(1)} collective-permute-done((bf16[2,128,384]{2,1,0:T(8,128)(2,1)S(1)}, bf16[2,128,384]{2,1,0:T(8,128)(2,1)S(1)}, u32[]{:S(2)}, u32[]{:S(2)}) %collective-permute-start.11) | collective-permute-done | bytes 196640 | tf_op jit(solution)/shard_map/ppermute | solution.py:420
  48.2 1.1 %history.1 = (f32[400,128]{1,0:T(8,128)S(1)}, bf16[400,128]{1,0:T(8,128)(2,1)S(1)}, bf16[400,128]{1,0:T(8,128)(2,1)S(1)}, bf16[400,128]{1,0:T(8,128)(2,1)S(1)}) custom-call(bf16[2,128,384]{2,1,0:T(8,128)(2,1)S(1)} %far.1.after_ref.far0, bf16[2,128,384]{2,1,0:T(8,128)(2,1)S(1)} %collective-permute-done.10.far1, ...), custom_call_target="tpu_custom_call" | custom-call | flops 2000000000 | bytes 4000000 | tf_op jit(solution)/shard_map/history/pallas_call | solution.py:698
  50.0 2.7 %collective-permute-start.15 = (bf16[400,128]{1,0:T(8,128)(2,1)S(1)}, bf16[400,128]{1,0:T(8,128)(2,1)S(1)}, u32[]{:S(2)}, u32[]{:S(2)}) collective-permute-start(bf16[400,128]{1,0:T(8,128)(2,1)S(1)} %get-tuple-element.29), channel_id=1, source_target_pairs={{0,64},{8,72},{16,80},{24,88},{32,96},{40,104},{48,112},{56,120},{... | collective-permute-start | bytes 307208 | tf_op jit(solution)/shard_map/ppermute | solution.py:424
  52.7 1.5 %collective-permute-start.16 = (bf16[400,128]{1,0:T(8,128)(2,1)S(1)}, bf16[400,128]{1,0:T(8,128)(2,1)S(1)}, u32[]{:S(2)}, u32[]{:S(2)}) collective-permute-start(bf16[400,128]{1,0:T(8,128)(2,1)S(1)} %get-tuple-element.30), channel_id=1, source_target_pairs={{0,96},{8,104},{16,112},{24,120},{32,0},{40,8},{48,16},{56,24},{64... | collective-permute-start | bytes 307208 | tf_op jit(solution)/shard_map/ppermute | solution.py:424
  54.1 3.4 %collective-permute-done.14.part1 = bf16[400,128]{1,0:T(8,128)(2,1)S(1)} collective-permute-done((bf16[400,128]{1,0:T(8,128)(2,1)S(1)}, bf16[400,128]{1,0:T(8,128)(2,1)S(1)}, u32[]{:S(2)}, u32[]{:S(2)}) %collective-permute-start.14) | collective-permute-done | bytes 102432 | tf_op jit(solution)/shard_map/ppermute | solution.py:424
  (47 shorter events, 6.4 us)
Async XLA Ops:
  0.0 16.2 %copy-start.3 = (f32[8,128]{1,0:T(8,128)S(1)}, f32[8,128]{1,0:T(8,128)}, u32[]{:S(2)}) copy-start(f32[8,128]{1,0:T(8,128)} %constant.13.clone.freq_ref) | copy-start | bytes 12292
  0.0 16.2 %copy-start.4 = (s32[16]{0:T(128)S(1)}, s32[16]{0:T(128)}, u32[]{:S(2)}) copy-start(s32[16]{0:T(128)} %kinds_ref.5) | copy-start | bytes 196
  0.0 19.5 %copy-start.5 = (bf16[512,384]{1,0:T(8,128)(2,1)S(1)}, bf16[512,384]{1,0:T(8,128)(2,1)}, u32[]{:S(2)}) copy-start(bf16[512,384]{1,0:T(8,128)(2,1)} %mid_hbm.1) | copy-start | bytes 1179652
  2.4 30.3 %copy-start.6 = (bf16[64,384]{1,0:T(8,128)(2,1)S(1)}, bf16[64,384]{1,0:T(8,128)(2,1)}, u32[]{:S(2)}) copy-start(bf16[64,384]{1,0:T(8,128)(2,1)} %get-tuple-element.19.ref0) | copy-start | bytes 147460
  2.4 17.1 %all-to-all-start = ((bf16[16,80,128]{2,1,0:T(8,128)(2,1)}), bf16[16,80,128]{2,1,0:T(8,128)(2,1)S(1)}, u32[]{:S(2)}, u32[]{:S(2)}) async-start(bf16[16,80,128]{2,1,0:T(8,128)(2,1)} %get-tuple-element.18.after_ref), calls=%async_computation | async-start | bytes 655360 | tf_op jit(solution)/shard_map/all_to_all | solution.py:744
  9.6 8.6 %collective-permute-start = (bf16[64,384]{1,0:T(8,128)(2,1)}, bf16[64,384]{1,0:T(8,128)(2,1)S(1)}, u32[]{:S(2)}, u32[]{:S(2)}) collective-permute-start(bf16[64,384]{1,0:T(8,128)(2,1)} %get-tuple-element.19.ref0), channel_id=1, source_target_pairs={{0,2},{2,4},{4,6},{6,0},{1,3},{3,5},{5,7},{7,1},{8,10},{10,12},{12... | collective-permute-start | bytes 147464 | tf_op jit(solution)/shard_map/ppermute | solution.py:308
  11.6 6.6 %collective-permute-start.1 = (bf16[64,384]{1,0:T(8,128)(2,1)}, bf16[64,384]{1,0:T(8,128)(2,1)S(1)}, u32[]{:S(2)}, u32[]{:S(2)}) collective-permute-start(bf16[64,384]{1,0:T(8,128)(2,1)} %get-tuple-element.19.ref0), channel_id=1, source_target_pairs={{0,4},{2,6},{4,0},{6,2},{1,5},{3,7},{5,1},{7,3},{8,12},{10,14},{12... | collective-permute-start | bytes 147464 | tf_op jit(solution)/shard_map/ppermute | solution.py:308
  15.2 4.3 %collective-permute-start.2 = (bf16[64,384]{1,0:T(8,128)(2,1)}, bf16[64,384]{1,0:T(8,128)(2,1)S(1)}, u32[]{:S(2)}, u32[]{:S(2)}) collective-permute-start(bf16[64,384]{1,0:T(8,128)(2,1)} %get-tuple-element.19.ref0), channel_id=1, source_target_pairs={{0,6},{2,0},{4,2},{6,4},{1,7},{3,1},{5,3},{7,5},{8,14},{10,8},{12,... | collective-permute-start | bytes 147464 | tf_op jit(solution)/shard_map/ppermute | solution.py:308
  19.5 14.4 %slice-start = ((s8[7077888]{0:T(1024)(128)(4,1)}), s8[2883584]{0:T(1024)(128)(4,1)S(1)}, s32[]{:S(2)}) async-start(s8[7077888]{0:T(1024)(128)(4,1)} %bitcast.2), calls=%async_computation.1 | async-start | bytes 5767168
  22.5 11.3 %slice-start.1 = ((s8[7077888]{0:T(1024)(128)(4,1)}), s8[4194304]{0:T(1024)(128)(4,1)S(1)}, s32[]{:S(2)}) async-start(s8[7077888]{0:T(1024)(128)(4,1)} %bitcast.2), calls=%async_computation.2 | async-start | bytes 8388608
  22.6 7.8 %collective-permute-start.3 = (bf16[160,384]{1,0:T(8,128)(2,1)S(1)}, bf16[160,384]{1,0:T(8,128)(2,1)S(1)}, u32[]{:S(2)}, u32[]{:S(2)}) collective-permute-start(bf16[160,384]{1,0:T(8,128)(2,1)S(1)} %embed.1.mine0.after_ref), channel_id=1, source_target_pairs={{0,2},{2,4},{4,6},{6,0},{1,3},{3,5},{5,7},{7,1},{8,10},{10,12},{12... | collective-permute-start | bytes 368648 | tf_op jit(solution)/shard_map/ppermute | solution.py:308
  24.1 8.1 %collective-permute-start.4 = (bf16[160,384]{1,0:T(8,128)(2,1)S(1)}, bf16[160,384]{1,0:T(8,128)(2,1)S(1)}, u32[]{:S(2)}, u32[]{:S(2)}) collective-permute-start(bf16[160,384]{1,0:T(8,128)(2,1)S(1)} %embed.1.mine0.after_ref), channel_id=1, source_target_pairs={{0,4},{2,6},{4,0},{6,2},{1,5},{3,7},{5,1},{7,3},{8,12},{10,14},{12... | collective-permute-start | bytes 368648 | tf_op jit(solution)/shard_map/ppermute | solution.py:308
  27.6 4.9 %collective-permute-start.5 = (bf16[160,384]{1,0:T(8,128)(2,1)S(1)}, bf16[160,384]{1,0:T(8,128)(2,1)S(1)}, u32[]{:S(2)}, u32[]{:S(2)}) collective-permute-start(bf16[160,384]{1,0:T(8,128)(2,1)S(1)} %embed.1.mine0.after_ref), channel_id=1, source_target_pairs={{0,6},{2,0},{4,2},{6,4},{1,7},{3,1},{5,3},{7,5},{8,14},{10,8},{12,... | collective-permute-start | bytes 368648 | tf_op jit(solution)/shard_map/ppermute | solution.py:308
  28.7 4.5 %collective-permute-start.6 = (bf16[160,384]{1,0:T(8,128)(2,1)S(1)}, bf16[160,384]{1,0:T(8,128)(2,1)S(1)}, u32[]{:S(2)}, u32[]{:S(2)}) collective-permute-start(bf16[160,384]{1,0:T(8,128)(2,1)S(1)} %embed.1.mine0.after_ref), channel_id=1, source_target_pairs={{0,1},{1,0},{2,3},{3,2},{4,5},{5,4},{6,7},{7,6},{8,9},{9,8},{10,11... | collective-permute-start | bytes 368648 | tf_op jit(solution)/shard_map/ppermute | solution.py:314
  30.4 2.8 %collective-permute-start.7 = (bf16[160,384]{1,0:T(8,128)(2,1)S(1)}, bf16[160,384]{1,0:T(8,128)(2,1)S(1)}, u32[]{:S(2)}, u32[]{:S(2)}) collective-permute-start(bf16[160,384]{1,0:T(8,128)(2,1)S(1)} %collective-permute-done.3.mine1), channel_id=1, source_target_pairs={{0,1},{1,0},{2,3},{3,2},{4,5},{5,4},{6,7},{7,6},{8,9},{9,8},{10,11... | collective-permute-start | bytes 368648 | tf_op jit(solution)/shard_map/ppermute | solution.py:314
  32.2 1.3 %collective-permute-start.8 = (bf16[160,384]{1,0:T(8,128)(2,1)S(1)}, bf16[160,384]{1,0:T(8,128)(2,1)S(1)}, u32[]{:S(2)}, u32[]{:S(2)}) collective-permute-start(bf16[160,384]{1,0:T(8,128)(2,1)S(1)} %collective-permute-done.4.mine2), channel_id=1, source_target_pairs={{0,1},{1,0},{2,3},{3,2},{4,5},{5,4},{6,7},{7,6},{8,9},{9,8},{10,11... | collective-permute-start | bytes 368648 | tf_op jit(solution)/shard_map/ppermute | solution.py:314
  32.5 1.3 %collective-permute-start.9 = (bf16[160,384]{1,0:T(8,128)(2,1)S(1)}, bf16[160,384]{1,0:T(8,128)(2,1)S(1)}, u32[]{:S(2)}, u32[]{:S(2)}) collective-permute-start(bf16[160,384]{1,0:T(8,128)(2,1)S(1)} %collective-permute-done.5.mine3), channel_id=1, source_target_pairs={{0,1},{1,0},{2,3},{3,2},{4,5},{5,4},{6,7},{7,6},{8,9},{9,8},{10,11... | collective-permute-start | bytes 368648 | tf_op jit(solution)/shard_map/ppermute | solution.py:314
  32.7 6.9 %collective-permute-start.13 = (bf16[4,64,384]{2,1,0:T(8,128)(2,1)S(1)}, bf16[4,64,384]{2,1,0:T(8,128)(2,1)S(1)}, u32[]{:S(2)}, u32[]{:S(2)}) collective-permute-start(bf16[4,64,384]{2,1,0:T(8,128)(2,1)S(1)} %stack.1.same_ref), channel_id=1, source_target_pairs={{0,1},{1,0},{2,3},{3,2},{4,5},{5,4},{6,7},{7,6},{8,9},{9,8},{10,11... | collective-permute-start | bytes 589832 | tf_op jit(solution)/shard_map/ppermute | solution.py:314
  35.5 10.0 %collective-permute-start.10 = (bf16[2,128,384]{2,1,0:T(8,128)(2,1)S(1)}, bf16[2,128,384]{2,1,0:T(8,128)(2,1)S(1)}, u32[]{:S(2)}, u32[]{:S(2)}) collective-permute-start(bf16[2,128,384]{2,1,0:T(8,128)(2,1)S(1)} %far.1.after_ref.far0), channel_id=1, source_target_pairs={{0,16},{8,24},{16,0},{24,8},{32,48},{40,56},{48,32},{56,40},{64,80... | collective-permute-start | bytes 589832 | tf_op jit(solution)/shard_map/ppermute | solution.py:420
  37.6 9.7 %collective-permute-start.11 = (bf16[2,128,384]{2,1,0:T(8,128)(2,1)S(1)}, bf16[2,128,384]{2,1,0:T(8,128)(2,1)S(1)}, u32[]{:S(2)}, u32[]{:S(2)}) collective-permute-start(bf16[2,128,384]{2,1,0:T(8,128)(2,1)S(1)} %far.1.after_ref.far0), channel_id=1, source_target_pairs={{0,24},{8,0},{16,8},{24,16},{32,56},{40,32},{48,40},{56,48},{64,88... | collective-permute-start | bytes 589832 | tf_op jit(solution)/shard_map/ppermute | solution.py:420
  38.8 9.4 %collective-permute-start.12 = (bf16[2,128,384]{2,1,0:T(8,128)(2,1)S(1)}, bf16[2,128,384]{2,1,0:T(8,128)(2,1)S(1)}, u32[]{:S(2)}, u32[]{:S(2)}) collective-permute-start(bf16[2,128,384]{2,1,0:T(8,128)(2,1)S(1)} %far.1.after_ref.far0), channel_id=1, source_target_pairs={{0,8},{8,16},{16,24},{24,0},{32,40},{40,48},{48,56},{56,32},{64,72... | collective-permute-start | bytes 589832 | tf_op jit(solution)/shard_map/ppermute | solution.py:420
  49.4 8.2 %collective-permute-start.14 = (bf16[400,128]{1,0:T(8,128)(2,1)S(1)}, bf16[400,128]{1,0:T(8,128)(2,1)S(1)}, u32[]{:S(2)}, u32[]{:S(2)}) collective-permute-start(bf16[400,128]{1,0:T(8,128)(2,1)S(1)} %get-tuple-element.28), channel_id=1, source_target_pairs={{0,32},{8,40},{16,48},{24,56},{32,64},{40,72},{48,80},{56,88},{64,... | collective-permute-start | bytes 307208 | tf_op jit(solution)/shard_map/ppermute | solution.py:424
  50.0 7.6 %collective-permute-start.15 = (bf16[400,128]{1,0:T(8,128)(2,1)S(1)}, bf16[400,128]{1,0:T(8,128)(2,1)S(1)}, u32[]{:S(2)}, u32[]{:S(2)}) collective-permute-start(bf16[400,128]{1,0:T(8,128)(2,1)S(1)} %get-tuple-element.29), channel_id=1, source_target_pairs={{0,64},{8,72},{16,80},{24,88},{32,96},{40,104},{48,112},{56,120},{... | collective-permute-start | bytes 307208 | tf_op jit(solution)/shard_map/ppermute | solution.py:424
  52.7 5.5 %collective-permute-start.16 = (bf16[400,128]{1,0:T(8,128)(2,1)S(1)}, bf16[400,128]{1,0:T(8,128)(2,1)S(1)}, u32[]{:S(2)}, u32[]{:S(2)}) collective-permute-start(bf16[400,128]{1,0:T(8,128)(2,1)S(1)} %get-tuple-element.30), channel_id=1, source_target_pairs={{0,96},{8,104},{16,112},{24,120},{32,0},{40,8},{48,16},{56,24},{64... | collective-permute-start | bytes 307208 | tf_op jit(solution)/shard_map/ppermute | solution.py:424
  (6 other events, 51.3 us)

commit v5 on v4

--- a/solution.py
+++ b/solution.py
@@ -203,23 +203,19 @@
 def embed_kernel(
     kinds_ref,
     recv_ref,
-    mid_hbm,
+    mid_ref,
     coarse_hbm,
     fine1,
     fine2,
     fine3,
     table_ref,
     out_ref,
-    mid_ref,
     coarse_ref,
     mid_buf,
     coarse_buf,
-    mid_sem,
     coarse_sems,
 ):
     del fine1, fine2, fine3, table_ref
-    mid_copy = pltpu.make_async_copy(mid_hbm, mid_ref, mid_sem)
-    mid_copy.start()
     coarse_copies = []
     for g in range(4):
         part = pl.ds(1024 * g, 1024)
@@ -256,7 +252,6 @@
     )
     order = select_columns(512, 512, lambda j: (j & 3) * 128 + (j >> 2))
     tokens = dot(tokens, order).astype(BF)
-    mid_copy.wait()
     out_ref[0:112, :] = dot(tokens, mid_ref[...]).astype(BF)
     cells = coarse_buf[0:8].reshape(512, 128)
     order = select_rows(
@@ -287,14 +282,12 @@
     return pl.pallas_call(
         embed_kernel,
         out_shape=jax.ShapeDtypeStruct((160, patch_mid.shape[1]), BF),
-        in_specs=[SMEM, VMEM] + [ANY] * 6,
+        in_specs=[SMEM, VMEM, VMEM] + [ANY] * 5,
         out_specs=VMEM,
         scratch_shapes=[
-            pltpu.VMEM(patch_mid.shape, BF),
             pltpu.VMEM(patch_coarse.shape, BF),
             pltpu.VMEM((8, 64, 128), BF),
             pltpu.VMEM((9, 64, 128), BF),
-            pltpu.SemaphoreType.DMA,
             pltpu.SemaphoreType.DMA((4,)),
         ],
         compiler_params=params(EMBED),
@@ -549,16 +542,21 @@
     )(kinds, *gathered[0], *gathered[1], folded, gram, cosine, sine, times)
 
 
-def near_kernel(query_ref, key_ref, value_ref, num_ref, den_ref):
+def near_kernel(query_ref, key_ref, value_ref, far_ref, num_ref, den_ref):
     heads = query_ref.shape[0] // HEAD_DIM
     for h in range(heads):
         at = slice(HEAD_DIM * h, HEAD_DIM * (h + 1))
         weights = jnp.exp2(dot(key_ref[at, :], query_ref[at, :], ((0,), (0,))))
-        den_ref[h : h + 1, :] = jnp.sum(weights, axis=0, keepdims=True)
-        num_ref[at, :] = dot(value_ref[at, :], weights.astype(BF))
-
-
-def attend_near(queries, keys, values):
+        own_weights = jnp.exp2(dot(far_ref[0, :, at], query_ref[at, :]))
+        den_ref[h : h + 1, :] = jnp.sum(weights, axis=0, keepdims=True) + jnp.sum(
+            own_weights, axis=0, keepdims=True
+        )
+        num_ref[at, :] = dot(value_ref[at, :], weights.astype(BF)) + dot(
+            far_ref[1, :, at], own_weights.astype(BF), ((0,), (0,))
+        )
+
+
+def attend_near(queries, keys, values, far):
     columns, count = queries.shape
     return pl.pallas_call(
         near_kernel,
@@ -566,12 +564,12 @@
             jax.ShapeDtypeStruct((columns, count), F32),
             jax.ShapeDtypeStruct((8, count), F32),
         ),
-        in_specs=[VMEM] * 3,
+        in_specs=[VMEM] * 4,
         out_specs=(VMEM, VMEM),
         compiler_params=params(),
         cost_estimate=cost(4e9, 1e7, 2e6),
         name="near",
-    )(queries, keys, values)
+    )(queries, keys, values, far)
 
 
 def row_angles(kinds_ref, freq_ref):
@@ -671,7 +669,7 @@
     )(*gathered[0], *gathered[1], modulation, w_qkv, perm, table)
 
 
-def history_kernel(far0, far1, far3, far2, query_ref, num_ref, den_ref, out0, out1, out2, out3):
+def history_kernel(far1, far2, far3, query_ref, num_ref, den_ref, out0, out1, out2, out3):
     heads = query_ref.shape[0] // HEAD_DIM
     count = query_ref.shape[1]
     outs = (out0, out1, out2, out3)
@@ -679,7 +677,7 @@
     tail = jnp.zeros((16, count), F32)
     for h in range(heads):
         at = slice(HEAD_DIM * h, HEAD_DIM * (h + 1))
-        fars = (far0, far1, far3, far2)
+        fars = (far1, far2, far3)
         keys = jnp.concatenate([far[0, :, at] for far in fars], axis=0)
         values = jnp.concatenate([far[1, :, at] for far in fars], axis=0)
         weights = jnp.exp2(dot(keys, query_ref[at, :]))
@@ -698,7 +696,7 @@
     return pl.pallas_call(
         history_kernel,
         out_shape=tuple(jax.ShapeDtypeStruct((columns + 16, 128), t) for t in (F32, BF, BF, BF)),
-        in_specs=[VMEM] * 7,
+        in_specs=[VMEM] * 6,
         out_specs=tuple([VMEM] * 4),
         compiler_params=params(),
         cost_estimate=cost(2e9, 4e6, 1e6),
@@ -754,8 +752,8 @@
     queries, keys, values = make_tokens(
         slab_kernel, gathered, folded, gram, cosine, sine, times
     )
-    numerator, denominator = attend_near(queries, keys, values)
-    fars = [far, far2, far3, far1]
+    numerator, denominator = attend_near(queries, keys, values, far)
+    fars = [far2, far3, far1]
     parts = attend_history(fars, queries, numerator, denominator)
     part2 = along_y(parts[2], 2)
     return combine([parts[0], along_y(parts[1], 1), part2, along_y(parts[3], 3)])

time: 59.2 us -> 59 us (level)
  waiting for transfers between devices: 12.7 us -> 12.1 us
  transfers between devices with their start and end apart: 18 -> 18, of which waited for: 10 -> 10; matrix products, arithmetic and copies ran while one was open for 0% -> 0% of each run, Pallas kernels for 14% -> 15%
where the time goes in v5:
time: 59 us; the launch traced here: 58.7 us
  starting transfers between devices  29.5 us (50%)
  Pallas kernels  15.9 us (27%)
  waiting for transfers between devices  12.1 us (21%)
  local copies, waits for them, and re-layouts  1.04 us (2%)
    ppermute x6, starting transfers between devices, along_head(): lax.ppermute(block, 'head', [(i, (i + d) % 4) for i in range(4)])  12.7 us
    all_to_all x1, starting transfers between devices, per_device(): received = lax.all_to_all(sent, 'frame', 0, 0, tiled=True)  7.31 us
    ppermute x6, waiting for transfers between devices, along_head(): lax.ppermute(block, 'head', [(i, (i + d) % 4) for i in range(4)])  5.16 us
    ppermute x3, starting transfers between devices, along_y(): lax.ppermute(value, 'frame', [(i, (i + 4 * d) % 16) for i in range(16)])  4.77 us
    ppermute x3, starting transfers between devices, along_x(): lax.ppermute(value, 'frame', [(i, i // 4 * 4 + (i + d) % 4) for i in rang...  4.15 us
    ppermute x3, waiting for transfers between devices, along_y(): lax.ppermute(value, 'frame', [(i, (i + 4 * d) % 16) for i in range(16)])  4.01 us
    pallas_call x1, Pallas kernels, embed(): pl.pallas_call(embed_kernel, out_shape=jax.ShapeDtypeStruct((160, patch_m...  2.94 us
    pallas_call x1, Pallas kernels, fold(): pl.pallas_call(fold_kernel, out_shape=(jax.ShapeDtypeStruct((3, 144, colu...  2.31 us
  transfers between devices with their start and end apart: 18, of which 10 were waited for; matrix products, arithmetic and copies ran while one was open for 0% of the time, Pallas kernels for 15%

profile of v5, /device:TPU:0, one launch (start us, length us, event | category | flops | bytes accessed | tf_op | source)
XLA Modules:
  0.0 58.7 jit_solution(15475710736002807478)
XLA Ops:
  0.0 2.3 %prepare.1 = (bf16[16,80,128]{2,1,0:T(8,128)(2,1)}, bf16[64,384]{1,0:T(8,128)(2,1)}) custom-call(s32[16]{0:T(128)} %kinds_ref.5, bf16[512,256]{1,0:T(8,128)(2,1)} %bitcast.4, bf16[64,128]{1,0:T(8,128)(2,1)} %bitcast.5, bf16[64,384]{1,0:T(8,128)(2,1)} %fine_hbm.1), custom_call_target="tpu_custom_call" | custom-call | flops 20000000000 | bytes 1000000 | tf_op jit(solution)/shard_map/prepare/pallas_call | solution.py:183
  2.3 7.3 %all-to-all-start = ((bf16[16,80,128]{2,1,0:T(8,128)(2,1)}), bf16[16,80,128]{2,1,0:T(8,128)(2,1)S(1)}, u32[]{:S(2)}, u32[]{:S(2)}) async-start(bf16[16,80,128]{2,1,0:T(8,128)(2,1)} %get-tuple-element.18.after_ref), calls=%async_computation | async-start | bytes 655360 | tf_op jit(solution)/shard_map/all_to_all | solution.py:742
  9.6 2.0 %collective-permute-start = (bf16[64,384]{1,0:T(8,128)(2,1)}, bf16[64,384]{1,0:T(8,128)(2,1)S(1)}, u32[]{:S(2)}, u32[]{:S(2)}) collective-permute-start(bf16[64,384]{1,0:T(8,128)(2,1)} %get-tuple-element.19.ref0), channel_id=1, source_target_pairs={{0,2},{2,4},{4,6},{6,0},{1,3},{3,5},{5,7},{7,1},{8,10},{10,12},{12... | collective-permute-start | bytes 147464 | tf_op jit(solution)/shard_map/ppermute | solution.py:301
  11.6 3.6 %collective-permute-start.1 = (bf16[64,384]{1,0:T(8,128)(2,1)}, bf16[64,384]{1,0:T(8,128)(2,1)S(1)}, u32[]{:S(2)}, u32[]{:S(2)}) collective-permute-start(bf16[64,384]{1,0:T(8,128)(2,1)} %get-tuple-element.19.ref0), channel_id=1, source_target_pairs={{0,4},{2,6},{4,0},{6,2},{1,5},{3,7},{5,1},{7,3},{8,12},{10,14},{12... | collective-permute-start | bytes 147464 | tf_op jit(solution)/shard_map/ppermute | solution.py:301
  15.2 1.0 %collective-permute-start.2 = (bf16[64,384]{1,0:T(8,128)(2,1)}, bf16[64,384]{1,0:T(8,128)(2,1)S(1)}, u32[]{:S(2)}, u32[]{:S(2)}) collective-permute-start(bf16[64,384]{1,0:T(8,128)(2,1)} %get-tuple-element.19.ref0), channel_id=1, source_target_pairs={{0,6},{2,0},{4,2},{6,4},{1,7},{3,1},{5,3},{7,5},{8,14},{10,8},{12,... | collective-permute-start | bytes 147464 | tf_op jit(solution)/shard_map/ppermute | solution.py:301
  17.2 1.0 %table.1.table_ref = f32[2,128,128]{2,1,0:T(8,128)S(1)} custom-call(s32[16]{0:T(128)S(1)} %copy-done.4, f32[8,128]{1,0:T(8,128)S(1)} %copy-done.3, bf16[16,80,128]{2,1,0:T(8,128)(2,1)S(1)} %copy-done), custom_call_target="tpu_custom_call" | custom-call | flops 100000 | bytes 1000 | tf_op jit(solution)/shard_map/table/pallas_call | solution.py:613
  18.2 1.3 %collective-permute-done.2.fine3.ref3 = bf16[64,384]{1,0:T(8,128)(2,1)S(1)} collective-permute-done((bf16[64,384]{1,0:T(8,128)(2,1)}, bf16[64,384]{1,0:T(8,128)(2,1)S(1)}, u32[]{:S(2)}, u32[]{:S(2)}) %collective-permute-start.2) | collective-permute-done | bytes 49184 | tf_op jit(solution)/shard_map/ppermute | solution.py:301
  19.5 2.9 %embed.1.mine0.after_ref = bf16[160,384]{1,0:T(8,128)(2,1)S(1)} custom-call(s32[16]{0:T(128)S(1)} %copy-done.4, bf16[16,80,128]{2,1,0:T(8,128)(2,1)S(1)} %all-to-all-done.recv_ref, bf16[512,384]{1,0:T(8,128)(2,1)S(1)} %copy-done.5, bf16[4096,384]{1,0:T(8,128)(2,1)} %coarse_hbm.1, bf16[64,384]{1,0:T(8,128)(2,1)S(1)} %collective-permute-done.fine1.ref1, ...), custom_call_target="tpu_custom_call" | custom-call | flops 2000000000 | bytes 5000000 | tf_op jit(solution)/shard_map/embed/pallas_call | solution.py:282
  22.5 1.5 %collective-permute-start.3 = (bf16[160,384]{1,0:T(8,128)(2,1)S(1)}, bf16[160,384]{1,0:T(8,128)(2,1)S(1)}, u32[]{:S(2)}, u32[]{:S(2)}) collective-permute-start(bf16[160,384]{1,0:T(8,128)(2,1)S(1)} %embed.1.mine0.after_ref), channel_id=1, source_target_pairs={{0,2},{2,4},{4,6},{6,0},{1,3},{3,5},{5,7},{7,1},{8,10},{10,12},{12... | collective-permute-start | bytes 368648 | tf_op jit(solution)/shard_map/ppermute | solution.py:301
  24.0 3.6 %collective-permute-start.4 = (bf16[160,384]{1,0:T(8,128)(2,1)S(1)}, bf16[160,384]{1,0:T(8,128)(2,1)S(1)}, u32[]{:S(2)}, u32[]{:S(2)}) collective-permute-start(bf16[160,384]{1,0:T(8,128)(2,1)S(1)} %embed.1.mine0.after_ref), channel_id=1, source_target_pairs={{0,4},{2,6},{4,0},{6,2},{1,5},{3,7},{5,1},{7,3},{8,12},{10,14},{12... | collective-permute-start | bytes 368648 | tf_op jit(solution)/shard_map/ppermute | solution.py:301
  27.6 1.0 %collective-permute-start.5 = (bf16[160,384]{1,0:T(8,128)(2,1)S(1)}, bf16[160,384]{1,0:T(8,128)(2,1)S(1)}, u32[]{:S(2)}, u32[]{:S(2)}) collective-permute-start(bf16[160,384]{1,0:T(8,128)(2,1)S(1)} %embed.1.mine0.after_ref), channel_id=1, source_target_pairs={{0,6},{2,0},{4,2},{6,4},{1,7},{3,1},{5,3},{7,5},{8,14},{10,8},{12,... | collective-permute-start | bytes 368648 | tf_op jit(solution)/shard_map/ppermute | solution.py:301
  28.6 1.7 %collective-permute-done.3.mine1 = bf16[160,384]{1,0:T(8,128)(2,1)S(1)} collective-permute-done((bf16[160,384]{1,0:T(8,128)(2,1)S(1)}, bf16[160,384]{1,0:T(8,128)(2,1)S(1)}, u32[]{:S(2)}, u32[]{:S(2)}) %collective-permute-start.3) | collective-permute-done | bytes 122912 | tf_op jit(solution)/shard_map/ppermute | solution.py:301
  30.3 1.8 %collective-permute-done.4.mine2 = bf16[160,384]{1,0:T(8,128)(2,1)S(1)} collective-permute-done((bf16[160,384]{1,0:T(8,128)(2,1)S(1)}, bf16[160,384]{1,0:T(8,128)(2,1)S(1)}, u32[]{:S(2)}, u32[]{:S(2)}) %collective-permute-start.4) | collective-permute-done | bytes 122912 | tf_op jit(solution)/shard_map/ppermute | solution.py:301
  33.8 1.6 %far.1.after_ref.far_ref = bf16[2,128,384]{2,1,0:T(8,128)(2,1)S(1)} custom-call(bf16[160,384]{1,0:T(8,128)(2,1)S(1)} %embed.1.mine0.after_ref, bf16[160,384]{1,0:T(8,128)(2,1)S(1)} %collective-permute-done.3.mine1, bf16[160,384]{1,0:T(8,128)(2,1)S(1)} %collective-permute-done.4.mine2, bf16[160,384]{1,0:T(8,128)(2,1)S(1)} %collective-permute-done.5.mine3, ...), custom_call_target="tpu_custom_call" | custom-call | flops 2000000000 | bytes 10000000 | tf_op jit(solution)/shard_map/far/pallas_call | solution.py:660
  35.4 2.1 %collective-permute-start.10 = (bf16[2,128,384]{2,1,0:T(8,128)(2,1)S(1)}, bf16[2,128,384]{2,1,0:T(8,128)(2,1)S(1)}, u32[]{:S(2)}, u32[]{:S(2)}) collective-permute-start(bf16[2,128,384]{2,1,0:T(8,128)(2,1)S(1)} %far.1.after_ref.far_ref), channel_id=1, source_target_pairs={{0,16},{8,24},{16,0},{24,8},{32,48},{40,56},{48,32},{56,40},{64,80... | collective-permute-start | bytes 589832 | tf_op jit(solution)/shard_map/ppermute | solution.py:413
  37.5 1.2 %collective-permute-start.11 = (bf16[2,128,384]{2,1,0:T(8,128)(2,1)S(1)}, bf16[2,128,384]{2,1,0:T(8,128)(2,1)S(1)}, u32[]{:S(2)}, u32[]{:S(2)}) collective-permute-start(bf16[2,128,384]{2,1,0:T(8,128)(2,1)S(1)} %far.1.after_ref.far_ref), channel_id=1, source_target_pairs={{0,24},{8,0},{16,8},{24,16},{32,56},{40,32},{48,40},{56,48},{64,88... | collective-permute-start | bytes 589832 | tf_op jit(solution)/shard_map/ppermute | solution.py:413
  39.5 2.3 %fold.1 = (bf16[3,144,384]{2,1,0:T(8,128)(2,1)S(1)}, f32[64,64]{1,0:T(8,128)S(1)}) custom-call(bf16[4,64,384]{2,1,0:T(8,128)(2,1)S(1)} %stack.1.same_ref, bf16[4,64,384]{2,1,0:T(8,128)(2,1)S(1)} %collective-permute-done.13.other_ref, f32[2,3072]{1,0:T(2,128)S(1)} %copy-done.2, bf16[3,3072,384]{2,1,0:T(8,128)(2,1)S(1)} %bitcast.3, ...), custom_call_target="tpu_custom_call" | custom-call | flops 1000000 | bytes 10000 | tf_op jit(solution)/shard_map/fold/pallas_call | solution.py:397
  41.9 1.9 %tokens.1 = (bf16[384,512]{1,0:T(8,128)(2,1)S(1)}, bf16[384,1024]{1,0:T(8,128)(2,1)S(1)}, bf16[384,1024]{1,0:T(8,128)(2,1)S(1)}) custom-call(s32[16]{0:T(128)S(1)} %copy-done.4, bf16[160,384]{1,0:T(8,128)(2,1)S(1)} %embed.1.mine0.after_ref, bf16[160,384]{1,0:T(8,128)(2,1)S(1)} %collective-permute-done.3.mine1, ...), custom_call_target="tpu_custom_call" | custom-call | flops 2000000000 | bytes 8000000 | tf_op jit(solution)/shard_map/tokens/pallas_call | solution.py:529
  43.8 2.1 %near.1 = (f32[384,512]{1,0:T(8,128)S(1)}, f32[8,512]{1,0:T(8,128)S(1)}) custom-call(bf16[384,512]{1,0:T(8,128)(2,1)S(1)} %get-tuple-element.22.query_ref, bf16[384,1024]{1,0:T(8,128)(2,1)S(1)} %get-tuple-element.23.key_ref, bf16[384,1024]{1,0:T(8,128)(2,1)S(1)} %get-tuple-element.24.value_ref, bf16[2,128,384]{2,1,0:T(8,128)(2,1)S(1)} %far.1.after_ref.far_ref), custom_call_target="tpu_custom_call" | custom-call | flops 4000000000 | bytes 10000000 | tf_op jit(solution)/shard_map/near/pallas_call | solution.py:561
  45.9 1.3 %collective-permute-done.11.far2 = bf16[2,128,384]{2,1,0:T(8,128)(2,1)S(1)} collective-permute-done((bf16[2,128,384]{2,1,0:T(8,128)(2,1)S(1)}, bf16[2,128,384]{2,1,0:T(8,128)(2,1)S(1)}, u32[]{:S(2)}, u32[]{:S(2)}) %collective-permute-start.11) | collective-permute-done | bytes 196640 | tf_op jit(solution)/shard_map/ppermute | solution.py:413
  48.2 1.0 %history.1 = (f32[400,128]{1,0:T(8,128)S(1)}, bf16[400,128]{1,0:T(8,128)(2,1)S(1)}, bf16[400,128]{1,0:T(8,128)(2,1)S(1)}, bf16[400,128]{1,0:T(8,128)(2,1)S(1)}) custom-call(bf16[2,128,384]{2,1,0:T(8,128)(2,1)S(1)} %collective-permute-done.10.far1, bf16[2,128,384]{2,1,0:T(8,128)(2,1)S(1)} %collective-permute-done.11.far2, ...), custom_call_target="tpu_custom_call" | custom-call | flops 2000000000 | bytes 4000000 | tf_op jit(solution)/shard_map/history/pallas_call | solution.py:696
  49.8 2.7 %collective-permute-start.15 = (bf16[400,128]{1,0:T(8,128)(2,1)S(1)}, bf16[400,128]{1,0:T(8,128)(2,1)S(1)}, u32[]{:S(2)}, u32[]{:S(2)}) collective-permute-start(bf16[400,128]{1,0:T(8,128)(2,1)S(1)} %get-tuple-element.29), channel_id=1, source_target_pairs={{0,64},{8,72},{16,80},{24,88},{32,96},{40,104},{48,112},{56,120},{... | collective-permute-start | bytes 307208 | tf_op jit(solution)/shard_map/ppermute | solution.py:417
  52.5 1.5 %collective-permute-start.16 = (bf16[400,128]{1,0:T(8,128)(2,1)S(1)}, bf16[400,128]{1,0:T(8,128)(2,1)S(1)}, u32[]{:S(2)}, u32[]{:S(2)}) collective-permute-start(bf16[400,128]{1,0:T(8,128)(2,1)S(1)} %get-tuple-element.30), channel_id=1, source_target_pairs={{0,96},{8,104},{16,112},{24,120},{32,0},{40,8},{48,16},{56,24},{64... | collective-permute-start | bytes 307208 | tf_op jit(solution)/shard_map/ppermute | solution.py:417
  54.0 3.4 %collective-permute-done.14.part1 = bf16[400,128]{1,0:T(8,128)(2,1)S(1)} collective-permute-done((bf16[400,128]{1,0:T(8,128)(2,1)S(1)}, bf16[400,128]{1,0:T(8,128)(2,1)S(1)}, u32[]{:S(2)}, u32[]{:S(2)}) %collective-permute-start.14) | collective-permute-done | bytes 102432 | tf_op jit(solution)/shard_map/ppermute | solution.py:417
  (47 shorter events, 6.4 us)
Async XLA Ops:
  0.0 16.2 %copy-start.3 = (f32[8,128]{1,0:T(8,128)S(1)}, f32[8,128]{1,0:T(8,128)}, u32[]{:S(2)}) copy-start(f32[8,128]{1,0:T(8,128)} %constant.13.clone.freq_ref) | copy-start | bytes 12292
  0.0 16.2 %copy-start.4 = (s32[16]{0:T(128)S(1)}, s32[16]{0:T(128)}, u32[]{:S(2)}) copy-start(s32[16]{0:T(128)} %kinds_ref.5) | copy-start | bytes 196
  0.0 19.5 %copy-start.5 = (bf16[512,384]{1,0:T(8,128)(2,1)S(1)}, bf16[512,384]{1,0:T(8,128)(2,1)}, u32[]{:S(2)}) copy-start(bf16[512,384]{1,0:T(8,128)(2,1)} %mid_ref.1) | copy-start | bytes 1179652
  2.3 30.3 %copy-start.6 = (bf16[64,384]{1,0:T(8,128)(2,1)S(1)}, bf16[64,384]{1,0:T(8,128)(2,1)}, u32[]{:S(2)}) copy-start(bf16[64,384]{1,0:T(8,128)(2,1)} %get-tuple-element.19.ref0) | copy-start | bytes 147460
  2.3 17.2 %all-to-all-start = ((bf16[16,80,128]{2,1,0:T(8,128)(2,1)}), bf16[16,80,128]{2,1,0:T(8,128)(2,1)S(1)}, u32[]{:S(2)}, u32[]{:S(2)}) async-start(bf16[16,80,128]{2,1,0:T(8,128)(2,1)} %get-tuple-element.18.after_ref), calls=%async_computation | async-start | bytes 655360 | tf_op jit(solution)/shard_map/all_to_all | solution.py:742
  9.6 8.6 %collective-permute-start = (bf16[64,384]{1,0:T(8,128)(2,1)}, bf16[64,384]{1,0:T(8,128)(2,1)S(1)}, u32[]{:S(2)}, u32[]{:S(2)}) collective-permute-start(bf16[64,384]{1,0:T(8,128)(2,1)} %get-tuple-element.19.ref0), channel_id=1, source_target_pairs={{0,2},{2,4},{4,6},{6,0},{1,3},{3,5},{5,7},{7,1},{8,10},{10,12},{12... | collective-permute-start | bytes 147464 | tf_op jit(solution)/shard_map/ppermute | solution.py:301
  11.6 6.6 %collective-permute-start.1 = (bf16[64,384]{1,0:T(8,128)(2,1)}, bf16[64,384]{1,0:T(8,128)(2,1)S(1)}, u32[]{:S(2)}, u32[]{:S(2)}) collective-permute-start(bf16[64,384]{1,0:T(8,128)(2,1)} %get-tuple-element.19.ref0), channel_id=1, source_target_pairs={{0,4},{2,6},{4,0},{6,2},{1,5},{3,7},{5,1},{7,3},{8,12},{10,14},{12... | collective-permute-start | bytes 147464 | tf_op jit(solution)/shard_map/ppermute | solution.py:301
  15.2 4.3 %collective-permute-start.2 = (bf16[64,384]{1,0:T(8,128)(2,1)}, bf16[64,384]{1,0:T(8,128)(2,1)S(1)}, u32[]{:S(2)}, u32[]{:S(2)}) collective-permute-start(bf16[64,384]{1,0:T(8,128)(2,1)} %get-tuple-element.19.ref0), channel_id=1, source_target_pairs={{0,6},{2,0},{4,2},{6,4},{1,7},{3,1},{5,3},{7,5},{8,14},{10,8},{12,... | collective-permute-start | bytes 147464 | tf_op jit(solution)/shard_map/ppermute | solution.py:301
  19.5 14.3 %slice-start = ((s8[7077888]{0:T(1024)(128)(4,1)}), s8[2883584]{0:T(1024)(128)(4,1)S(1)}, s32[]{:S(2)}) async-start(s8[7077888]{0:T(1024)(128)(4,1)} %bitcast.2), calls=%async_computation.1 | async-start | bytes 5767168
  22.5 11.3 %slice-start.1 = ((s8[7077888]{0:T(1024)(128)(4,1)}), s8[4194304]{0:T(1024)(128)(4,1)S(1)}, s32[]{:S(2)}) async-start(s8[7077888]{0:T(1024)(128)(4,1)} %bitcast.2), calls=%async_computation.2 | async-start | bytes 8388608
  22.5 7.8 %collective-permute-start.3 = (bf16[160,384]{1,0:T(8,128)(2,1)S(1)}, bf16[160,384]{1,0:T(8,128)(2,1)S(1)}, u32[]{:S(2)}, u32[]{:S(2)}) collective-permute-start(bf16[160,384]{1,0:T(8,128)(2,1)S(1)} %embed.1.mine0.after_ref), channel_id=1, source_target_pairs={{0,2},{2,4},{4,6},{6,0},{1,3},{3,5},{5,7},{7,1},{8,10},{10,12},{12... | collective-permute-start | bytes 368648 | tf_op jit(solution)/shard_map/ppermute | solution.py:301
  24.0 8.1 %collective-permute-start.4 = (bf16[160,384]{1,0:T(8,128)(2,1)S(1)}, bf16[160,384]{1,0:T(8,128)(2,1)S(1)}, u32[]{:S(2)}, u32[]{:S(2)}) collective-permute-start(bf16[160,384]{1,0:T(8,128)(2,1)S(1)} %embed.1.mine0.after_ref), channel_id=1, source_target_pairs={{0,4},{2,6},{4,0},{6,2},{1,5},{3,7},{5,1},{7,3},{8,12},{10,14},{12... | collective-permute-start | bytes 368648 | tf_op jit(solution)/shard_map/ppermute | solution.py:301
  27.6 4.9 %collective-permute-start.5 = (bf16[160,384]{1,0:T(8,128)(2,1)S(1)}, bf16[160,384]{1,0:T(8,128)(2,1)S(1)}, u32[]{:S(2)}, u32[]{:S(2)}) collective-permute-start(bf16[160,384]{1,0:T(8,128)(2,1)S(1)} %embed.1.mine0.after_ref), channel_id=1, source_target_pairs={{0,6},{2,0},{4,2},{6,4},{1,7},{3,1},{5,3},{7,5},{8,14},{10,8},{12,... | collective-permute-start | bytes 368648 | tf_op jit(solution)/shard_map/ppermute | solution.py:301
  28.6 4.5 %collective-permute-start.6 = (bf16[160,384]{1,0:T(8,128)(2,1)S(1)}, bf16[160,384]{1,0:T(8,128)(2,1)S(1)}, u32[]{:S(2)}, u32[]{:S(2)}) collective-permute-start(bf16[160,384]{1,0:T(8,128)(2,1)S(1)} %embed.1.mine0.after_ref), channel_id=1, source_target_pairs={{0,1},{1,0},{2,3},{3,2},{4,5},{5,4},{6,7},{7,6},{8,9},{9,8},{10,11... | collective-permute-start | bytes 368648 | tf_op jit(solution)/shard_map/ppermute | solution.py:307
  30.3 2.8 %collective-permute-start.7 = (bf16[160,384]{1,0:T(8,128)(2,1)S(1)}, bf16[160,384]{1,0:T(8,128)(2,1)S(1)}, u32[]{:S(2)}, u32[]{:S(2)}) collective-permute-start(bf16[160,384]{1,0:T(8,128)(2,1)S(1)} %collective-permute-done.3.mine1), channel_id=1, source_target_pairs={{0,1},{1,0},{2,3},{3,2},{4,5},{5,4},{6,7},{7,6},{8,9},{9,8},{10,11... | collective-permute-start | bytes 368648 | tf_op jit(solution)/shard_map/ppermute | solution.py:307
  32.1 1.3 %collective-permute-start.8 = (bf16[160,384]{1,0:T(8,128)(2,1)S(1)}, bf16[160,384]{1,0:T(8,128)(2,1)S(1)}, u32[]{:S(2)}, u32[]{:S(2)}) collective-permute-start(bf16[160,384]{1,0:T(8,128)(2,1)S(1)} %collective-permute-done.4.mine2), channel_id=1, source_target_pairs={{0,1},{1,0},{2,3},{3,2},{4,5},{5,4},{6,7},{7,6},{8,9},{9,8},{10,11... | collective-permute-start | bytes 368648 | tf_op jit(solution)/shard_map/ppermute | solution.py:307
  32.5 1.3 %collective-permute-start.9 = (bf16[160,384]{1,0:T(8,128)(2,1)S(1)}, bf16[160,384]{1,0:T(8,128)(2,1)S(1)}, u32[]{:S(2)}, u32[]{:S(2)}) collective-permute-start(bf16[160,384]{1,0:T(8,128)(2,1)S(1)} %collective-permute-done.5.mine3), channel_id=1, source_target_pairs={{0,1},{1,0},{2,3},{3,2},{4,5},{5,4},{6,7},{7,6},{8,9},{9,8},{10,11... | collective-permute-start | bytes 368648 | tf_op jit(solution)/shard_map/ppermute | solution.py:307
  32.7 6.9 %collective-permute-start.13 = (bf16[4,64,384]{2,1,0:T(8,128)(2,1)S(1)}, bf16[4,64,384]{2,1,0:T(8,128)(2,1)S(1)}, u32[]{:S(2)}, u32[]{:S(2)}) collective-permute-start(bf16[4,64,384]{2,1,0:T(8,128)(2,1)S(1)} %stack.1.same_ref), channel_id=1, source_target_pairs={{0,1},{1,0},{2,3},{3,2},{4,5},{5,4},{6,7},{7,6},{8,9},{9,8},{10,11... | collective-permute-start | bytes 589832 | tf_op jit(solution)/shard_map/ppermute | solution.py:307
  35.4 10.5 %collective-permute-start.10 = (bf16[2,128,384]{2,1,0:T(8,128)(2,1)S(1)}, bf16[2,128,384]{2,1,0:T(8,128)(2,1)S(1)}, u32[]{:S(2)}, u32[]{:S(2)}) collective-permute-start(bf16[2,128,384]{2,1,0:T(8,128)(2,1)S(1)} %far.1.after_ref.far_ref), channel_id=1, source_target_pairs={{0,16},{8,24},{16,0},{24,8},{32,48},{40,56},{48,32},{56,40},{64,80... | collective-permute-start | bytes 589832 | tf_op jit(solution)/shard_map/ppermute | solution.py:413
  37.5 9.7 %collective-permute-start.11 = (bf16[2,128,384]{2,1,0:T(8,128)(2,1)S(1)}, bf16[2,128,384]{2,1,0:T(8,128)(2,1)S(1)}, u32[]{:S(2)}, u32[]{:S(2)}) collective-permute-start(bf16[2,128,384]{2,1,0:T(8,128)(2,1)S(1)} %far.1.after_ref.far_ref), channel_id=1, source_target_pairs={{0,24},{8,0},{16,8},{24,16},{32,56},{40,32},{48,40},{56,48},{64,88... | collective-permute-start | bytes 589832 | tf_op jit(solution)/shard_map/ppermute | solution.py:413
  38.7 9.4 %collective-permute-start.12 = (bf16[2,128,384]{2,1,0:T(8,128)(2,1)S(1)}, bf16[2,128,384]{2,1,0:T(8,128)(2,1)S(1)}, u32[]{:S(2)}, u32[]{:S(2)}) collective-permute-start(bf16[2,128,384]{2,1,0:T(8,128)(2,1)S(1)} %far.1.after_ref.far_ref), channel_id=1, source_target_pairs={{0,8},{8,16},{16,24},{24,0},{32,40},{40,48},{48,56},{56,32},{64,72... | collective-permute-start | bytes 589832 | tf_op jit(solution)/shard_map/ppermute | solution.py:413
  49.2 8.2 %collective-permute-start.14 = (bf16[400,128]{1,0:T(8,128)(2,1)S(1)}, bf16[400,128]{1,0:T(8,128)(2,1)S(1)}, u32[]{:S(2)}, u32[]{:S(2)}) collective-permute-start(bf16[400,128]{1,0:T(8,128)(2,1)S(1)} %get-tuple-element.28), channel_id=1, source_target_pairs={{0,32},{8,40},{16,48},{24,56},{32,64},{40,72},{48,80},{56,88},{64,... | collective-permute-start | bytes 307208 | tf_op jit(solution)/shard_map/ppermute | solution.py:417
  49.8 7.6 %collective-permute-start.15 = (bf16[400,128]{1,0:T(8,128)(2,1)S(1)}, bf16[400,128]{1,0:T(8,128)(2,1)S(1)}, u32[]{:S(2)}, u32[]{:S(2)}) collective-permute-start(bf16[400,128]{1,0:T(8,128)(2,1)S(1)} %get-tuple-element.29), channel_id=1, source_target_pairs={{0,64},{8,72},{16,80},{24,88},{32,96},{40,104},{48,112},{56,120},{... | collective-permute-start | bytes 307208 | tf_op jit(solution)/shard_map/ppermute | solution.py:417
  52.5 5.5 %collective-permute-start.16 = (bf16[400,128]{1,0:T(8,128)(2,1)S(1)}, bf16[400,128]{1,0:T(8,128)(2,1)S(1)}, u32[]{:S(2)}, u32[]{:S(2)}) collective-permute-start(bf16[400,128]{1,0:T(8,128)(2,1)S(1)} %get-tuple-element.30), channel_id=1, source_target_pairs={{0,96},{8,104},{16,112},{24,120},{32,0},{40,8},{48,16},{56,24},{64... | collective-permute-start | bytes 307208 | tf_op jit(solution)/shard_map/ppermute | solution.py:417
  (6 other events, 51.3 us)

commit v6 on v5

--- a/solution.py
+++ b/solution.py
@@ -120,6 +120,15 @@
     own = select_rows(
         16, 64, lambda i: ((first + (i & 7)) & 31) * 2 + ((first + (i & 7)) >> 5)
     )
+    mid_cols = select_rows(256, 256, lambda i: (i & 63) * 4 + (i >> 6))
+    mid_lanes = select_columns(
+        512,
+        512,
+        lambda j: ((j >> 8) * 2 + ((j >> 2) & 1)) * 128
+        + ((j >> 3) & 15) * 8
+        + ((j >> 7) & 1) * 4
+        + (j & 3),
+    )
     kinds_copy.wait()
     kind = kinds_ref[lax.axis_index("frame")]
     sec_copy.wait()
@@ -143,17 +152,8 @@
 
     @pl.when(kind == 1)
     def _():
-        cols = select_rows(256, 256, lambda i: (i & 63) * 4 + (i >> 6))
-        lanes = select_columns(
-            512,
-            512,
-            lambda j: ((j >> 8) * 2 + ((j >> 2) & 1)) * 128
-            + ((j >> 3) & 15) * 8
-            + ((j >> 7) & 1) * 4
-            + (j & 3),
-        )
         hist_copy.wait()
-        out = dot(dot(cols, hist_ref[...], ((1,), (1,))).astype(BF), lanes).astype(BF)
+        out = dot(dot(mid_cols, hist_ref[...], ((1,), (1,))).astype(BF), mid_lanes).astype(BF)
         for d in range(16):
             g, q = d // 4, d % 4
             for w in range(4):
@@ -225,6 +225,7 @@
         coarse_copies[g].start()
     mid_count = jnp.int32(0)
     coarse_count = jnp.int32(0)
+    fine_slab = jnp.int32(0)
     for s in range(16):
         kind = kinds_ref[s]
         block = recv_ref[s, 0:64, :]
@@ -232,12 +233,10 @@
         coarse_buf[jnp.where(kind == 2, jnp.minimum(coarse_count, 7), 8)] = block
         mid_count += jnp.where(kind == 1, 1, 0)
         coarse_count += jnp.where(kind == 2, 1, 0)
-
-        @pl.when(kind == 0)
-        def _(block=block):
-            out_ref[128:144, 0:128] = block[0:16]
-            out_ref[128:144, 128:256] = block[16:32]
-
+        fine_slab += jnp.where(kind == 0, s, 0)
+    fine = recv_ref[fine_slab, 0:32, :]
+    out_ref[128:144, 0:128] = fine[0:16]
+    out_ref[128:144, 128:256] = fine[16:32]
     me = lax.axis_index("frame")
     x, y = me & 3, me >> 2
     frames = [((y + d) & 3) * 4 + x for d in range(4)] + [4 * y + i for i in range(4)]
@@ -669,7 +668,33 @@
     )(*gathered[0], *gathered[1], modulation, w_qkv, perm, table)
 
 
-def history_kernel(far1, far2, far3, query_ref, num_ref, den_ref, out0, out1, out2, out3):
+def middle_kernel(far_ref, query_ref, num_ref, den_ref, out_ref, sum_ref):
+    heads = query_ref.shape[0] // HEAD_DIM
+    for h in range(heads):
+        at = slice(HEAD_DIM * h, HEAD_DIM * (h + 1))
+        weights = jnp.exp2(dot(far_ref[0, :, at], query_ref[at, :]))
+        sum_ref[h : h + 1, :] = den_ref[h : h + 1, :] + jnp.sum(weights, axis=0, keepdims=True)
+        out_ref[at, :] = num_ref[at, :] + dot(
+            far_ref[1, :, at], weights.astype(BF), ((0,), (0,))
+        )
+
+
+def attend_first(far, queries, numerator, denominator):
+    return pl.pallas_call(
+        middle_kernel,
+        out_shape=(
+            jax.ShapeDtypeStruct(numerator.shape, F32),
+            jax.ShapeDtypeStruct(denominator.shape, F32),
+        ),
+        in_specs=[VMEM] * 4,
+        out_specs=(VMEM, VMEM),
+        compiler_params=params(),
+        cost_estimate=cost(2e9, 1e6, 1e6),
+        name="first",
+    )(far, queries, numerator, denominator)
+
+
+def history_kernel(far1, far3, query_ref, num_ref, den_ref, out0, out1, out2, out3):
     heads = query_ref.shape[0] // HEAD_DIM
     count = query_ref.shape[1]
     outs = (out0, out1, out2, out3)
@@ -677,7 +702,7 @@
     tail = jnp.zeros((16, count), F32)
     for h in range(heads):
         at = slice(HEAD_DIM * h, HEAD_DIM * (h + 1))
-        fars = (far1, far2, far3)
+        fars = (far1, far3)
         keys = jnp.concatenate([far[0, :, at] for far in fars], axis=0)
         values = jnp.concatenate([far[1, :, at] for far in fars], axis=0)
         weights = jnp.exp2(dot(keys, query_ref[at, :]))
@@ -696,7 +721,7 @@
     return pl.pallas_call(
         history_kernel,
         out_shape=tuple(jax.ShapeDtypeStruct((columns + 16, 128), t) for t in (F32, BF, BF, BF)),
-        in_specs=[VMEM] * 6,
+        in_specs=[VMEM] * 5,
         out_specs=tuple([VMEM] * 4),
         compiler_params=params(),
         cost_estimate=cost(2e9, 4e6, 1e6),
@@ -753,7 +778,8 @@
         slab_kernel, gathered, folded, gram, cosine, sine, times
     )
     numerator, denominator = attend_near(queries, keys, values, far)
-    fars = [far2, far3, far1]
+    numerator, denominator = attend_first(far2, queries, numerator, denominator)
+    fars = [far3, far1]
     parts = attend_history(fars, queries, numerator, denominator)
     part2 = along_y(parts[2], 2)
     return combine([parts[0], along_y(parts[1], 1), part2, along_y(parts[3], 3)])

time: 59 us -> 58.9 us (level)
  waiting for transfers between devices: 12.1 us -> 11.3 us
  Pallas kernels: 15.9 us -> 16.6 us
    pallas_call x0 -> x1, Pallas kernels: none -> 0.75 us  [attend_first(): pl.pallas_call(middle_kernel, out_shape=(jax.ShapeDtypeStruct(numerator.s...]
    ppermute x3, waiting for transfers between devices: 2.22 us -> 1.49 us  [along_x(): lax.ppermute(value, 'frame', [(i, i // 4 * 4 + (i + d) % 4) for i in rang...]
  transfers between devices with their start and end apart: 18 -> 18, of which waited for: 10 -> 10; matrix products, arithmetic and copies ran while one was open for 0% -> 0% of each run, Pallas kernels for 15% -> 16%
where the time goes in v6:
time: 58.9 us; the launch traced here: 58.6 us
  starting transfers between devices  29.4 us (50%)
  Pallas kernels  16.6 us (28%)
  waiting for transfers between devices  11.3 us (19%)
  local copies, waits for them, and re-layouts  1.04 us (2%)
    ppermute x6, starting transfers between devices, along_head(): lax.ppermute(block, 'head', [(i, (i + d) % 4) for i in range(4)])  12.7 us
    all_to_all x1, starting transfers between devices, per_device(): received = lax.all_to_all(sent, 'frame', 0, 0, tiled=True)  7.26 us
    ppermute x6, waiting for transfers between devices, along_head(): lax.ppermute(block, 'head', [(i, (i + d) % 4) for i in range(4)])  5.17 us
    ppermute x3, starting transfers between devices, along_y(): lax.ppermute(value, 'frame', [(i, (i + 4 * d) % 16) for i in range(16)])  4.78 us
    ppermute x3, starting transfers between devices, along_x(): lax.ppermute(value, 'frame', [(i, i // 4 * 4 + (i + d) % 4) for i in rang...  4.13 us
    ppermute x3, waiting for transfers between devices, along_y(): lax.ppermute(value, 'frame', [(i, (i + 4 * d) % 16) for i in range(16)])  4 us
    pallas_call x1, Pallas kernels, embed(): pl.pallas_call(embed_kernel, out_shape=jax.ShapeDtypeStruct((160, patch_m...  2.99 us
    pallas_call x1, Pallas kernels, fold(): pl.pallas_call(fold_kernel, out_shape=(jax.ShapeDtypeStruct((3, 144, colu...  2.31 us
  transfers between devices with their start and end apart: 18, of which 10 were waited for; matrix products, arithmetic and copies ran while one was open for 0% of the time, Pallas kernels for 16%

profile of v6, /device:TPU:0, one launch (start us, length us, event | category | flops | bytes accessed | tf_op | source)
XLA Modules:
  0.0 58.6 jit_solution(14316766695489899452)
XLA Ops:
  0.0 2.3 %prepare.1 = (bf16[16,80,128]{2,1,0:T(8,128)(2,1)}, bf16[64,384]{1,0:T(8,128)(2,1)}) custom-call(s32[16]{0:T(128)} %kinds_ref.5, bf16[512,256]{1,0:T(8,128)(2,1)} %bitcast.4, bf16[64,128]{1,0:T(8,128)(2,1)} %bitcast.5, bf16[64,384]{1,0:T(8,128)(2,1)} %fine_hbm.1), custom_call_target="tpu_custom_call" | custom-call | flops 20000000000 | bytes 1000000 | tf_op jit(solution)/shard_map/prepare/pallas_call | solution.py:183
  2.3 7.3 %all-to-all-start = ((bf16[16,80,128]{2,1,0:T(8,128)(2,1)}), bf16[16,80,128]{2,1,0:T(8,128)(2,1)S(1)}, u32[]{:S(2)}, u32[]{:S(2)}) async-start(bf16[16,80,128]{2,1,0:T(8,128)(2,1)} %get-tuple-element.20.after_ref), calls=%async_computation | async-start | bytes 655360 | tf_op jit(solution)/shard_map/all_to_all | solution.py:767
  9.6 2.0 %collective-permute-start = (bf16[64,384]{1,0:T(8,128)(2,1)}, bf16[64,384]{1,0:T(8,128)(2,1)S(1)}, u32[]{:S(2)}, u32[]{:S(2)}) collective-permute-start(bf16[64,384]{1,0:T(8,128)(2,1)} %get-tuple-element.21.ref0), channel_id=1, source_target_pairs={{0,2},{2,4},{4,6},{6,0},{1,3},{3,5},{5,7},{7,1},{8,10},{10,12},{12... | collective-permute-start | bytes 147464 | tf_op jit(solution)/shard_map/ppermute | solution.py:300
  11.6 3.6 %collective-permute-start.1 = (bf16[64,384]{1,0:T(8,128)(2,1)}, bf16[64,384]{1,0:T(8,128)(2,1)S(1)}, u32[]{:S(2)}, u32[]{:S(2)}) collective-permute-start(bf16[64,384]{1,0:T(8,128)(2,1)} %get-tuple-element.21.ref0), channel_id=1, source_target_pairs={{0,4},{2,6},{4,0},{6,2},{1,5},{3,7},{5,1},{7,3},{8,12},{10,14},{12... | collective-permute-start | bytes 147464 | tf_op jit(solution)/shard_map/ppermute | solution.py:300
  15.2 1.0 %collective-permute-start.2 = (bf16[64,384]{1,0:T(8,128)(2,1)}, bf16[64,384]{1,0:T(8,128)(2,1)S(1)}, u32[]{:S(2)}, u32[]{:S(2)}) collective-permute-start(bf16[64,384]{1,0:T(8,128)(2,1)} %get-tuple-element.21.ref0), channel_id=1, source_target_pairs={{0,6},{2,0},{4,2},{6,4},{1,7},{3,1},{5,3},{7,5},{8,14},{10,8},{12,... | collective-permute-start | bytes 147464 | tf_op jit(solution)/shard_map/ppermute | solution.py:300
  16.2 1.0 %copy-done = bf16[16,80,128]{2,1,0:T(8,128)(2,1)S(1)} copy-done((bf16[16,80,128]{2,1,0:T(8,128)(2,1)S(1)}, bf16[16,80,128]{2,1,0:T(8,128)(2,1)}, u32[]{:S(2)}) %copy-start) | copy-done | bytes 327704
  17.2 1.0 %table.1.table_ref = f32[2,128,128]{2,1,0:T(8,128)S(1)} custom-call(s32[16]{0:T(128)S(1)} %copy-done.4, f32[8,128]{1,0:T(8,128)S(1)} %copy-done.3, bf16[16,80,128]{2,1,0:T(8,128)(2,1)S(1)} %copy-done), custom_call_target="tpu_custom_call" | custom-call | flops 100000 | bytes 1000 | tf_op jit(solution)/shard_map/table/pallas_call | solution.py:612
  18.2 1.3 %collective-permute-done.2.fine3.ref3 = bf16[64,384]{1,0:T(8,128)(2,1)S(1)} collective-permute-done((bf16[64,384]{1,0:T(8,128)(2,1)}, bf16[64,384]{1,0:T(8,128)(2,1)S(1)}, u32[]{:S(2)}, u32[]{:S(2)}) %collective-permute-start.2) | collective-permute-done | bytes 49184 | tf_op jit(solution)/shard_map/ppermute | solution.py:300
  19.5 3.0 %embed.1.mine0.after_ref = bf16[160,384]{1,0:T(8,128)(2,1)S(1)} custom-call(s32[16]{0:T(128)S(1)} %copy-done.4, bf16[16,80,128]{2,1,0:T(8,128)(2,1)S(1)} %all-to-all-done.recv_ref, bf16[512,384]{1,0:T(8,128)(2,1)S(1)} %copy-done.5, bf16[4096,384]{1,0:T(8,128)(2,1)} %coarse_hbm.1, bf16[64,384]{1,0:T(8,128)(2,1)S(1)} %collective-permute-done.fine1.ref1, ...), custom_call_target="tpu_custom_call" | custom-call | flops 2000000000 | bytes 5000000 | tf_op jit(solution)/shard_map/embed/pallas_call | solution.py:281
  22.5 1.5 %collective-permute-start.3 = (bf16[160,384]{1,0:T(8,128)(2,1)S(1)}, bf16[160,384]{1,0:T(8,128)(2,1)S(1)}, u32[]{:S(2)}, u32[]{:S(2)}) collective-permute-start(bf16[160,384]{1,0:T(8,128)(2,1)S(1)} %embed.1.mine0.after_ref), channel_id=1, source_target_pairs={{0,2},{2,4},{4,6},{6,0},{1,3},{3,5},{5,7},{7,1},{8,10},{10,12},{12... | collective-permute-start | bytes 368648 | tf_op jit(solution)/shard_map/ppermute | solution.py:300
  24.0 3.6 %collective-permute-start.4 = (bf16[160,384]{1,0:T(8,128)(2,1)S(1)}, bf16[160,384]{1,0:T(8,128)(2,1)S(1)}, u32[]{:S(2)}, u32[]{:S(2)}) collective-permute-start(bf16[160,384]{1,0:T(8,128)(2,1)S(1)} %embed.1.mine0.after_ref), channel_id=1, source_target_pairs={{0,4},{2,6},{4,0},{6,2},{1,5},{3,7},{5,1},{7,3},{8,12},{10,14},{12... | collective-permute-start | bytes 368648 | tf_op jit(solution)/shard_map/ppermute | solution.py:300
  27.6 1.0 %collective-permute-start.5 = (bf16[160,384]{1,0:T(8,128)(2,1)S(1)}, bf16[160,384]{1,0:T(8,128)(2,1)S(1)}, u32[]{:S(2)}, u32[]{:S(2)}) collective-permute-start(bf16[160,384]{1,0:T(8,128)(2,1)S(1)} %embed.1.mine0.after_ref), channel_id=1, source_target_pairs={{0,6},{2,0},{4,2},{6,4},{1,7},{3,1},{5,3},{7,5},{8,14},{10,8},{12,... | collective-permute-start | bytes 368648 | tf_op jit(solution)/shard_map/ppermute | solution.py:300
  28.6 1.7 %collective-permute-done.3.mine1 = bf16[160,384]{1,0:T(8,128)(2,1)S(1)} collective-permute-done((bf16[160,384]{1,0:T(8,128)(2,1)S(1)}, bf16[160,384]{1,0:T(8,128)(2,1)S(1)}, u32[]{:S(2)}, u32[]{:S(2)}) %collective-permute-start.3) | collective-permute-done | bytes 122912 | tf_op jit(solution)/shard_map/ppermute | solution.py:300
  30.3 1.8 %collective-permute-done.4.mine2 = bf16[160,384]{1,0:T(8,128)(2,1)S(1)} collective-permute-done((bf16[160,384]{1,0:T(8,128)(2,1)S(1)}, bf16[160,384]{1,0:T(8,128)(2,1)S(1)}, u32[]{:S(2)}, u32[]{:S(2)}) %collective-permute-start.4) | collective-permute-done | bytes 122912 | tf_op jit(solution)/shard_map/ppermute | solution.py:300
  33.9 1.6 %far.1.after_ref.far_ref = bf16[2,128,384]{2,1,0:T(8,128)(2,1)S(1)} custom-call(bf16[160,384]{1,0:T(8,128)(2,1)S(1)} %embed.1.mine0.after_ref, bf16[160,384]{1,0:T(8,128)(2,1)S(1)} %collective-permute-done.3.mine1, bf16[160,384]{1,0:T(8,128)(2,1)S(1)} %collective-permute-done.4.mine2, bf16[160,384]{1,0:T(8,128)(2,1)S(1)} %collective-permute-done.5.mine3, ...), custom_call_target="tpu_custom_call" | custom-call | flops 2000000000 | bytes 10000000 | tf_op jit(solution)/shard_map/far/pallas_call | solution.py:659
  35.4 2.1 %collective-permute-start.13 = (bf16[2,128,384]{2,1,0:T(8,128)(2,1)S(1)}, bf16[2,128,384]{2,1,0:T(8,128)(2,1)S(1)}, u32[]{:S(2)}, u32[]{:S(2)}) collective-permute-start(bf16[2,128,384]{2,1,0:T(8,128)(2,1)S(1)} %far.1.after_ref.far_ref), channel_id=1, source_target_pairs={{0,16},{8,24},{16,0},{24,8},{32,48},{40,56},{48,32},{56,40},{64,80... | collective-permute-start | bytes 589832 | tf_op jit(solution)/shard_map/ppermute | solution.py:412
  37.5 1.2 %collective-permute-start.10 = (bf16[2,128,384]{2,1,0:T(8,128)(2,1)S(1)}, bf16[2,128,384]{2,1,0:T(8,128)(2,1)S(1)}, u32[]{:S(2)}, u32[]{:S(2)}) collective-permute-start(bf16[2,128,384]{2,1,0:T(8,128)(2,1)S(1)} %far.1.after_ref.far_ref), channel_id=1, source_target_pairs={{0,24},{8,0},{16,8},{24,16},{32,56},{40,32},{48,40},{56,48},{64,88... | collective-permute-start | bytes 589832 | tf_op jit(solution)/shard_map/ppermute | solution.py:412
  39.6 2.3 %fold.1 = (bf16[3,144,384]{2,1,0:T(8,128)(2,1)S(1)}, f32[64,64]{1,0:T(8,128)S(1)}) custom-call(bf16[4,64,384]{2,1,0:T(8,128)(2,1)S(1)} %stack.1.same_ref, bf16[4,64,384]{2,1,0:T(8,128)(2,1)S(1)} %collective-permute-done.12.other_ref, f32[2,3072]{1,0:T(2,128)S(1)} %copy-done.2, bf16[3,3072,384]{2,1,0:T(8,128)(2,1)S(1)} %bitcast.3, ...), custom_call_target="tpu_custom_call" | custom-call | flops 1000000 | bytes 10000 | tf_op jit(solution)/shard_map/fold/pallas_call | solution.py:396
  41.9 1.9 %tokens.1 = (bf16[384,512]{1,0:T(8,128)(2,1)S(1)}, bf16[384,1024]{1,0:T(8,128)(2,1)S(1)}, bf16[384,1024]{1,0:T(8,128)(2,1)S(1)}) custom-call(s32[16]{0:T(128)S(1)} %copy-done.4, bf16[160,384]{1,0:T(8,128)(2,1)S(1)} %embed.1.mine0.after_ref, bf16[160,384]{1,0:T(8,128)(2,1)S(1)} %collective-permute-done.3.mine1, ...), custom_call_target="tpu_custom_call" | custom-call | flops 2000000000 | bytes 8000000 | tf_op jit(solution)/shard_map/tokens/pallas_call | solution.py:528
  43.8 2.1 %near.1 = (f32[384,512]{1,0:T(8,128)S(1)}, f32[8,512]{1,0:T(8,128)S(1)}) custom-call(bf16[384,512]{1,0:T(8,128)(2,1)S(1)} %get-tuple-element.24.query_ref, bf16[384,1024]{1,0:T(8,128)(2,1)S(1)} %get-tuple-element.25.key_ref, bf16[384,1024]{1,0:T(8,128)(2,1)S(1)} %get-tuple-element.26.value_ref, bf16[2,128,384]{2,1,0:T(8,128)(2,1)S(1)} %far.1.after_ref.far_ref), custom_call_target="tpu_custom_call" | custom-call | flops 4000000000 | bytes 10000000 | tf_op jit(solution)/shard_map/near/pallas_call | solution.py:560
  47.3 0.9 %collective-permute-done.11.far3 = bf16[2,128,384]{2,1,0:T(8,128)(2,1)S(1)} collective-permute-done((bf16[2,128,384]{2,1,0:T(8,128)(2,1)S(1)}, bf16[2,128,384]{2,1,0:T(8,128)(2,1)S(1)}, u32[]{:S(2)}, u32[]{:S(2)}) %collective-permute-start.11) | collective-permute-done | bytes 196640 | tf_op jit(solution)/shard_map/ppermute | solution.py:412
  49.7 2.7 %collective-permute-start.15 = (bf16[400,128]{1,0:T(8,128)(2,1)S(1)}, bf16[400,128]{1,0:T(8,128)(2,1)S(1)}, u32[]{:S(2)}, u32[]{:S(2)}) collective-permute-start(bf16[400,128]{1,0:T(8,128)(2,1)S(1)} %get-tuple-element.33), channel_id=1, source_target_pairs={{0,64},{8,72},{16,80},{24,88},{32,96},{40,104},{48,112},{56,120},{... | collective-permute-start | bytes 307208 | tf_op jit(solution)/shard_map/ppermute | solution.py:416
  52.4 1.5 %collective-permute-start.16 = (bf16[400,128]{1,0:T(8,128)(2,1)S(1)}, bf16[400,128]{1,0:T(8,128)(2,1)S(1)}, u32[]{:S(2)}, u32[]{:S(2)}) collective-permute-start(bf16[400,128]{1,0:T(8,128)(2,1)S(1)} %get-tuple-element.34), channel_id=1, source_target_pairs={{0,96},{8,104},{16,112},{24,120},{32,0},{40,8},{48,16},{56,24},{64... | collective-permute-start | bytes 307208 | tf_op jit(solution)/shard_map/ppermute | solution.py:416
  53.8 3.4 %collective-permute-done.14.part1 = bf16[400,128]{1,0:T(8,128)(2,1)S(1)} collective-permute-done((bf16[400,128]{1,0:T(8,128)(2,1)S(1)}, bf16[400,128]{1,0:T(8,128)(2,1)S(1)}, u32[]{:S(2)}, u32[]{:S(2)}) %collective-permute-start.14) | collective-permute-done | bytes 102432 | tf_op jit(solution)/shard_map/ppermute | solution.py:416
  (48 shorter events, 6.7 us)
Async XLA Ops:
  0.0 16.2 %copy-start.3 = (f32[8,128]{1,0:T(8,128)S(1)}, f32[8,128]{1,0:T(8,128)}, u32[]{:S(2)}) copy-start(f32[8,128]{1,0:T(8,128)} %constant.13.clone.freq_ref) | copy-start | bytes 12292
  0.0 16.2 %copy-start.4 = (s32[16]{0:T(128)S(1)}, s32[16]{0:T(128)}, u32[]{:S(2)}) copy-start(s32[16]{0:T(128)} %kinds_ref.5) | copy-start | bytes 196
  0.0 19.5 %copy-start.5 = (bf16[512,384]{1,0:T(8,128)(2,1)S(1)}, bf16[512,384]{1,0:T(8,128)(2,1)}, u32[]{:S(2)}) copy-start(bf16[512,384]{1,0:T(8,128)(2,1)} %mid_ref.1) | copy-start | bytes 1179652
  2.3 30.3 %copy-start.6 = (bf16[64,384]{1,0:T(8,128)(2,1)S(1)}, bf16[64,384]{1,0:T(8,128)(2,1)}, u32[]{:S(2)}) copy-start(bf16[64,384]{1,0:T(8,128)(2,1)} %get-tuple-element.21.ref0) | copy-start | bytes 147460
  2.3 17.1 %all-to-all-start = ((bf16[16,80,128]{2,1,0:T(8,128)(2,1)}), bf16[16,80,128]{2,1,0:T(8,128)(2,1)S(1)}, u32[]{:S(2)}, u32[]{:S(2)}) async-start(bf16[16,80,128]{2,1,0:T(8,128)(2,1)} %get-tuple-element.20.after_ref), calls=%async_computation | async-start | bytes 655360 | tf_op jit(solution)/shard_map/all_to_all | solution.py:767
  9.6 8.6 %collective-permute-start = (bf16[64,384]{1,0:T(8,128)(2,1)}, bf16[64,384]{1,0:T(8,128)(2,1)S(1)}, u32[]{:S(2)}, u32[]{:S(2)}) collective-permute-start(bf16[64,384]{1,0:T(8,128)(2,1)} %get-tuple-element.21.ref0), channel_id=1, source_target_pairs={{0,2},{2,4},{4,6},{6,0},{1,3},{3,5},{5,7},{7,1},{8,10},{10,12},{12... | collective-permute-start | bytes 147464 | tf_op jit(solution)/shard_map/ppermute | solution.py:300
  11.6 6.6 %collective-permute-start.1 = (bf16[64,384]{1,0:T(8,128)(2,1)}, bf16[64,384]{1,0:T(8,128)(2,1)S(1)}, u32[]{:S(2)}, u32[]{:S(2)}) collective-permute-start(bf16[64,384]{1,0:T(8,128)(2,1)} %get-tuple-element.21.ref0), channel_id=1, source_target_pairs={{0,4},{2,6},{4,0},{6,2},{1,5},{3,7},{5,1},{7,3},{8,12},{10,14},{12... | collective-permute-start | bytes 147464 | tf_op jit(solution)/shard_map/ppermute | solution.py:300
  15.2 4.3 %collective-permute-start.2 = (bf16[64,384]{1,0:T(8,128)(2,1)}, bf16[64,384]{1,0:T(8,128)(2,1)S(1)}, u32[]{:S(2)}, u32[]{:S(2)}) collective-permute-start(bf16[64,384]{1,0:T(8,128)(2,1)} %get-tuple-element.21.ref0), channel_id=1, source_target_pairs={{0,6},{2,0},{4,2},{6,4},{1,7},{3,1},{5,3},{7,5},{8,14},{10,8},{12,... | collective-permute-start | bytes 147464 | tf_op jit(solution)/shard_map/ppermute | solution.py:300
  19.5 14.3 %slice-start = ((s8[7077888]{0:T(1024)(128)(4,1)}), s8[2883584]{0:T(1024)(128)(4,1)S(1)}, s32[]{:S(2)}) async-start(s8[7077888]{0:T(1024)(128)(4,1)} %bitcast.2), calls=%async_computation.1 | async-start | bytes 5767168
  22.5 11.3 %slice-start.1 = ((s8[7077888]{0:T(1024)(128)(4,1)}), s8[4194304]{0:T(1024)(128)(4,1)S(1)}, s32[]{:S(2)}) async-start(s8[7077888]{0:T(1024)(128)(4,1)} %bitcast.2), calls=%async_computation.2 | async-start | bytes 8388608
  22.5 7.8 %collective-permute-start.3 = (bf16[160,384]{1,0:T(8,128)(2,1)S(1)}, bf16[160,384]{1,0:T(8,128)(2,1)S(1)}, u32[]{:S(2)}, u32[]{:S(2)}) collective-permute-start(bf16[160,384]{1,0:T(8,128)(2,1)S(1)} %embed.1.mine0.after_ref), channel_id=1, source_target_pairs={{0,2},{2,4},{4,6},{6,0},{1,3},{3,5},{5,7},{7,1},{8,10},{10,12},{12... | collective-permute-start | bytes 368648 | tf_op jit(solution)/shard_map/ppermute | solution.py:300
  24.0 8.1 %collective-permute-start.4 = (bf16[160,384]{1,0:T(8,128)(2,1)S(1)}, bf16[160,384]{1,0:T(8,128)(2,1)S(1)}, u32[]{:S(2)}, u32[]{:S(2)}) collective-permute-start(bf16[160,384]{1,0:T(8,128)(2,1)S(1)} %embed.1.mine0.after_ref), channel_id=1, source_target_pairs={{0,4},{2,6},{4,0},{6,2},{1,5},{3,7},{5,1},{7,3},{8,12},{10,14},{12... | collective-permute-start | bytes 368648 | tf_op jit(solution)/shard_map/ppermute | solution.py:300
  27.6 4.9 %collective-permute-start.5 = (bf16[160,384]{1,0:T(8,128)(2,1)S(1)}, bf16[160,384]{1,0:T(8,128)(2,1)S(1)}, u32[]{:S(2)}, u32[]{:S(2)}) collective-permute-start(bf16[160,384]{1,0:T(8,128)(2,1)S(1)} %embed.1.mine0.after_ref), channel_id=1, source_target_pairs={{0,6},{2,0},{4,2},{6,4},{1,7},{3,1},{5,3},{7,5},{8,14},{10,8},{12,... | collective-permute-start | bytes 368648 | tf_op jit(solution)/shard_map/ppermute | solution.py:300
  28.6 4.5 %collective-permute-start.6 = (bf16[160,384]{1,0:T(8,128)(2,1)S(1)}, bf16[160,384]{1,0:T(8,128)(2,1)S(1)}, u32[]{:S(2)}, u32[]{:S(2)}) collective-permute-start(bf16[160,384]{1,0:T(8,128)(2,1)S(1)} %embed.1.mine0.after_ref), channel_id=1, source_target_pairs={{0,1},{1,0},{2,3},{3,2},{4,5},{5,4},{6,7},{7,6},{8,9},{9,8},{10,11... | collective-permute-start | bytes 368648 | tf_op jit(solution)/shard_map/ppermute | solution.py:306
  30.3 2.8 %collective-permute-start.7 = (bf16[160,384]{1,0:T(8,128)(2,1)S(1)}, bf16[160,384]{1,0:T(8,128)(2,1)S(1)}, u32[]{:S(2)}, u32[]{:S(2)}) collective-permute-start(bf16[160,384]{1,0:T(8,128)(2,1)S(1)} %collective-permute-done.3.mine1), channel_id=1, source_target_pairs={{0,1},{1,0},{2,3},{3,2},{4,5},{5,4},{6,7},{7,6},{8,9},{9,8},{10,11... | collective-permute-start | bytes 368648 | tf_op jit(solution)/shard_map/ppermute | solution.py:306
  32.1 1.3 %collective-permute-start.8 = (bf16[160,384]{1,0:T(8,128)(2,1)S(1)}, bf16[160,384]{1,0:T(8,128)(2,1)S(1)}, u32[]{:S(2)}, u32[]{:S(2)}) collective-permute-start(bf16[160,384]{1,0:T(8,128)(2,1)S(1)} %collective-permute-done.4.mine2), channel_id=1, source_target_pairs={{0,1},{1,0},{2,3},{3,2},{4,5},{5,4},{6,7},{7,6},{8,9},{9,8},{10,11... | collective-permute-start | bytes 368648 | tf_op jit(solution)/shard_map/ppermute | solution.py:306
  32.5 1.3 %collective-permute-start.9 = (bf16[160,384]{1,0:T(8,128)(2,1)S(1)}, bf16[160,384]{1,0:T(8,128)(2,1)S(1)}, u32[]{:S(2)}, u32[]{:S(2)}) collective-permute-start(bf16[160,384]{1,0:T(8,128)(2,1)S(1)} %collective-permute-done.5.mine3), channel_id=1, source_target_pairs={{0,1},{1,0},{2,3},{3,2},{4,5},{5,4},{6,7},{7,6},{8,9},{9,8},{10,11... | collective-permute-start | bytes 368648 | tf_op jit(solution)/shard_map/ppermute | solution.py:306
  32.7 6.9 %collective-permute-start.12 = (bf16[4,64,384]{2,1,0:T(8,128)(2,1)S(1)}, bf16[4,64,384]{2,1,0:T(8,128)(2,1)S(1)}, u32[]{:S(2)}, u32[]{:S(2)}) collective-permute-start(bf16[4,64,384]{2,1,0:T(8,128)(2,1)S(1)} %stack.1.same_ref), channel_id=1, source_target_pairs={{0,1},{1,0},{2,3},{3,2},{4,5},{5,4},{6,7},{7,6},{8,9},{9,8},{10,11... | collective-permute-start | bytes 589832 | tf_op jit(solution)/shard_map/ppermute | solution.py:306
  35.4 10.5 %collective-permute-start.13 = (bf16[2,128,384]{2,1,0:T(8,128)(2,1)S(1)}, bf16[2,128,384]{2,1,0:T(8,128)(2,1)S(1)}, u32[]{:S(2)}, u32[]{:S(2)}) collective-permute-start(bf16[2,128,384]{2,1,0:T(8,128)(2,1)S(1)} %far.1.after_ref.far_ref), channel_id=1, source_target_pairs={{0,16},{8,24},{16,0},{24,8},{32,48},{40,56},{48,32},{56,40},{64,80... | collective-permute-start | bytes 589832 | tf_op jit(solution)/shard_map/ppermute | solution.py:412
  37.5 9.7 %collective-permute-start.10 = (bf16[2,128,384]{2,1,0:T(8,128)(2,1)S(1)}, bf16[2,128,384]{2,1,0:T(8,128)(2,1)S(1)}, u32[]{:S(2)}, u32[]{:S(2)}) collective-permute-start(bf16[2,128,384]{2,1,0:T(8,128)(2,1)S(1)} %far.1.after_ref.far_ref), channel_id=1, source_target_pairs={{0,24},{8,0},{16,8},{24,16},{32,56},{40,32},{48,40},{56,48},{64,88... | collective-permute-start | bytes 589832 | tf_op jit(solution)/shard_map/ppermute | solution.py:412
  38.7 9.4 %collective-permute-start.11 = (bf16[2,128,384]{2,1,0:T(8,128)(2,1)S(1)}, bf16[2,128,384]{2,1,0:T(8,128)(2,1)S(1)}, u32[]{:S(2)}, u32[]{:S(2)}) collective-permute-start(bf16[2,128,384]{2,1,0:T(8,128)(2,1)S(1)} %far.1.after_ref.far_ref), channel_id=1, source_target_pairs={{0,8},{8,16},{16,24},{24,0},{32,40},{40,48},{48,56},{56,32},{64,72... | collective-permute-start | bytes 589832 | tf_op jit(solution)/shard_map/ppermute | solution.py:412
  49.0 8.2 %collective-permute-start.14 = (bf16[400,128]{1,0:T(8,128)(2,1)S(1)}, bf16[400,128]{1,0:T(8,128)(2,1)S(1)}, u32[]{:S(2)}, u32[]{:S(2)}) collective-permute-start(bf16[400,128]{1,0:T(8,128)(2,1)S(1)} %get-tuple-element.32), channel_id=1, source_target_pairs={{0,32},{8,40},{16,48},{24,56},{32,64},{40,72},{48,80},{56,88},{64,... | collective-permute-start | bytes 307208 | tf_op jit(solution)/shard_map/ppermute | solution.py:416
  49.7 7.6 %collective-permute-start.15 = (bf16[400,128]{1,0:T(8,128)(2,1)S(1)}, bf16[400,128]{1,0:T(8,128)(2,1)S(1)}, u32[]{:S(2)}, u32[]{:S(2)}) collective-permute-start(bf16[400,128]{1,0:T(8,128)(2,1)S(1)} %get-tuple-element.33), channel_id=1, source_target_pairs={{0,64},{8,72},{16,80},{24,88},{32,96},{40,104},{48,112},{56,120},{... | collective-permute-start | bytes 307208 | tf_op jit(solution)/shard_map/ppermute | solution.py:416
  52.4 5.5 %collective-permute-start.16 = (bf16[400,128]{1,0:T(8,128)(2,1)S(1)}, bf16[400,128]{1,0:T(8,128)(2,1)S(1)}, u32[]{:S(2)}, u32[]{:S(2)}) collective-permute-start(bf16[400,128]{1,0:T(8,128)(2,1)S(1)} %get-tuple-element.34), channel_id=1, source_target_pairs={{0,96},{8,104},{16,112},{24,120},{32,0},{40,8},{48,16},{56,24},{64... | collective-permute-start | bytes 307208 | tf_op jit(solution)/shard_map/ppermute | solution.py:416
  (6 other events, 51.3 us)

commit v7 on v6

--- a/solution.py
+++ b/solution.py
@@ -694,7 +694,7 @@
     )(far, queries, numerator, denominator)
 
 
-def history_kernel(far1, far3, query_ref, num_ref, den_ref, out0, out1, out2, out3):
+def history_kernel(far1, query_ref, num_ref, den_ref, out0, out1, out2, out3):
     heads = query_ref.shape[0] // HEAD_DIM
     count = query_ref.shape[1]
     outs = (out0, out1, out2, out3)
@@ -702,7 +702,7 @@
     tail = jnp.zeros((16, count), F32)
     for h in range(heads):
         at = slice(HEAD_DIM * h, HEAD_DIM * (h + 1))
-        fars = (far1, far3)
+        fars = (far1,)
         keys = jnp.concatenate([far[0, :, at] for far in fars], axis=0)
         values = jnp.concatenate([far[1, :, at] for far in fars], axis=0)
         weights = jnp.exp2(dot(keys, query_ref[at, :]))
@@ -721,7 +721,7 @@
     return pl.pallas_call(
         history_kernel,
         out_shape=tuple(jax.ShapeDtypeStruct((columns + 16, 128), t) for t in (F32, BF, BF, BF)),
-        in_specs=[VMEM] * 5,
+        in_specs=[VMEM] * 4,
         out_specs=tuple([VMEM] * 4),
         compiler_params=params(),
         cost_estimate=cost(2e9, 4e6, 1e6),
@@ -779,7 +779,8 @@
     )
     numerator, denominator = attend_near(queries, keys, values, far)
     numerator, denominator = attend_first(far2, queries, numerator, denominator)
-    fars = [far3, far1]
+    numerator, denominator = attend_first(far3, queries, numerator, denominator)
+    fars = [far1]
     parts = attend_history(fars, queries, numerator, denominator)
     part2 = along_y(parts[2], 2)
     return combine([parts[0], along_y(parts[1], 1), part2, along_y(parts[3], 3)])

time: 58.9 us -> 58.9 us (level)
  waiting for transfers between devices: 11.3 us -> 9.84 us
  starting transfers between devices: 29.4 us -> 30.3 us
    ppermute x3, starting transfers between devices: 4.78 us -> 5.54 us  [along_y(): lax.ppermute(value, 'frame', [(i, (i + 4 * d) % 16) for i in range(16)])]
    ppermute x3, waiting for transfers between devices: 4 us -> 3.24 us  [along_y(): lax.ppermute(value, 'frame', [(i, (i + 4 * d) % 16) for i in range(16)])]
    ppermute x3, waiting for transfers between devices: 1.49 us -> 0.74 us  [along_x(): lax.ppermute(value, 'frame', [(i, i // 4 * 4 + (i + d) % 4) for i in rang...]
    pallas_call x1 -> x2, Pallas kernels: 0.75 us -> 1.5 us  [attend_first(): pl.pallas_call(middle_kernel, out_shape=(jax.ShapeDtypeStruct(numerator.s...]
  transfers between devices with their start and end apart: 18 -> 18, of which waited for: 10 -> 11; matrix products, arithmetic and copies ran while one was open for 0% -> 0% of each run, Pallas kernels for 16% -> 18%
where the time goes in v7:
time: 58.9 us; the launch traced here: 58.5 us
  starting transfers between devices  30.3 us (51%)
  Pallas kernels  17.1 us (29%)
  waiting for transfers between devices  9.84 us (17%)
  local copies, waits for them, and re-layouts  1.04 us (2%)
    ppermute x6, starting transfers between devices, along_head(): lax.ppermute(block, 'head', [(i, (i + d) % 4) for i in range(4)])  12.7 us
    all_to_all x1, starting transfers between devices, per_device(): received = lax.all_to_all(sent, 'frame', 0, 0, tiled=True)  7.36 us
    ppermute x3, starting transfers between devices, along_y(): lax.ppermute(value, 'frame', [(i, (i + 4 * d) % 16) for i in range(16)])  5.54 us
    ppermute x6, waiting for transfers between devices, along_head(): lax.ppermute(block, 'head', [(i, (i + d) % 4) for i in range(4)])  5.17 us
    ppermute x3, starting transfers between devices, along_x(): lax.ppermute(value, 'frame', [(i, i // 4 * 4 + (i + d) % 4) for i in rang...  4.13 us
    ppermute x3, waiting for transfers between devices, along_y(): lax.ppermute(value, 'frame', [(i, (i + 4 * d) % 16) for i in range(16)])  3.24 us
    pallas_call x1, Pallas kernels, embed(): pl.pallas_call(embed_kernel, out_shape=jax.ShapeDtypeStruct((160, patch_m...  2.99 us
    pallas_call x1, Pallas kernels, fold(): pl.pallas_call(fold_kernel, out_shape=(jax.ShapeDtypeStruct((3, 144, colu...  2.31 us
  transfers between devices with their start and end apart: 18, of which 11 were waited for; matrix products, arithmetic and copies ran while one was open for 0% of the time, Pallas kernels for 18%

profile of v7, /device:TPU:0, one launch (start us, length us, event | category | flops | bytes accessed | tf_op | source)
XLA Modules:
  0.0 58.5 jit_solution(5083478213010788158)
XLA Ops:
  0.0 2.2 %prepare.1 = (bf16[16,80,128]{2,1,0:T(8,128)(2,1)}, bf16[64,384]{1,0:T(8,128)(2,1)}) custom-call(s32[16]{0:T(128)} %kinds_ref.5, bf16[512,256]{1,0:T(8,128)(2,1)} %bitcast.4, bf16[64,128]{1,0:T(8,128)(2,1)} %bitcast.5, bf16[64,384]{1,0:T(8,128)(2,1)} %fine_hbm.1), custom_call_target="tpu_custom_call" | custom-call | flops 20000000000 | bytes 1000000 | tf_op jit(solution)/shard_map/prepare/pallas_call | solution.py:183
  2.2 7.4 %all-to-all-start = ((bf16[16,80,128]{2,1,0:T(8,128)(2,1)}), bf16[16,80,128]{2,1,0:T(8,128)(2,1)S(1)}, u32[]{:S(2)}, u32[]{:S(2)}) async-start(bf16[16,80,128]{2,1,0:T(8,128)(2,1)} %get-tuple-element.22.after_ref), calls=%async_computation | async-start | bytes 655360 | tf_op jit(solution)/shard_map/all_to_all | solution.py:767
  9.6 2.0 %collective-permute-start = (bf16[64,384]{1,0:T(8,128)(2,1)}, bf16[64,384]{1,0:T(8,128)(2,1)S(1)}, u32[]{:S(2)}, u32[]{:S(2)}) collective-permute-start(bf16[64,384]{1,0:T(8,128)(2,1)} %get-tuple-element.23.ref0), channel_id=1, source_target_pairs={{0,2},{2,4},{4,6},{6,0},{1,3},{3,5},{5,7},{7,1},{8,10},{10,12},{12... | collective-permute-start | bytes 147464 | tf_op jit(solution)/shard_map/ppermute | solution.py:300
  11.6 3.6 %collective-permute-start.1 = (bf16[64,384]{1,0:T(8,128)(2,1)}, bf16[64,384]{1,0:T(8,128)(2,1)S(1)}, u32[]{:S(2)}, u32[]{:S(2)}) collective-permute-start(bf16[64,384]{1,0:T(8,128)(2,1)} %get-tuple-element.23.ref0), channel_id=1, source_target_pairs={{0,4},{2,6},{4,0},{6,2},{1,5},{3,7},{5,1},{7,3},{8,12},{10,14},{12... | collective-permute-start | bytes 147464 | tf_op jit(solution)/shard_map/ppermute | solution.py:300
  15.2 1.0 %collective-permute-start.2 = (bf16[64,384]{1,0:T(8,128)(2,1)}, bf16[64,384]{1,0:T(8,128)(2,1)S(1)}, u32[]{:S(2)}, u32[]{:S(2)}) collective-permute-start(bf16[64,384]{1,0:T(8,128)(2,1)} %get-tuple-element.23.ref0), channel_id=1, source_target_pairs={{0,6},{2,0},{4,2},{6,4},{1,7},{3,1},{5,3},{7,5},{8,14},{10,8},{12,... | collective-permute-start | bytes 147464 | tf_op jit(solution)/shard_map/ppermute | solution.py:300
  17.2 1.0 %table.1.table_ref = f32[2,128,128]{2,1,0:T(8,128)S(1)} custom-call(s32[16]{0:T(128)S(1)} %copy-done.4, f32[8,128]{1,0:T(8,128)S(1)} %copy-done.3, bf16[16,80,128]{2,1,0:T(8,128)(2,1)S(1)} %copy-done), custom_call_target="tpu_custom_call" | custom-call | flops 100000 | bytes 1000 | tf_op jit(solution)/shard_map/table/pallas_call | solution.py:612
  18.2 1.3 %collective-permute-done.2.fine3.ref3 = bf16[64,384]{1,0:T(8,128)(2,1)S(1)} collective-permute-done((bf16[64,384]{1,0:T(8,128)(2,1)}, bf16[64,384]{1,0:T(8,128)(2,1)S(1)}, u32[]{:S(2)}, u32[]{:S(2)}) %collective-permute-start.2) | collective-permute-done | bytes 49184 | tf_op jit(solution)/shard_map/ppermute | solution.py:300
  19.5 3.0 %embed.1.mine0.after_ref = bf16[160,384]{1,0:T(8,128)(2,1)S(1)} custom-call(s32[16]{0:T(128)S(1)} %copy-done.4, bf16[16,80,128]{2,1,0:T(8,128)(2,1)S(1)} %all-to-all-done.recv_ref, bf16[512,384]{1,0:T(8,128)(2,1)S(1)} %copy-done.5, bf16[4096,384]{1,0:T(8,128)(2,1)} %coarse_hbm.1, bf16[64,384]{1,0:T(8,128)(2,1)S(1)} %collective-permute-done.fine1.ref1, ...), custom_call_target="tpu_custom_call" | custom-call | flops 2000000000 | bytes 5000000 | tf_op jit(solution)/shard_map/embed/pallas_call | solution.py:281
  22.5 1.5 %collective-permute-start.3 = (bf16[160,384]{1,0:T(8,128)(2,1)S(1)}, bf16[160,384]{1,0:T(8,128)(2,1)S(1)}, u32[]{:S(2)}, u32[]{:S(2)}) collective-permute-start(bf16[160,384]{1,0:T(8,128)(2,1)S(1)} %embed.1.mine0.after_ref), channel_id=1, source_target_pairs={{0,2},{2,4},{4,6},{6,0},{1,3},{3,5},{5,7},{7,1},{8,10},{10,12},{12... | collective-permute-start | bytes 368648 | tf_op jit(solution)/shard_map/ppermute | solution.py:300
  24.0 3.6 %collective-permute-start.4 = (bf16[160,384]{1,0:T(8,128)(2,1)S(1)}, bf16[160,384]{1,0:T(8,128)(2,1)S(1)}, u32[]{:S(2)}, u32[]{:S(2)}) collective-permute-start(bf16[160,384]{1,0:T(8,128)(2,1)S(1)} %embed.1.mine0.after_ref), channel_id=1, source_target_pairs={{0,4},{2,6},{4,0},{6,2},{1,5},{3,7},{5,1},{7,3},{8,12},{10,14},{12... | collective-permute-start | bytes 368648 | tf_op jit(solution)/shard_map/ppermute | solution.py:300
  27.6 1.0 %collective-permute-start.5 = (bf16[160,384]{1,0:T(8,128)(2,1)S(1)}, bf16[160,384]{1,0:T(8,128)(2,1)S(1)}, u32[]{:S(2)}, u32[]{:S(2)}) collective-permute-start(bf16[160,384]{1,0:T(8,128)(2,1)S(1)} %embed.1.mine0.after_ref), channel_id=1, source_target_pairs={{0,6},{2,0},{4,2},{6,4},{1,7},{3,1},{5,3},{7,5},{8,14},{10,8},{12,... | collective-permute-start | bytes 368648 | tf_op jit(solution)/shard_map/ppermute | solution.py:300
  28.6 1.7 %collective-permute-done.3.mine1 = bf16[160,384]{1,0:T(8,128)(2,1)S(1)} collective-permute-done((bf16[160,384]{1,0:T(8,128)(2,1)S(1)}, bf16[160,384]{1,0:T(8,128)(2,1)S(1)}, u32[]{:S(2)}, u32[]{:S(2)}) %collective-permute-start.3) | collective-permute-done | bytes 122912 | tf_op jit(solution)/shard_map/ppermute | solution.py:300
  30.3 1.8 %collective-permute-done.4.mine2 = bf16[160,384]{1,0:T(8,128)(2,1)S(1)} collective-permute-done((bf16[160,384]{1,0:T(8,128)(2,1)S(1)}, bf16[160,384]{1,0:T(8,128)(2,1)S(1)}, u32[]{:S(2)}, u32[]{:S(2)}) %collective-permute-start.4) | collective-permute-done | bytes 122912 | tf_op jit(solution)/shard_map/ppermute | solution.py:300
  33.9 1.6 %far.1.after_ref.far_ref = bf16[2,128,384]{2,1,0:T(8,128)(2,1)S(1)} custom-call(bf16[160,384]{1,0:T(8,128)(2,1)S(1)} %embed.1.mine0.after_ref, bf16[160,384]{1,0:T(8,128)(2,1)S(1)} %collective-permute-done.3.mine1, bf16[160,384]{1,0:T(8,128)(2,1)S(1)} %collective-permute-done.4.mine2, bf16[160,384]{1,0:T(8,128)(2,1)S(1)} %collective-permute-done.5.mine3, ...), custom_call_target="tpu_custom_call" | custom-call | flops 2000000000 | bytes 10000000 | tf_op jit(solution)/shard_map/far/pallas_call | solution.py:659
  35.4 2.1 %collective-permute-start.13 = (bf16[2,128,384]{2,1,0:T(8,128)(2,1)S(1)}, bf16[2,128,384]{2,1,0:T(8,128)(2,1)S(1)}, u32[]{:S(2)}, u32[]{:S(2)}) collective-permute-start(bf16[2,128,384]{2,1,0:T(8,128)(2,1)S(1)} %far.1.after_ref.far_ref), channel_id=1, source_target_pairs={{0,16},{8,24},{16,0},{24,8},{32,48},{40,56},{48,32},{56,40},{64,80... | collective-permute-start | bytes 589832 | tf_op jit(solution)/shard_map/ppermute | solution.py:412
  37.5 1.2 %collective-permute-start.12 = (bf16[2,128,384]{2,1,0:T(8,128)(2,1)S(1)}, bf16[2,128,384]{2,1,0:T(8,128)(2,1)S(1)}, u32[]{:S(2)}, u32[]{:S(2)}) collective-permute-start(bf16[2,128,384]{2,1,0:T(8,128)(2,1)S(1)} %far.1.after_ref.far_ref), channel_id=1, source_target_pairs={{0,24},{8,0},{16,8},{24,16},{32,56},{40,32},{48,40},{56,48},{64,88... | collective-permute-start | bytes 589832 | tf_op jit(solution)/shard_map/ppermute | solution.py:412
  39.6 2.3 %fold.1 = (bf16[3,144,384]{2,1,0:T(8,128)(2,1)S(1)}, f32[64,64]{1,0:T(8,128)S(1)}) custom-call(bf16[4,64,384]{2,1,0:T(8,128)(2,1)S(1)} %stack.1.same_ref, bf16[4,64,384]{2,1,0:T(8,128)(2,1)S(1)} %collective-permute-done.11.other_ref, f32[2,3072]{1,0:T(2,128)S(1)} %copy-done.2, bf16[3,3072,384]{2,1,0:T(8,128)(2,1)S(1)} %bitcast.3, ...), custom_call_target="tpu_custom_call" | custom-call | flops 1000000 | bytes 10000 | tf_op jit(solution)/shard_map/fold/pallas_call | solution.py:396
  41.9 1.9 %tokens.1 = (bf16[384,512]{1,0:T(8,128)(2,1)S(1)}, bf16[384,1024]{1,0:T(8,128)(2,1)S(1)}, bf16[384,1024]{1,0:T(8,128)(2,1)S(1)}) custom-call(s32[16]{0:T(128)S(1)} %copy-done.4, bf16[160,384]{1,0:T(8,128)(2,1)S(1)} %embed.1.mine0.after_ref, bf16[160,384]{1,0:T(8,128)(2,1)S(1)} %collective-permute-done.3.mine1, ...), custom_call_target="tpu_custom_call" | custom-call | flops 2000000000 | bytes 8000000 | tf_op jit(solution)/shard_map/tokens/pallas_call | solution.py:528
  43.8 2.1 %near.1 = (f32[384,512]{1,0:T(8,128)S(1)}, f32[8,512]{1,0:T(8,128)S(1)}) custom-call(bf16[384,512]{1,0:T(8,128)(2,1)S(1)} %get-tuple-element.26.query_ref, bf16[384,1024]{1,0:T(8,128)(2,1)S(1)} %get-tuple-element.27.key_ref, bf16[384,1024]{1,0:T(8,128)(2,1)S(1)} %get-tuple-element.28.value_ref, bf16[2,128,384]{2,1,0:T(8,128)(2,1)S(1)} %far.1.after_ref.far_ref), custom_call_target="tpu_custom_call" | custom-call | flops 4000000000 | bytes 10000000 | tf_op jit(solution)/shard_map/near/pallas_call | solution.py:560
  48.9 1.4 %collective-permute-start.14 = (bf16[400,128]{1,0:T(8,128)(2,1)S(1)}, bf16[400,128]{1,0:T(8,128)(2,1)S(1)}, u32[]{:S(2)}, u32[]{:S(2)}) collective-permute-start(bf16[400,128]{1,0:T(8,128)(2,1)S(1)} %get-tuple-element.36), channel_id=1, source_target_pairs={{0,32},{8,40},{16,48},{24,56},{32,64},{40,72},{48,80},{56,88},{64,... | collective-permute-start | bytes 307208 | tf_op jit(solution)/shard_map/ppermute | solution.py:416
  50.3 2.7 %collective-permute-start.15 = (bf16[400,128]{1,0:T(8,128)(2,1)S(1)}, bf16[400,128]{1,0:T(8,128)(2,1)S(1)}, u32[]{:S(2)}, u32[]{:S(2)}) collective-permute-start(bf16[400,128]{1,0:T(8,128)(2,1)S(1)} %get-tuple-element.37), channel_id=1, source_target_pairs={{0,64},{8,72},{16,80},{24,88},{32,96},{40,104},{48,112},{56,120},{... | collective-permute-start | bytes 307208 | tf_op jit(solution)/shard_map/ppermute | solution.py:416
  53.0 1.5 %collective-permute-start.16 = (bf16[400,128]{1,0:T(8,128)(2,1)S(1)}, bf16[400,128]{1,0:T(8,128)(2,1)S(1)}, u32[]{:S(2)}, u32[]{:S(2)}) collective-permute-start(bf16[400,128]{1,0:T(8,128)(2,1)S(1)} %get-tuple-element.38), channel_id=1, source_target_pairs={{0,96},{8,104},{16,112},{24,120},{32,0},{40,8},{48,16},{56,24},{64... | collective-permute-start | bytes 307208 | tf_op jit(solution)/shard_map/ppermute | solution.py:416
  54.5 1.6 %collective-permute-done.14.part1 = bf16[400,128]{1,0:T(8,128)(2,1)S(1)} collective-permute-done((bf16[400,128]{1,0:T(8,128)(2,1)S(1)}, bf16[400,128]{1,0:T(8,128)(2,1)S(1)}, u32[]{:S(2)}, u32[]{:S(2)}) %collective-permute-start.14) | collective-permute-done | bytes 102432 | tf_op jit(solution)/shard_map/ppermute | solution.py:416
  56.1 1.2 %collective-permute-done.15.part2 = bf16[400,128]{1,0:T(8,128)(2,1)S(1)} collective-permute-done((bf16[400,128]{1,0:T(8,128)(2,1)S(1)}, bf16[400,128]{1,0:T(8,128)(2,1)S(1)}, u32[]{:S(2)}, u32[]{:S(2)}) %collective-permute-start.15) | collective-permute-done | bytes 102432 | tf_op jit(solution)/shard_map/ppermute | solution.py:416
  (49 shorter events, 7.7 us)
Async XLA Ops:
  0.0 16.2 %copy-start.3 = (f32[8,128]{1,0:T(8,128)S(1)}, f32[8,128]{1,0:T(8,128)}, u32[]{:S(2)}) copy-start(f32[8,128]{1,0:T(8,128)} %constant.13.clone.freq_ref) | copy-start | bytes 12292
  0.0 16.2 %copy-start.4 = (s32[16]{0:T(128)S(1)}, s32[16]{0:T(128)}, u32[]{:S(2)}) copy-start(s32[16]{0:T(128)} %kinds_ref.5) | copy-start | bytes 196
  0.0 19.5 %copy-start.5 = (bf16[512,384]{1,0:T(8,128)(2,1)S(1)}, bf16[512,384]{1,0:T(8,128)(2,1)}, u32[]{:S(2)}) copy-start(bf16[512,384]{1,0:T(8,128)(2,1)} %mid_ref.1) | copy-start | bytes 1179652
  2.2 30.4 %copy-start.6 = (bf16[64,384]{1,0:T(8,128)(2,1)S(1)}, bf16[64,384]{1,0:T(8,128)(2,1)}, u32[]{:S(2)}) copy-start(bf16[64,384]{1,0:T(8,128)(2,1)} %get-tuple-element.23.ref0) | copy-start | bytes 147460
  2.2 17.3 %all-to-all-start = ((bf16[16,80,128]{2,1,0:T(8,128)(2,1)}), bf16[16,80,128]{2,1,0:T(8,128)(2,1)S(1)}, u32[]{:S(2)}, u32[]{:S(2)}) async-start(bf16[16,80,128]{2,1,0:T(8,128)(2,1)} %get-tuple-element.22.after_ref), calls=%async_computation | async-start | bytes 655360 | tf_op jit(solution)/shard_map/all_to_all | solution.py:767
  9.6 8.6 %collective-permute-start = (bf16[64,384]{1,0:T(8,128)(2,1)}, bf16[64,384]{1,0:T(8,128)(2,1)S(1)}, u32[]{:S(2)}, u32[]{:S(2)}) collective-permute-start(bf16[64,384]{1,0:T(8,128)(2,1)} %get-tuple-element.23.ref0), channel_id=1, source_target_pairs={{0,2},{2,4},{4,6},{6,0},{1,3},{3,5},{5,7},{7,1},{8,10},{10,12},{12... | collective-permute-start | bytes 147464 | tf_op jit(solution)/shard_map/ppermute | solution.py:300
  11.6 6.6 %collective-permute-start.1 = (bf16[64,384]{1,0:T(8,128)(2,1)}, bf16[64,384]{1,0:T(8,128)(2,1)S(1)}, u32[]{:S(2)}, u32[]{:S(2)}) collective-permute-start(bf16[64,384]{1,0:T(8,128)(2,1)} %get-tuple-element.23.ref0), channel_id=1, source_target_pairs={{0,4},{2,6},{4,0},{6,2},{1,5},{3,7},{5,1},{7,3},{8,12},{10,14},{12... | collective-permute-start | bytes 147464 | tf_op jit(solution)/shard_map/ppermute | solution.py:300
  15.2 4.3 %collective-permute-start.2 = (bf16[64,384]{1,0:T(8,128)(2,1)}, bf16[64,384]{1,0:T(8,128)(2,1)S(1)}, u32[]{:S(2)}, u32[]{:S(2)}) collective-permute-start(bf16[64,384]{1,0:T(8,128)(2,1)} %get-tuple-element.23.ref0), channel_id=1, source_target_pairs={{0,6},{2,0},{4,2},{6,4},{1,7},{3,1},{5,3},{7,5},{8,14},{10,8},{12,... | collective-permute-start | bytes 147464 | tf_op jit(solution)/shard_map/ppermute | solution.py:300
  19.5 14.3 %slice-start = ((s8[7077888]{0:T(1024)(128)(4,1)}), s8[2883584]{0:T(1024)(128)(4,1)S(1)}, s32[]{:S(2)}) async-start(s8[7077888]{0:T(1024)(128)(4,1)} %bitcast.2), calls=%async_computation.1 | async-start | bytes 5767168
  22.5 11.3 %slice-start.1 = ((s8[7077888]{0:T(1024)(128)(4,1)}), s8[4194304]{0:T(1024)(128)(4,1)S(1)}, s32[]{:S(2)}) async-start(s8[7077888]{0:T(1024)(128)(4,1)} %bitcast.2), calls=%async_computation.2 | async-start | bytes 8388608
  22.5 7.8 %collective-permute-start.3 = (bf16[160,384]{1,0:T(8,128)(2,1)S(1)}, bf16[160,384]{1,0:T(8,128)(2,1)S(1)}, u32[]{:S(2)}, u32[]{:S(2)}) collective-permute-start(bf16[160,384]{1,0:T(8,128)(2,1)S(1)} %embed.1.mine0.after_ref), channel_id=1, source_target_pairs={{0,2},{2,4},{4,6},{6,0},{1,3},{3,5},{5,7},{7,1},{8,10},{10,12},{12... | collective-permute-start | bytes 368648 | tf_op jit(solution)/shard_map/ppermute | solution.py:300
  24.0 8.1 %collective-permute-start.4 = (bf16[160,384]{1,0:T(8,128)(2,1)S(1)}, bf16[160,384]{1,0:T(8,128)(2,1)S(1)}, u32[]{:S(2)}, u32[]{:S(2)}) collective-permute-start(bf16[160,384]{1,0:T(8,128)(2,1)S(1)} %embed.1.mine0.after_ref), channel_id=1, source_target_pairs={{0,4},{2,6},{4,0},{6,2},{1,5},{3,7},{5,1},{7,3},{8,12},{10,14},{12... | collective-permute-start | bytes 368648 | tf_op jit(solution)/shard_map/ppermute | solution.py:300
  27.6 4.9 %collective-permute-start.5 = (bf16[160,384]{1,0:T(8,128)(2,1)S(1)}, bf16[160,384]{1,0:T(8,128)(2,1)S(1)}, u32[]{:S(2)}, u32[]{:S(2)}) collective-permute-start(bf16[160,384]{1,0:T(8,128)(2,1)S(1)} %embed.1.mine0.after_ref), channel_id=1, source_target_pairs={{0,6},{2,0},{4,2},{6,4},{1,7},{3,1},{5,3},{7,5},{8,14},{10,8},{12,... | collective-permute-start | bytes 368648 | tf_op jit(solution)/shard_map/ppermute | solution.py:300
  28.6 4.5 %collective-permute-start.6 = (bf16[160,384]{1,0:T(8,128)(2,1)S(1)}, bf16[160,384]{1,0:T(8,128)(2,1)S(1)}, u32[]{:S(2)}, u32[]{:S(2)}) collective-permute-start(bf16[160,384]{1,0:T(8,128)(2,1)S(1)} %embed.1.mine0.after_ref), channel_id=1, source_target_pairs={{0,1},{1,0},{2,3},{3,2},{4,5},{5,4},{6,7},{7,6},{8,9},{9,8},{10,11... | collective-permute-start | bytes 368648 | tf_op jit(solution)/shard_map/ppermute | solution.py:306
  30.3 2.8 %collective-permute-start.7 = (bf16[160,384]{1,0:T(8,128)(2,1)S(1)}, bf16[160,384]{1,0:T(8,128)(2,1)S(1)}, u32[]{:S(2)}, u32[]{:S(2)}) collective-permute-start(bf16[160,384]{1,0:T(8,128)(2,1)S(1)} %collective-permute-done.3.mine1), channel_id=1, source_target_pairs={{0,1},{1,0},{2,3},{3,2},{4,5},{5,4},{6,7},{7,6},{8,9},{9,8},{10,11... | collective-permute-start | bytes 368648 | tf_op jit(solution)/shard_map/ppermute | solution.py:306
  32.1 1.3 %collective-permute-start.8 = (bf16[160,384]{1,0:T(8,128)(2,1)S(1)}, bf16[160,384]{1,0:T(8,128)(2,1)S(1)}, u32[]{:S(2)}, u32[]{:S(2)}) collective-permute-start(bf16[160,384]{1,0:T(8,128)(2,1)S(1)} %collective-permute-done.4.mine2), channel_id=1, source_target_pairs={{0,1},{1,0},{2,3},{3,2},{4,5},{5,4},{6,7},{7,6},{8,9},{9,8},{10,11... | collective-permute-start | bytes 368648 | tf_op jit(solution)/shard_map/ppermute | solution.py:306
  32.5 1.3 %collective-permute-start.9 = (bf16[160,384]{1,0:T(8,128)(2,1)S(1)}, bf16[160,384]{1,0:T(8,128)(2,1)S(1)}, u32[]{:S(2)}, u32[]{:S(2)}) collective-permute-start(bf16[160,384]{1,0:T(8,128)(2,1)S(1)} %collective-permute-done.5.mine3), channel_id=1, source_target_pairs={{0,1},{1,0},{2,3},{3,2},{4,5},{5,4},{6,7},{7,6},{8,9},{9,8},{10,11... | collective-permute-start | bytes 368648 | tf_op jit(solution)/shard_map/ppermute | solution.py:306
  32.7 6.9 %collective-permute-start.11 = (bf16[4,64,384]{2,1,0:T(8,128)(2,1)S(1)}, bf16[4,64,384]{2,1,0:T(8,128)(2,1)S(1)}, u32[]{:S(2)}, u32[]{:S(2)}) collective-permute-start(bf16[4,64,384]{2,1,0:T(8,128)(2,1)S(1)} %stack.1.same_ref), channel_id=1, source_target_pairs={{0,1},{1,0},{2,3},{3,2},{4,5},{5,4},{6,7},{7,6},{8,9},{9,8},{10,11... | collective-permute-start | bytes 589832 | tf_op jit(solution)/shard_map/ppermute | solution.py:306
  35.4 10.5 %collective-permute-start.13 = (bf16[2,128,384]{2,1,0:T(8,128)(2,1)S(1)}, bf16[2,128,384]{2,1,0:T(8,128)(2,1)S(1)}, u32[]{:S(2)}, u32[]{:S(2)}) collective-permute-start(bf16[2,128,384]{2,1,0:T(8,128)(2,1)S(1)} %far.1.after_ref.far_ref), channel_id=1, source_target_pairs={{0,16},{8,24},{16,0},{24,8},{32,48},{40,56},{48,32},{56,40},{64,80... | collective-permute-start | bytes 589832 | tf_op jit(solution)/shard_map/ppermute | solution.py:412
  37.5 9.7 %collective-permute-start.12 = (bf16[2,128,384]{2,1,0:T(8,128)(2,1)S(1)}, bf16[2,128,384]{2,1,0:T(8,128)(2,1)S(1)}, u32[]{:S(2)}, u32[]{:S(2)}) collective-permute-start(bf16[2,128,384]{2,1,0:T(8,128)(2,1)S(1)} %far.1.after_ref.far_ref), channel_id=1, source_target_pairs={{0,24},{8,0},{16,8},{24,16},{32,56},{40,32},{48,40},{56,48},{64,88... | collective-permute-start | bytes 589832 | tf_op jit(solution)/shard_map/ppermute | solution.py:412
  38.7 9.4 %collective-permute-start.10 = (bf16[2,128,384]{2,1,0:T(8,128)(2,1)S(1)}, bf16[2,128,384]{2,1,0:T(8,128)(2,1)S(1)}, u32[]{:S(2)}, u32[]{:S(2)}) collective-permute-start(bf16[2,128,384]{2,1,0:T(8,128)(2,1)S(1)} %far.1.after_ref.far_ref), channel_id=1, source_target_pairs={{0,8},{8,16},{16,24},{24,0},{32,40},{40,48},{48,56},{56,32},{64,72... | collective-permute-start | bytes 589832 | tf_op jit(solution)/shard_map/ppermute | solution.py:412
  48.9 7.1 %collective-permute-start.14 = (bf16[400,128]{1,0:T(8,128)(2,1)S(1)}, bf16[400,128]{1,0:T(8,128)(2,1)S(1)}, u32[]{:S(2)}, u32[]{:S(2)}) collective-permute-start(bf16[400,128]{1,0:T(8,128)(2,1)S(1)} %get-tuple-element.36), channel_id=1, source_target_pairs={{0,32},{8,40},{16,48},{24,56},{32,64},{40,72},{48,80},{56,88},{64,... | collective-permute-start | bytes 307208 | tf_op jit(solution)/shard_map/ppermute | solution.py:416
  50.3 6.9 %collective-permute-start.15 = (bf16[400,128]{1,0:T(8,128)(2,1)S(1)}, bf16[400,128]{1,0:T(8,128)(2,1)S(1)}, u32[]{:S(2)}, u32[]{:S(2)}) collective-permute-start(bf16[400,128]{1,0:T(8,128)(2,1)S(1)} %get-tuple-element.37), channel_id=1, source_target_pairs={{0,64},{8,72},{16,80},{24,88},{32,96},{40,104},{48,112},{56,120},{... | collective-permute-start | bytes 307208 | tf_op jit(solution)/shard_map/ppermute | solution.py:416
  53.0 4.7 %collective-permute-start.16 = (bf16[400,128]{1,0:T(8,128)(2,1)S(1)}, bf16[400,128]{1,0:T(8,128)(2,1)S(1)}, u32[]{:S(2)}, u32[]{:S(2)}) collective-permute-start(bf16[400,128]{1,0:T(8,128)(2,1)S(1)} %get-tuple-element.38), channel_id=1, source_target_pairs={{0,96},{8,104},{16,112},{24,120},{32,0},{40,8},{48,16},{56,24},{64... | collective-permute-start | bytes 307208 | tf_op jit(solution)/shard_map/ppermute | solution.py:416
  (6 other events, 51.3 us)
